TPU v7x, 32 devices: a whole 2x2x4 slice. The times are simulated.
32 devices in a mesh: ra: 8 (over y, x, core), dec: 4 (over z).
Axes of the slice: x: 2, y: 2, z: 4, core: 2. Of those that a mesh axis runs over, the one named last changes fastest.
Arguments:
- completeness: float32 [64, 64, 512], P(None, 'ra', 'dec'), may hold values from 0.3 to 1
- stencil: float32 [25, 64], replicated, may hold values from 0.02 to 0.08
- features: bfloat16 [96, 16384], P(None, ('ra', 'dec')), may hold values from -6 to 6
- frequencies: bfloat16 [96, 256], replicated, may hold values from -2 to 2
- gal_cell: int32 [16384], P(('ra', 'dec')), may hold values from 0 to 65535
- pip: bfloat16 [128, 12, 128, 128], P(('ra', 'dec')), may hold values from 0.019897461 to 0.19921875
- pair_src: int32 [128, 12], P(('ra', 'dec')), may hold values from 0 to 35
- pair_count: int32 [128], P(('ra', 'dec')), may hold values from 4 to 12
Outputs:
- basis_sums: bfloat16 [256, 16384], P(None, ('ra', 'dec'))
Inputs may be any that keep to these rules, and one draw needn't show every extreme that they name: pair_src = slot * 4 + block; slot q names the tile offset q // 3 - 1 along ra and q % 3 - 1 along dec, block a block of that tile. gal_cell = band * 8 * 128 + row * 128 + column of the galaxy's cell within its own tile. Slots at or past pair_count are ignored.
All inputs are finite; a program needn't handle non-finite values.
Results may differ from a plain program's by a relative error of at most 0.017.
Values may be sent and summed in bfloat16 or wider, within the bound.
No kernel may reach another device: no remote copies, remote signals or barrier semaphores. Data moves between devices by JAX's collectives and lax.ppermute only.
A program may use at most 64 MiB of HBM per device.

v0:
```python
import jax
import jax.numpy as jnp
from jax import lax
from jax.sharding import PartitionSpec as P


def padded(cells, sides, width):
    for axis, dim in sides:
        count = lax.axis_size(axis)
        ends = count - 1
        head = lax.slice_in_dim(cells, 0, width, axis=dim)
        tail = lax.slice_in_dim(cells, cells.shape[dim] - width, cells.shape[dim], axis=dim)
        cells = jnp.concatenate(
            [
                lax.ppermute(tail, axis, [(i, (i + 1) % count) for i in range(ends)]),
                cells,
                lax.ppermute(head, axis, [((i + 1) % count, i) for i in range(ends)]),
            ],
            axis=dim,
        )
    return cells


def spread(payload):
    return padded(payload, (("ra", 1), ("dec", 2)), 1)


def per_device(completeness, stencil, features, frequencies, gal_cell, pip, pair_src, pair_count):
    bands, cells_x, cells_y = completeness.shape
    grid = padded(completeness, (("ra", 1), ("dec", 2)), 2)
    smooth = jnp.zeros(completeness.shape, jnp.float32)
    for shift_a in range(5):
        for shift_c in range(5):
            smooth = (
                smooth
                + stencil[5 * shift_a + shift_c][:, None, None]
                * grid[:, shift_a : shift_a + cells_x, shift_c : shift_c + cells_y]
            )
    gweight = lax.rsqrt(smooth.reshape(-1)[gal_cell]).astype(jnp.bfloat16)
    theta = jnp.dot(frequencies.T, features, preferred_element_type=jnp.float32)
    wfloat = gweight.astype(jnp.float32)
    feats, galaxies = features.shape
    nfreq = frequencies.shape[1]
    blk = pip.shape[2]
    nblk = galaxies // blk
    cosine = jnp.cos(theta)
    sine = jnp.sin(theta)
    basis = jnp.concatenate([wfloat * cosine, wfloat * sine], 0).astype(jnp.bfloat16)
    near = spread(basis.reshape(2 * nfreq, 1, 1, galaxies))
    near = near.reshape(2 * nfreq, 9 * nblk, blk)
    slots = pip.shape[1]
    taken = near[:, pair_src]
    live = (jnp.arange(slots, dtype=jnp.int32)[None, :] < pair_count[:, None]).astype(jnp.bfloat16)
    taken = taken * live[None, :, :, None]
    sums = jnp.einsum("kbpj,bpij->kbi", taken, pip, preferred_element_type=jnp.float32)
    sums = sums.reshape(2 * nfreq, galaxies)
    result = wfloat * (cosine * sums[:nfreq] + sine * sums[nfreq:])
    return result.astype(jnp.bfloat16)


def solution(mesh):
    in_specs = (
        P(None, "ra", "dec"),
        P(),
        P(None, ("ra", "dec")),
        P(),
        P(("ra", "dec")),
        P(("ra", "dec"), None, None, None),
        P(("ra", "dec"), None),
        P(("ra", "dec")),
    )
    out_specs = P(None, ("ra", "dec"))
    return jax.shard_map(
        per_device, mesh=mesh, in_specs=in_specs, out_specs=out_specs, check_vma=False
    )
```

profile of v0, /device:TPU:2, one launch (start us, length us, event | category | flops | bytes accessed | tf_op | source)
XLA Modules:
  0.0 138.0 jit_solution(5195116612626168294)
XLA Ops:
  0.0 0.0 copy-start
  0.0 1.2 fusion.42
  1.2 1.9 %collective-permute-start = (f32[64,2,128]{2,1,0:T(2,128)S(1)}, f32[64,2,128]{2,1,0:T(2,128)S(1)}, u32[]{:S(2)}, u32[]{:S(2)}) collective-permute-start(f32[64,2,128]{2,1,0:T(2,128)S(1)} %get-tuple-element.13), channel_id=1, source_target_pairs={{0,4},{4,8},{8,12},{12,16},{16,20},{20,24},{24,28},{1,5},{5,9},{9,... | collective-permute-start | bytes 196616 | tf_op jit(solution)/shard_map/ppermute | solution.py:15
  3.1 3.6 %collective-permute-start.1 = (f32[64,2,128]{2,1,0:T(2,128)S(1)}, f32[64,2,128]{2,1,0:T(2,128)S(1)}, u32[]{:S(2)}, u32[]{:S(2)}) collective-permute-start(f32[64,2,128]{2,1,0:T(2,128)S(1)} %get-tuple-element.14), channel_id=1, source_target_pairs={{4,0},{8,4},{12,8},{16,12},{20,16},{24,20},{28,24},{5,1},{9,5},{13... | collective-permute-start | bytes 196616 | tf_op jit(solution)/shard_map/ppermute | solution.py:17
  6.8 1.0 slice_bitcast_fusion.24
  7.8 0.8 slice_bitcast_fusion.23
  8.6 1.0 constant_dynamic-update-slice_fusion.1
  9.6 0.7 compare_select_fusion.1
  10.3 3.0 %fusion.40 = (f32[256,512]{1,0:T(8,128)S(1)}, f32[256,512]{1,0:T(8,128)S(1)}) fusion(bf16[96,256]{1,0:T(8,128)(2,1)} %param.11, bf16[96,512]{1,0:T(8,128)(2,1)} %param.10), kind=kOutput, calls=%fused_computation.107 | convolution fusion | flops 25165824 | bytes 1196032 | tf_op jit(solution)/shard_map/dot_general | solution.py:40
  13.4 0.0 collective-permute-done
  13.4 0.0 collective-permute-done.1
  13.4 1.1 pad_maximum_fusion.3
  14.5 0.2 fusion.41
  14.7 3.5 %collective-permute-start.2 = (f32[64,12,2]{2,1,0:T(8,128)S(1)}, f32[64,12,2]{2,1,0:T(8,128)S(1)}, u32[]{:S(2)}, u32[]{:S(2)}) collective-permute-start(f32[64,12,2]{2,1,0:T(8,128)S(1)} %get-tuple-element.9), channel_id=1, source_target_pairs={{0,1},{1,2},{2,3},{4,5},{5,6},{6,7},{8,9},{9,10},{10,11},{12,13},{... | collective-permute-start | bytes 18440 | tf_op jit(solution)/shard_map/ppermute | solution.py:15
  18.2 1.3 collective-permute-start.3
  19.5 9.8 %collective-permute-done.2 = f32[64,12,2]{2,1,0:T(8,128)S(1)} collective-permute-done((f32[64,12,2]{2,1,0:T(8,128)S(1)}, f32[64,12,2]{2,1,0:T(8,128)S(1)}, u32[]{:S(2)}, u32[]{:S(2)}) %collective-permute-start.2) | collective-permute-done | bytes 6176 | tf_op jit(solution)/shard_map/ppermute | solution.py:15
  29.3 4.1 %collective-permute-done.3 = f32[64,12,2]{2,1,0:T(8,128)S(1)} collective-permute-done((f32[64,12,2]{2,1,0:T(8,128)S(1)}, f32[64,12,2]{2,1,0:T(8,128)S(1)}, u32[]{:S(2)}, u32[]{:S(2)}) %collective-permute-start.3) | collective-permute-done | bytes 6176 | tf_op jit(solution)/shard_map/ppermute | solution.py:17
  33.5 0.0 copy-done.1
  33.5 0.7 maximum_maximum_fusion
  34.2 3.1 %fusion.33 = f32[65536]{0:T(1024)S(1)} fusion(f32[64,12,130]{2,1,0:T(8,128)S(1)} %get-tuple-element.12, f32[64,10,128]{2,1,0:T(8,128)S(1)} %constant_dynamic-update-slice_fusion, f32[64,8,128]{2,1,0:T(8,128)S(1)} %copy-done.1, f32[64,2,128]{2,1,0:T(2,128)S(1)} %collective-permute-done, f32[64,12,130]{2,1,0:T(8,128)S(1)} %get-tuple-element.11, ...), kind=kLoop, calls=%fused_computation.45 | loop fusion | flops 3342336 | bytes 6363392 | tf_op jit(solution)/shard_map/reshape | solution.py:39
  37.3 0.0 copy-start.4
  37.3 0.0 copy-start.5
  37.4 3.1 %gather_fusion = f32[512]{0:T(512)S(1)} fusion(f32[65536]{0:T(1024)S(1)} %fusion.33, s32[1024]{0:T(1024)S(1)} %pad_clamp_fusion.1), kind=kCustom, calls=%fused_computation | custom fusion | bytes 6144 | tf_op jit(solution)/shard_map/gather | solution.py:39
  40.5 0.1 fusion.7
  40.7 1.9 %collective-permute-start.4 = (bf16[512,1,1,512]{3,0,2,1:T(8,128)(2,1)S(1)}, bf16[512,1,1,512]{3,0,2,1:T(8,128)(2,1)S(1)}, u32[]{:S(2)}, u32[]{:S(2)}) collective-permute-start(bf16[512,1,1,512]{3,0,2,1:T(8,128)(2,1)S(1)} %pad_maximum_fusion.4), channel_id=1, source_target_pairs={{0,4},{4,8},{8,12},{12,16},{16,20},{20,24},{24,28},{1,5},{5,9},{9,... | collective-permute-start | bytes 1572872 | tf_op jit(solution)/shard_map/ppermute | solution.py:15
  42.6 3.6 %collective-permute-start.5 = (bf16[512,1,1,512]{3,0,2,1:T(8,128)(2,1)S(1)}, bf16[512,1,1,512]{3,0,2,1:T(8,128)(2,1)S(1)}, u32[]{:S(2)}, u32[]{:S(2)}) collective-permute-start(bf16[512,1,1,512]{3,0,2,1:T(8,128)(2,1)S(1)} %pad_maximum_fusion.4), channel_id=1, source_target_pairs={{4,0},{8,4},{12,8},{16,12},{20,16},{24,20},{28,24},{5,1},{9,5},{13... | collective-permute-start | bytes 1572872 | tf_op jit(solution)/shard_map/ppermute | solution.py:17
  46.3 4.9 %collective-permute-done.4 = bf16[512,1,1,512]{3,0,2,1:T(8,128)(2,1)S(1)} collective-permute-done((bf16[512,1,1,512]{3,0,2,1:T(8,128)(2,1)S(1)}, bf16[512,1,1,512]{3,0,2,1:T(8,128)(2,1)S(1)}, u32[]{:S(2)}, u32[]{:S(2)}) %collective-permute-start.4) | collective-permute-done | bytes 524320 | tf_op jit(solution)/shard_map/ppermute | solution.py:15
  51.2 4.6 %collective-permute-done.5 = bf16[512,1,1,512]{3,0,2,1:T(8,128)(2,1)S(1)} collective-permute-done((bf16[512,1,1,512]{3,0,2,1:T(8,128)(2,1)S(1)}, bf16[512,1,1,512]{3,0,2,1:T(8,128)(2,1)S(1)}, u32[]{:S(2)}, u32[]{:S(2)}) %collective-permute-start.5) | collective-permute-done | bytes 524320 | tf_op jit(solution)/shard_map/ppermute | solution.py:17
  55.8 0.0 copy-done.2
  55.8 1.3 pad_maximum_fusion.1
  57.1 0.0 copy-done.3
  57.1 4.7 %collective-permute-start.6 = (bf16[512,3,1,512]{3,0,2,1:T(8,128)(2,1)}, bf16[512,3,1,512]{3,0,2,1:T(8,128)(2,1)}, u32[]{:S(2)}, u32[]{:S(2)}) collective-permute-start(bf16[512,3,1,512]{3,0,2,1:T(8,128)(2,1)} %pad_maximum_fusion.1), channel_id=1, source_target_pairs={{0,1},{1,2},{2,3},{4,5},{5,6},{6,7},{8,9},{9,10},{10,11},{12,13},{... | collective-permute-start | bytes 4718600 | tf_op jit(solution)/shard_map/ppermute | solution.py:15
  61.8 1.3 collective-permute-start.7
  63.1 0.1 reshape.105
  63.2 0.0 copy-done.5
  63.2 0.1 fusion.37
  63.3 32.1 %collective-permute-done.6 = bf16[512,3,1,512]{3,0,2,1:T(8,128)(2,1)} collective-permute-done((bf16[512,3,1,512]{3,0,2,1:T(8,128)(2,1)}, bf16[512,3,1,512]{3,0,2,1:T(8,128)(2,1)}, u32[]{:S(2)}, u32[]{:S(2)}) %collective-permute-start.6) | collective-permute-done | bytes 1572896 | tf_op jit(solution)/shard_map/ppermute | solution.py:15
  95.4 5.3 %collective-permute-done.7 = bf16[512,3,1,512]{3,0,2,1:T(8,128)(2,1)} collective-permute-done((bf16[512,3,1,512]{3,0,2,1:T(8,128)(2,1)}, bf16[512,3,1,512]{3,0,2,1:T(8,128)(2,1)}, u32[]{:S(2)}, u32[]{:S(2)}) %collective-permute-start.7) | collective-permute-done | bytes 1572896 | tf_op jit(solution)/shard_map/ppermute | solution.py:17
  100.7 5.4 %pad_maximum_fusion = bf16[512,3,3,512]{3,0,2,1:T(8,128)(2,1)} fusion(bf16[512,3,1,512]{3,0,2,1:T(8,128)(2,1)} %collective-permute-done.7, bf16[512,1,1,512]{3,0,2,1:T(8,128)(2,1)} %copy-done.3, bf16[256,1,1,512]{3,0,2,1:T(8,128)(2,1)S(1)} %get-tuple-element.41, bf16[256,1,1,512]{3,0,2,1:T(8,128)(2,1)S(1)} %get-tuple-element.40, ...), kind=kLoop, calls=%fused_computation.5 | loop fusion | flops 28311552 | bytes 9437184 | tf_op jit(solution)/shard_map/concatenate | solution.py:13
  106.1 6.7 %copy.11 = bf16[512,3,3,512]{0,3,2,1:T(8,128)(2,1)} copy(bf16[512,3,3,512]{3,0,2,1:T(8,128)(2,1)} %pad_maximum_fusion) | data formatting | bytes 9437184 | tf_op jit(solution)/shard_map/concatenate | solution.py:13
  112.8 6.6 %copy.12 = bf16[512,36,128]{2,0,1:T(8,128)(2,1)} copy(bf16[512,36,128]{0,2,1:T(8,128)(2,1)} %bitcast.73) | data formatting | bytes 9437184 | tf_op jit(solution)/shard_map/reshape | solution.py:50
  119.4 7.3 %gather_fusion.1 = bf16[48,512,128]{2,1,0:T(8,128)(2,1)} fusion(bf16[512,36,128]{2,0,1:T(8,128)(2,1)} %copy.12, s32[1024]{0:T(1024)S(1)} %pad_clamp_fusion), kind=kCustom, calls=%fused_computation.1 | custom fusion | bytes 12583104 | tf_op jit(solution)/shard_map/gather | solution.py:52
  126.7 0.0 copy-done
  126.7 4.9 %fusion.4 = f32[512,4,128]{0,2,1:T(8,128)S(1)} fusion(bf16[4,12,128,128]{3,2,1,0:T(8,128)(2,1)S(1)} %copy-done, bf16[4,12,512,128]{3,2,1,0:T(8,128)(2,1)} %bitcast.74, bf16[4,12]{1,0:T(4,128)(2,1)S(1)} %fusion.37), kind=kOutput, calls=%fused_computation.8 | convolution fusion | flops 808452096 | bytes 8912992 | tf_op jit(solution)/shard_map/kbpj,bpij->kbi/dot_general | solution.py:55
  131.7 1.1 fusion.39
  132.8 1.2 copy.16
  134.0 2.0 %copy.17 = f32[256,512]{1,0:T(8,128)} copy(f32[256,512]{0,1:T(8,128)} %bitcast.75) | data formatting | bytes 1048576 | tf_op jit(solution)/shard_map/slice | solution.py:57
  136.0 2.0 %multiply_convert_fusion = bf16[256,512]{1,0:T(8,128)(2,1)} fusion(f32[256,512]{1,0:T(8,128)S(1)} %get-tuple-element.8, f32[256,512]{1,0:T(8,128)} %copy.17, f32[256,512]{1,0:T(8,128)S(1)} %get-tuple-element.7, f32[256,512]{1,0:T(8,128)S(1)} %copy.16, f32[512]{0:T(512)S(1)} %fusion.38), kind=kLoop, calls=%fused_computation.15 | loop fusion | flops 655360 | bytes 2361344 | tf_op jit(solution)/shard_map/convert_element_type | solution.py:58
  (10 shorter events, 0.1 us)
Async XLA Ops:
  0.0 126.7 %copy-start = (bf16[4,12,128,128]{3,2,1,0:T(8,128)(2,1)S(1)}, bf16[4,12,128,128]{3,2,1,0:T(8,128)(2,1)}, u32[]{:S(2)}) copy-start(bf16[4,12,128,128]{3,2,1,0:T(8,128)(2,1)} %param.13) | copy-start | bytes 4718596
  0.0 33.5 %copy-start.1 = (f32[64,8,128]{2,1,0:T(8,128)S(1)}, f32[64,8,128]{2,1,0:T(8,128)}, u32[]{:S(2)}) copy-start(f32[64,8,128]{2,1,0:T(8,128)} %param.8) | copy-start | bytes 786436
  1.2 12.2 %collective-permute-start = (f32[64,2,128]{2,1,0:T(2,128)S(1)}, f32[64,2,128]{2,1,0:T(2,128)S(1)}, u32[]{:S(2)}, u32[]{:S(2)}) collective-permute-start(f32[64,2,128]{2,1,0:T(2,128)S(1)} %get-tuple-element.13), channel_id=1, source_target_pairs={{0,4},{4,8},{8,12},{12,16},{16,20},{20,24},{24,28},{1,5},{5,9},{9,... | collective-permute-start | bytes 196616 | tf_op jit(solution)/shard_map/ppermute | solution.py:15
  3.1 10.2 %collective-permute-start.1 = (f32[64,2,128]{2,1,0:T(2,128)S(1)}, f32[64,2,128]{2,1,0:T(2,128)S(1)}, u32[]{:S(2)}, u32[]{:S(2)}) collective-permute-start(f32[64,2,128]{2,1,0:T(2,128)S(1)} %get-tuple-element.14), channel_id=1, source_target_pairs={{4,0},{8,4},{12,8},{16,12},{20,16},{24,20},{28,24},{5,1},{9,5},{13... | collective-permute-start | bytes 196616 | tf_op jit(solution)/shard_map/ppermute | solution.py:17
  14.7 14.7 %collective-permute-start.2 = (f32[64,12,2]{2,1,0:T(8,128)S(1)}, f32[64,12,2]{2,1,0:T(8,128)S(1)}, u32[]{:S(2)}, u32[]{:S(2)}) collective-permute-start(f32[64,12,2]{2,1,0:T(8,128)S(1)} %get-tuple-element.9), channel_id=1, source_target_pairs={{0,1},{1,2},{2,3},{4,5},{5,6},{6,7},{8,9},{9,10},{10,11},{12,13},{... | collective-permute-start | bytes 18440 | tf_op jit(solution)/shard_map/ppermute | solution.py:15
  18.2 15.3 %collective-permute-start.3 = (f32[64,12,2]{2,1,0:T(8,128)S(1)}, f32[64,12,2]{2,1,0:T(8,128)S(1)}, u32[]{:S(2)}, u32[]{:S(2)}) collective-permute-start(f32[64,12,2]{2,1,0:T(8,128)S(1)} %get-tuple-element.10), channel_id=1, source_target_pairs={{1,0},{2,1},{3,2},{5,4},{6,5},{7,6},{9,8},{10,9},{11,10},{13,12},{... | collective-permute-start | bytes 18440 | tf_op jit(solution)/shard_map/ppermute | solution.py:17
  37.3 25.8 %copy-start.4 = (s32[4,12]{1,0:T(4,128)S(1)}, s32[4,12]{1,0:T(4,128)}, u32[]{:S(2)}) copy-start(s32[4,12]{1,0:T(4,128)} %param.14) | copy-start | bytes 580
  37.3 25.9 %copy-start.5 = (s32[4]{0:T(128)S(1)}, s32[4]{0:T(128)}, u32[]{:S(2)}) copy-start(s32[4]{0:T(128)} %param.15) | copy-start | bytes 52
  40.7 10.5 %collective-permute-start.4 = (bf16[512,1,1,512]{3,0,2,1:T(8,128)(2,1)S(1)}, bf16[512,1,1,512]{3,0,2,1:T(8,128)(2,1)S(1)}, u32[]{:S(2)}, u32[]{:S(2)}) collective-permute-start(bf16[512,1,1,512]{3,0,2,1:T(8,128)(2,1)S(1)} %pad_maximum_fusion.4), channel_id=1, source_target_pairs={{0,4},{4,8},{8,12},{12,16},{16,20},{20,24},{24,28},{1,5},{5,9},{9,... | collective-permute-start | bytes 1572872 | tf_op jit(solution)/shard_map/ppermute | solution.py:15
  42.6 13.2 %collective-permute-start.5 = (bf16[512,1,1,512]{3,0,2,1:T(8,128)(2,1)S(1)}, bf16[512,1,1,512]{3,0,2,1:T(8,128)(2,1)S(1)}, u32[]{:S(2)}, u32[]{:S(2)}) collective-permute-start(bf16[512,1,1,512]{3,0,2,1:T(8,128)(2,1)S(1)} %pad_maximum_fusion.4), channel_id=1, source_target_pairs={{4,0},{8,4},{12,8},{16,12},{20,16},{24,20},{28,24},{5,1},{9,5},{13... | collective-permute-start | bytes 1572872 | tf_op jit(solution)/shard_map/ppermute | solution.py:17
  51.2 4.6 %copy-start.2 = (bf16[512,1,1,512]{3,0,2,1:T(8,128)(2,1)}, bf16[512,1,1,512]{3,0,2,1:T(8,128)(2,1)S(1)}, u32[]{:S(2)}) copy-start(bf16[512,1,1,512]{3,0,2,1:T(8,128)(2,1)S(1)} %collective-permute-done.4) | copy-start | bytes 1572868
  55.8 1.3 copy-start.3
  57.1 38.2 %collective-permute-start.6 = (bf16[512,3,1,512]{3,0,2,1:T(8,128)(2,1)}, bf16[512,3,1,512]{3,0,2,1:T(8,128)(2,1)}, u32[]{:S(2)}, u32[]{:S(2)}) collective-permute-start(bf16[512,3,1,512]{3,0,2,1:T(8,128)(2,1)} %pad_maximum_fusion.1), channel_id=1, source_target_pairs={{0,1},{1,2},{2,3},{4,5},{5,6},{6,7},{8,9},{9,10},{10,11},{12,13},{... | collective-permute-start | bytes 4718600 | tf_op jit(solution)/shard_map/ppermute | solution.py:15
  61.8 38.9 %collective-permute-start.7 = (bf16[512,3,1,512]{3,0,2,1:T(8,128)(2,1)}, bf16[512,3,1,512]{3,0,2,1:T(8,128)(2,1)}, u32[]{:S(2)}, u32[]{:S(2)}) collective-permute-start(bf16[512,3,1,512]{3,0,2,1:T(8,128)(2,1)} %pad_maximum_fusion.1), channel_id=1, source_target_pairs={{1,0},{2,1},{3,2},{5,4},{6,5},{7,6},{9,8},{10,9},{11,10},{13,12},{... | collective-permute-start | bytes 4718600 | tf_op jit(solution)/shard_map/ppermute | solution.py:17
where the time goes:
time: 139 us; the launch traced here: 138 us
  waiting for transfers between devices  60.9 us (44%)
  local copies, waits for them, and re-layouts  32.5 us (23%)
  starting transfers between devices  21.9 us (16%)
  other arithmetic  14.5 us (10%)
  matrix products  7.99 us (6%)
    ppermute x4, waiting for transfers between devices, padded(): lax.ppermute(tail, axis, [(i, (i + 1) % count) for i in range(ends)])  46.8 us
    ppermute x4, waiting for transfers between devices, padded(): lax.ppermute(head, axis, [((i + 1) % count, i) for i in range(ends)])  14.1 us
    ppermute x4, starting transfers between devices, padded(): lax.ppermute(tail, axis, [(i, (i + 1) % count) for i in range(ends)])  12 us
    ppermute x4, starting transfers between devices, padded(): lax.ppermute(head, axis, [((i + 1) % count, i) for i in range(ends)])  9.86 us
    concatenate x4, other arithmetic, padded(): jnp.concatenate([lax.ppermute(tail, axis, [(i, (i + 1) % count) for i in...  8.43 us
    gather x1, local copies, waits for them, and re-layouts, per_device(): taken = near[:, pair_src]  7.35 us
    concatenate x2, local copies, waits for them, and re-layouts, padded(): jnp.concatenate([lax.ppermute(tail, axis, [(i, (i + 1) % count) for i in...  6.72 us
    reshape x1, local copies, waits for them, and re-layouts, per_device(): near = near.reshape(2 * nfreq, 9 * nblk, blk)  6.61 us
  transfers between devices with their start and end apart: 8, of which 6 were waited for; matrix products, arithmetic and copies ran while one was open for 5% of the time, Pallas kernels for 0%

commit v1 on v0

v1 whole, which is shorter than its diff:
```python
import functools
import math

import jax
import jax.numpy as jnp
from jax import lax
from jax.experimental import pallas as pl
from jax.experimental.pallas import tpu as pltpu
from jax.sharding import PartitionSpec as P

BF16 = jnp.bfloat16
F32 = jnp.float32
RIM = 16

VMEM = pl.BlockSpec(memory_space=pltpu.VMEM)
SMEM = pl.BlockSpec(memory_space=pltpu.SMEM)
ANY = pl.BlockSpec(memory_space=pl.ANY)

COS = (1.0, -19.739208802178716, 64.93939402266828, -85.45681720669371, 60.24464137187665, -26.42625678337438, 7.903536371318467, -1.7143907110886711)
SIN = (6.283185307179586, -41.34170224039975, 81.60524927607504, -76.70585975306136, 42.05869394489765, -15.094642576822986, 3.8199525848482803)


def params(limit=None, **kw):
    return pltpu.CompilerParams(vmem_limit_bytes=limit or (16 << 20), **kw)


def pairs(count, odd):
    out = []
    for i in range(odd, count - 1, 2):
        out += [(i, i + 1), (i + 1, i)]
    return out


def exchange(odd_payload, even_payload, axis):
    count = lax.axis_size(axis)
    return (
        lax.ppermute(odd_payload, axis, pairs(count, 1)),
        lax.ppermute(even_payload, axis, pairs(count, 0)),
    )


def dot(a, b, ca, cb):
    return lax.dot_general(a, b, (((ca,), (cb,)), ((), ())), preferred_element_type=F32)


def rim_kernel(comp_ref, rim_ref, rows_ref):
    bands, nx, ny = comp_ref.shape
    for x in range(nx):
        rows_ref[x * bands : (x + 1) * bands, :] = comp_ref[:, x, :]
    row = lax.broadcasted_iota(jnp.int32, (RIM, ny), 0)
    lane = lax.broadcasted_iota(jnp.int32, (RIM, ny), 1)
    pick = ((row < 2) & (lane == row)) | ((row >= 2) & (row < 4) & (lane == row + ny - 4))
    rim_ref[...] = dot(pick.astype(F32).astype(BF16), rows_ref[...].astype(BF16), 1, 1).astype(BF16)


def row_kernel(rows_ref, odd_ref, even_ref, to_odd_ref, to_even_ref):
    n = rows_ref.shape[0]
    two = to_odd_ref.shape[0] - 2 * RIM
    is_odd = lax.rem(lax.axis_index("ra"), 2) == 1

    def put(ref, start):
        ref[0:two, :] = rows_ref[start : start + two, :].astype(BF16)
        ref[two : two + RIM, :] = odd_ref[:, start : start + two]
        ref[two + RIM :, :] = even_ref[:, start : start + two]

    @pl.when(is_odd)
    def _():
        put(to_odd_ref, n - two)
        put(to_even_ref, 0)

    @pl.when(jnp.logical_not(is_odd))
    def _():
        put(to_odd_ref, 0)
        put(to_even_ref, n - two)


def weight_kernel(bands, rows_ref, d_odd_ref, d_even_ref, r_odd_ref, r_even_ref, stencil_ref, cell_ref, out_ref, st_ref, ext_ref, smooth_ref):
    n, ny = rows_ref.shape
    nx = n // bands
    two = 2 * bands
    ra_odd = lax.rem(lax.axis_index("ra"), 2) == 1
    dec_odd = lax.rem(lax.axis_index("dec"), 2) == 1

    row = lax.broadcasted_iota(jnp.int32, (RIM, ny), 0)
    lane = lax.broadcasted_iota(jnp.int32, (RIM, ny), 1)
    after = ((row < 2) & (lane == row)).astype(F32).astype(BF16)
    before = ((row >= 2) & (row < 4) & (lane == row + ny - 4)).astype(F32).astype(BF16)
    place_odd = jnp.where(dec_odd, after, before)
    place_even = jnp.where(dec_odd, before, after)

    def halo(odd, even):
        return dot(odd, place_odd, 0, 0) + dot(even, place_even, 0, 0)

    up = jnp.where(ra_odd, r_odd_ref[...], r_even_ref[...])
    down = jnp.where(ra_odd, r_even_ref[...], r_odd_ref[...])

    def extend(start, cells, edge):
        size = cells.shape[0]
        at = lax.broadcasted_iota(jnp.int32, cells.shape, 1)
        ext_ref[2, start : start + size, :] = cells
        ext_ref[3, start : start + size, :] = pltpu.roll(jnp.where(at < 1, edge, cells), ny - 1, 1)
        ext_ref[4, start : start + size, :] = pltpu.roll(jnp.where(at < 2, edge, cells), ny - 2, 1)
        ext_ref[1, start : start + size, :] = pltpu.roll(jnp.where(at > ny - 2, edge, cells), 1, 1)
        ext_ref[0, start : start + size, :] = pltpu.roll(jnp.where(at > ny - 3, edge, cells), 2, 1)

    extend(two, rows_ref[...], halo(d_odd_ref[...], d_even_ref[...]))
    extend(0, down[:two].astype(F32), halo(down[two : two + RIM], down[two + RIM :]))
    extend(two + n, up[:two].astype(F32), halo(up[two : two + RIM], up[two + RIM :]))

    st_ref[...] = jnp.zeros_like(st_ref)
    st_ref[0 : stencil_ref.shape[0], 0:bands] = stencil_ref[...]
    by_band = st_ref[...].T
    for g in range(bands // 8):
        accs = [jnp.zeros((8, ny), F32) for _ in range(nx)]
        for c in range(5):
            for a in range(5):
                k = 5 * a + c
                w = jnp.broadcast_to(by_band[8 * g : 8 * g + 8, k : k + 1], (8, ny))
                for x in range(nx):
                    base = (x + a) * bands + 8 * g
                    accs[x] = accs[x] + w * ext_ref[c, base : base + 8, :]
        for x in range(nx):
            smooth_ref[x * bands + 8 * g : x * bands + 8 * g + 8, :] = accs[x]

    smooth = smooth_ref[...]
    high = smooth.astype(BF16)
    low = (smooth - high.astype(F32)).astype(BF16)
    cell = cell_ref[...]
    galaxies = cell.shape[1]
    slot = (cell // ny % nx) * bands + cell // (nx * ny)
    hit = lax.broadcasted_iota(jnp.int32, (n, galaxies), 0) == slot
    hit = jnp.where(hit, 1.0, 0.0).astype(BF16)
    found = dot(high, hit, 0, 0) + dot(low, hit, 0, 0)
    at = lax.broadcasted_iota(jnp.int32, (ny, galaxies), 0) == cell % ny
    value = jnp.sum(jnp.where(at, found, 0.0), axis=0, keepdims=True)
    out_ref[...] = jnp.broadcast_to(lax.rsqrt(value), out_ref.shape).astype(BF16)


def stack_weight_kernel(own_ref, odd_ref, even_ref, out_ref):
    at = lax.broadcasted_iota(jnp.int32, out_ref.shape, 0)
    out = jnp.where(at == 1, odd_ref[...].astype(F32), own_ref[...].astype(F32))
    out_ref[...] = jnp.where(at == 2, even_ref[...].astype(F32), out).astype(BF16)


def stack_rows_kernel(a_ref, b_ref, c_ref, out_ref):
    n = a_ref.shape[0]
    out_ref[0:n, :] = a_ref[...]
    out_ref[n : 2 * n, :] = b_ref[...]
    out_ref[2 * n :, :] = c_ref[...]


def sincos(theta):
    turns = theta * (0.5 / math.pi)
    magic = 12582912.0
    r = turns - ((turns + magic) - magic)
    z = r * r
    c = jnp.full_like(z, COS[-1])
    for k in COS[-2::-1]:
        c = c * z + k
    s = jnp.full_like(z, SIN[-1])
    for k in SIN[-2::-1]:
        s = s * z + k
    return c, s * r


def basis_kernel(first, tiles, nblk, freq_ref, *refs):
    feat_refs, out_ref, ft_ref = refs[: len(tiles)], refs[-2], refs[-1]
    feats, nfreq = freq_ref.shape
    blk = out_ref.shape[2]
    ft_ref[...] = freq_ref[...].astype(F32).T.astype(BF16)
    at = first
    for feat_ref, count in zip(feat_refs, tiles, strict=True):
        for t in range(count):
            for b in range(nblk):
                x = feat_ref[t * feats : (t + 1) * feats, b * blk : (b + 1) * blk]
                c, s = sincos(dot(ft_ref[...], x, 1, 0))
                out_ref[at, 0:nfreq, :] = c.astype(BF16)
                out_ref[at, nfreq:, :] = s.astype(BF16)
                at += 1


def pair_kernel(src_ref, count_ref, pip_ref, basis_ref, w_own_ref, w_odd_ref, w_even_ref, out_ref, w_ref):
    nblk, slots, blk, _ = pip_ref.shape
    nfreq = out_ref.shape[0]
    ra_odd = lax.rem(lax.axis_index("ra"), 2)
    dec_odd = lax.rem(lax.axis_index("dec"), 2)
    for i, ref in enumerate((w_own_ref, w_odd_ref, w_even_ref)):
        for j in range(3):
            for b in range(nblk):
                at = (3 * i + j) * nblk + b
                w_ref[at : at + 1, :] = ref[j : j + 1, b * blk : (b + 1) * blk].astype(F32)

    def side(step, odd):
        up = 2 - odd
        return jnp.where(step == 1, 0, jnp.where(step == 2, up, 3 - up))

    for a in range(nblk):
        def place(p):
            s = src_ref[a, p]
            q = s // nblk
            return (3 * side(q // 3, ra_odd) + side(q % 3, dec_odd)) * nblk + s % nblk

        total = None
        for p in range(0, slots, 2):
            lhs, rhs = [], []
            for k in (p, p + 1):
                at = place(k)
                live = jnp.where(k < count_ref[a], 1.0, 0.0)
                lhs.append(basis_ref[at])
                rhs.append((pip_ref[a, k].astype(F32) * (w_ref[pl.ds(at, 1), :] * live)).astype(BF16))
            part = dot(jnp.concatenate(lhs, 1), jnp.concatenate(rhs, 1), 1, 1)
            total = part if total is None else total + part
        own = basis_ref[a].astype(F32)
        folded = own[:nfreq] * total[:nfreq] + own[nfreq:] * total[nfreq:]
        out_ref[:, a * blk : (a + 1) * blk] = (folded * w_ref[a : a + 1, :]).astype(BF16)


def vm(shape, dtype):
    return pltpu.VMEM(shape, dtype)


def per_device(completeness, stencil, features, frequencies, gal_cell, pip, pair_src, pair_count):
    bands, nx, ny = completeness.shape
    feats, galaxies = features.shape
    nfreq = frequencies.shape[1]
    nblk, slots, blk, _ = pip.shape
    n = bands * nx
    two = 2 * bands

    rim, rows = pl.pallas_call(
        rim_kernel, out_shape=(vm((RIM, n), BF16), vm((n, ny), F32)), in_specs=[VMEM], out_specs=(VMEM, VMEM),
        compiler_params=params(), name="rim",
    )(completeness)
    d_odd, d_even = exchange(rim, rim, "dec")
    f_odd, f_even = exchange(features, features, "dec")

    to_odd, to_even = pl.pallas_call(
        row_kernel, out_shape=(vm((two + 2 * RIM, ny), BF16),) * 2, in_specs=[VMEM] * 3, out_specs=(VMEM, VMEM),
        compiler_params=params(), name="rows",
    )(rows, d_odd, d_even)
    r_odd, r_even = exchange(to_odd, to_even, "ra")
    column = pl.pallas_call(
        stack_rows_kernel, out_shape=vm((3 * feats, galaxies), BF16), in_specs=[VMEM] * 3, out_specs=VMEM,
        compiler_params=params(), name="stack_features",
    )(features, f_odd, f_even)
    c_odd, c_even = exchange(column, column, "ra")

    def basis(first, tiles, arrays, buffer):
        blocks = 9 * nblk
        shape = vm((blocks, 2 * nfreq, blk), BF16)
        body = functools.partial(basis_kernel, first, tiles, nblk)
        work = sum(tiles) * nfreq * galaxies
        common = dict(
            out_shape=shape, out_specs=VMEM, scratch_shapes=[pltpu.VMEM((nfreq, feats), BF16)], compiler_params=params(),
            cost_estimate=pl.CostEstimate(flops=work * 2 * feats + 24 * work, bytes_accessed=work * 4, transcendentals=0),
            name="basis%d" % first,
        )
        if buffer is None:
            return pl.pallas_call(body, in_specs=[VMEM] * (1 + len(arrays)), **common)(frequencies, *arrays)

        def aliased(freq_ref, *refs):
            body(freq_ref, *refs[: len(arrays)], *refs[len(arrays) + 1 :])

        return pl.pallas_call(
            aliased, in_specs=[VMEM] * (1 + len(arrays)) + [VMEM], input_output_aliases={1 + len(arrays): 0}, **common
        )(frequencies, *arrays, buffer)

    table = basis(0, (1,), (features,), None)
    table = basis(nblk, (1, 1), (f_odd, f_even), table)

    weight = pl.pallas_call(
        functools.partial(weight_kernel, bands), out_shape=vm((RIM, galaxies), BF16), in_specs=[VMEM] * 7, out_specs=VMEM,
        scratch_shapes=[pltpu.VMEM((32, 128), F32), pltpu.VMEM((5, n + 2 * two, ny), F32), pltpu.VMEM((n, ny), F32)],
        compiler_params=params(), name="weight",
    )(rows, d_odd, d_even, r_odd, r_even, stencil, gal_cell.reshape(1, galaxies))
    w_odd, w_even = exchange(weight, weight, "dec")
    w_column = pl.pallas_call(
        stack_weight_kernel, out_shape=vm((RIM, galaxies), BF16), in_specs=[VMEM] * 3, out_specs=VMEM,
        compiler_params=params(), name="stack_weights",
    )(weight, w_odd, w_even)
    table = basis(3 * nblk, (3, 3), (c_odd, c_even), table)
    x_odd, x_even = exchange(w_column, w_column, "ra")
    return pl.pallas_call(
        pair_kernel, out_shape=jax.ShapeDtypeStruct((nfreq, galaxies), BF16), in_specs=[SMEM, SMEM] + [VMEM] * 5, out_specs=VMEM,
        scratch_shapes=[pltpu.VMEM((9 * nblk + 4, blk), F32)],
        compiler_params=params(), name="pairs",
    )(pair_src, pair_count, pip, table, w_column, x_odd, x_even)


def solution(mesh):
    in_specs = (
        P(None, "ra", "dec"),
        P(),
        P(None, ("ra", "dec")),
        P(),
        P(("ra", "dec")),
        P(("ra", "dec"), None, None, None),
        P(("ra", "dec"), None),
        P(("ra", "dec")),
    )
    out_specs = P(None, ("ra", "dec"))
    return jax.shard_map(per_device, mesh=mesh, in_specs=in_specs, out_specs=out_specs, check_vma=False)
```

time: 139 us -> 50.3 us (0.36)
  the two profiles are of different devices: /device:TPU:2 before, /device:TPU:1 now
where the time goes in v1:
time: 50.3 us; the launch traced here: 49.4 us
  starting transfers between devices  28.3 us (56%)
  Pallas kernels  11 us (22%)
  waiting for transfers between devices  4.96 us (10%)
  local copies, waits for them, and re-layouts  4.95 us (10%)
    ppermute x6, starting transfers between devices, exchange(): lax.ppermute(odd_payload, axis, pairs(count, 1))  15.8 us
    ppermute x6, starting transfers between devices, exchange(): lax.ppermute(even_payload, axis, pairs(count, 0))  12.5 us
    pallas_call x2, Pallas kernels, basis(): pl.pallas_call(aliased, in_specs=[VMEM] * (1 + len(arrays)) + [VMEM], inp...  5.08 us
    unnamed x20, local copies, waits for them, and re-layouts  4.95 us
    ppermute x6, waiting for transfers between devices, exchange(): lax.ppermute(even_payload, axis, pairs(count, 0))  3.35 us
    pallas_call x1, Pallas kernels, per_device(): pl.pallas_call(pair_kernel, out_shape=jax.ShapeDtypeStruct((nfreq, galaxi...  3.18 us
    pallas_call x1, Pallas kernels, per_device(): pl.pallas_call(functools.partial(weight_kernel, bands), out_shape=vm((RIM...  1.62 us
    ppermute x6, waiting for transfers between devices, exchange(): lax.ppermute(odd_payload, axis, pairs(count, 1))  1.61 us
  transfers between devices with their start and end apart: 12, of which 3 were waited for; matrix products, arithmetic and copies ran while one was open for 0% of the time, Pallas kernels for 16%

profile of v1, /device:TPU:1, one launch (start us, length us, event | category | flops | bytes accessed | tf_op | source)
XLA Modules:
  0.0 49.4 jit_solution(14696357701772775378)
XLA Ops:
  0.0 0.0 copy-start.2
  0.0 0.8 %collective-permute-start = (bf16[96,512]{1,0:T(8,128)(2,1)}, bf16[96,512]{1,0:T(8,128)(2,1)S(1)}, u32[]{:S(2)}, u32[]{:S(2)}) collective-permute-start(bf16[96,512]{1,0:T(8,128)(2,1)} %refs_0_.1), channel_id=1, source_target_pairs={{1,2},{2,1},{5,6},{6,5},{9,10},{10,9},{13,14},{14,13},{17,18},{18,... | collective-permute-start | bytes 294920 | tf_op jit(solution)/shard_map/ppermute | solution.py:37
  0.8 4.7 %collective-permute-start.1 = (bf16[96,512]{1,0:T(8,128)(2,1)}, bf16[96,512]{1,0:T(8,128)(2,1)S(1)}, u32[]{:S(2)}, u32[]{:S(2)}) collective-permute-start(bf16[96,512]{1,0:T(8,128)(2,1)} %refs_0_.1), channel_id=1, source_target_pairs={{0,1},{1,0},{2,3},{3,2},{4,5},{5,4},{6,7},{7,6},{8,9},{9,8},{10,11... | collective-permute-start | bytes 294920 | tf_op jit(solution)/shard_map/ppermute | solution.py:38
  5.5 0.0 collective-permute-done.b_ref.refs_0_
  5.5 2.2 %collective-permute-done.1.c_ref.refs_1_ = bf16[96,512]{1,0:T(8,128)(2,1)S(1)} collective-permute-done((bf16[96,512]{1,0:T(8,128)(2,1)}, bf16[96,512]{1,0:T(8,128)(2,1)S(1)}, u32[]{:S(2)}, u32[]{:S(2)}) %collective-permute-start.1) | collective-permute-done | bytes 98336 | tf_op jit(solution)/shard_map/ppermute | solution.py:38
  7.7 0.0 copy-start.3
  7.8 0.9 %copy-done.3 = bf16[96,512]{1,0:T(8,128)(2,1)S(1)} copy-done((bf16[96,512]{1,0:T(8,128)(2,1)S(1)}, bf16[96,512]{1,0:T(8,128)(2,1)}, u32[]{:S(2)}) %copy-start.3) | copy-done | bytes 98328
  8.7 4.8 %collective-permute-start.2 = (bf16[288,512]{1,0:T(8,128)(2,1)S(1)}, bf16[288,512]{1,0:T(8,128)(2,1)S(1)}, u32[]{:S(2)}, u32[]{:S(2)}) collective-permute-start(bf16[288,512]{1,0:T(8,128)(2,1)S(1)} %stack_features.1), channel_id=1, source_target_pairs={{4,8},{8,4},{12,16},{16,12},{20,24},{24,20},{5,9},{9,5},{13,17},{1... | collective-permute-start | bytes 884744 | tf_op jit(solution)/shard_map/ppermute | solution.py:37
  13.5 0.1 collective-permute-start.3
  13.6 0.0 copy-start.5
  13.6 0.9 %copy-done.5 = f32[64,8,128]{2,1,0:T(8,128)S(1)} copy-done((f32[64,8,128]{2,1,0:T(8,128)S(1)}, f32[64,8,128]{2,1,0:T(8,128)}, u32[]{:S(2)}) %copy-start.5) | copy-done | bytes 262168
  14.5 0.3 rim.1
  14.8 0.7 %collective-permute-start.4 = (bf16[16,512]{1,0:T(8,128)(2,1)S(1)}, bf16[16,512]{1,0:T(8,128)(2,1)S(1)}, u32[]{:S(2)}, u32[]{:S(2)}) collective-permute-start(bf16[16,512]{1,0:T(8,128)(2,1)S(1)} %get-tuple-element.10), channel_id=1, source_target_pairs={{1,2},{2,1},{5,6},{6,5},{9,10},{10,9},{13,14},{14,13},{17,18},{18,... | collective-permute-start | bytes 49160 | tf_op jit(solution)/shard_map/ppermute | solution.py:37
  15.5 3.2 %collective-permute-start.5 = (bf16[16,512]{1,0:T(8,128)(2,1)S(1)}, bf16[16,512]{1,0:T(8,128)(2,1)S(1)}, u32[]{:S(2)}, u32[]{:S(2)}) collective-permute-start(bf16[16,512]{1,0:T(8,128)(2,1)S(1)} %get-tuple-element.10), channel_id=1, source_target_pairs={{0,1},{1,0},{2,3},{3,2},{4,5},{5,4},{6,7},{7,6},{8,9},{9,8},{10,11... | collective-permute-start | bytes 49160 | tf_op jit(solution)/shard_map/ppermute | solution.py:38
  18.7 0.0 collective-permute-done.4.odd_ref.d_odd_ref
  18.7 1.1 %collective-permute-done.5.even_ref.d_even_ref = bf16[16,512]{1,0:T(8,128)(2,1)S(1)} collective-permute-done((bf16[16,512]{1,0:T(8,128)(2,1)S(1)}, bf16[16,512]{1,0:T(8,128)(2,1)S(1)}, u32[]{:S(2)}, u32[]{:S(2)}) %collective-permute-start.5) | collective-permute-done | bytes 16416 | tf_op jit(solution)/shard_map/ppermute | solution.py:38
  19.8 4.6 %collective-permute-start.6 = (bf16[160,128]{1,0:T(8,128)(2,1)S(1)}, bf16[160,128]{1,0:T(8,128)(2,1)S(1)}, u32[]{:S(2)}, u32[]{:S(2)}) collective-permute-start(bf16[160,128]{1,0:T(8,128)(2,1)S(1)} %get-tuple-element.11), channel_id=1, source_target_pairs={{4,8},{8,4},{12,16},{16,12},{20,24},{24,20},{5,9},{9,5},{13,17},{1... | collective-permute-start | bytes 122888 | tf_op jit(solution)/shard_map/ppermute | solution.py:37
  24.5 0.1 collective-permute-start.7
  24.6 1.6 %collective-permute-done.6.r_odd_ref = bf16[160,128]{1,0:T(8,128)(2,1)S(1)} collective-permute-done((bf16[160,128]{1,0:T(8,128)(2,1)S(1)}, bf16[160,128]{1,0:T(8,128)(2,1)S(1)}, u32[]{:S(2)}, u32[]{:S(2)}) %collective-permute-start.6) | collective-permute-done | bytes 40992 | tf_op jit(solution)/shard_map/ppermute | solution.py:37
  26.2 0.0 collective-permute-done.7.r_even_ref
  26.2 0.0 copy-start.6
  26.2 0.7 %copy-done.6 = f32[25,64]{1,0:T(8,128)S(1)} copy-done((f32[25,64]{1,0:T(8,128)S(1)}, f32[25,64]{1,0:T(8,128)}, u32[]{:S(2)}) %copy-start.6) | copy-done | bytes 6424
  26.9 0.0 copy-start.8
  26.9 0.7 %copy-done.8 = s32[512]{0:T(512)S(1)} copy-done((s32[512]{0:T(512)S(1)}, s32[512]{0:T(512)}, u32[]{:S(2)}) %copy-start.8) | copy-done | bytes 2072
  27.6 1.6 %weight.1.own_ref = bf16[16,512]{1,0:T(8,128)(2,1)S(1)} custom-call(f32[512,128]{1,0:T(8,128)S(1)} %get-tuple-element.9.rows_ref, bf16[16,512]{1,0:T(8,128)(2,1)S(1)} %collective-permute-done.4.odd_ref.d_odd_ref, bf16[16,512]{1,0:T(8,128)(2,1)S(1)} %collective-permute-done.5.even_ref.d_even_ref, bf16[160,128]{1,0:T(8,128)(2,1)S(1)} %collective-permute-done.6.r_odd_ref, ...), custom_call_target="tpu_custom_call" | custom-call | tf_op jit(solution)/shard_map/weight/pallas_call | solution.py:271
  29.2 0.7 %collective-permute-start.8 = (bf16[16,512]{1,0:T(8,128)(2,1)S(1)}, bf16[16,512]{1,0:T(8,128)(2,1)S(1)}, u32[]{:S(2)}, u32[]{:S(2)}) collective-permute-start(bf16[16,512]{1,0:T(8,128)(2,1)S(1)} %weight.1.own_ref), channel_id=1, source_target_pairs={{1,2},{2,1},{5,6},{6,5},{9,10},{10,9},{13,14},{14,13},{17,18},{18,... | collective-permute-start | bytes 49160 | tf_op jit(solution)/shard_map/ppermute | solution.py:37
  29.9 4.4 %collective-permute-start.9 = (bf16[16,512]{1,0:T(8,128)(2,1)S(1)}, bf16[16,512]{1,0:T(8,128)(2,1)S(1)}, u32[]{:S(2)}, u32[]{:S(2)}) collective-permute-start(bf16[16,512]{1,0:T(8,128)(2,1)S(1)} %weight.1.own_ref), channel_id=1, source_target_pairs={{0,1},{1,0},{2,3},{3,2},{4,5},{5,4},{6,7},{7,6},{8,9},{9,8},{10,11... | collective-permute-start | bytes 49160 | tf_op jit(solution)/shard_map/ppermute | solution.py:38
  34.2 0.8 %copy-done.1 = bf16[96,256]{1,0:T(8,128)(2,1)S(1)} copy-done((bf16[96,256]{1,0:T(8,128)(2,1)S(1)}, bf16[96,256]{1,0:T(8,128)(2,1)}, u32[]{:S(2)}) %copy-start.1) | copy-done | bytes 49176
  35.0 0.9 %copy-done.4 = bf16[96,512]{1,0:T(8,128)(2,1)S(1)} copy-done((bf16[96,512]{1,0:T(8,128)(2,1)S(1)}, bf16[96,512]{1,0:T(8,128)(2,1)}, u32[]{:S(2)}) %copy-start.4) | copy-done | bytes 98328
  35.9 0.8 %basis0.1.refs_2_ = bf16[36,512,128]{2,1,0:T(8,128)(2,1)S(1)} custom-call(bf16[96,256]{1,0:T(8,128)(2,1)S(1)} %copy-done.1, bf16[96,512]{1,0:T(8,128)(2,1)S(1)} %copy-done.4), custom_call_target="tpu_custom_call" | custom-call | flops 28311552 | bytes 524288 | tf_op jit(solution)/shard_map/basis0/pallas_call | solution.py:259
  36.7 0.0 collective-permute-done.8.odd_ref
  36.7 0.0 collective-permute-done.9.even_ref
  36.7 4.2 %collective-permute-start.10 = (bf16[16,512]{1,0:T(8,128)(2,1)S(1)}, bf16[16,512]{1,0:T(8,128)(2,1)S(1)}, u32[]{:S(2)}, u32[]{:S(2)}) collective-permute-start(bf16[16,512]{1,0:T(8,128)(2,1)S(1)} %stack_weights.1.w_own_ref), channel_id=1, source_target_pairs={{4,8},{8,4},{12,16},{16,12},{20,24},{24,20},{5,9},{9,5},{13,17},{1... | collective-permute-start | bytes 49160 | tf_op jit(solution)/shard_map/ppermute | solution.py:37
  40.9 0.1 collective-permute-start.11
  41.0 0.0 copy-done.2
  41.0 1.3 %basis4.1.refs_2_ = bf16[36,512,128]{2,1,0:T(8,128)(2,1)S(1)} custom-call(bf16[96,256]{1,0:T(8,128)(2,1)S(1)} %copy-done.2, bf16[96,512]{1,0:T(8,128)(2,1)S(1)} %collective-permute-done.b_ref.refs_0_, bf16[96,512]{1,0:T(8,128)(2,1)S(1)} %collective-permute-done.1.c_ref.refs_1_, bf16[36,512,128]{2,1,0:T(8,128)(2,1)S(1)} %basis0.1.refs_2_), custom_call_target="tpu_custom_call", output_to_operand_aliasing={{}: (3, {})} | custom-call | flops 56623104 | bytes 1048576 | tf_op jit(solution)/shard_map/basis4/pallas_call | solution.py:264
  42.4 0.0 copy-start
  42.4 0.0 copy-start.7
  42.4 0.0 copy-start.9
  42.4 0.0 collective-permute-done.2.refs_0_
  42.4 0.0 collective-permute-done.3.refs_1_
  42.4 3.7 %basis12.1.basis_ref = bf16[36,512,128]{2,1,0:T(8,128)(2,1)S(1)} custom-call(bf16[96,256]{1,0:T(8,128)(2,1)S(1)} %copy-done.2, bf16[288,512]{1,0:T(8,128)(2,1)S(1)} %collective-permute-done.2.refs_0_, bf16[288,512]{1,0:T(8,128)(2,1)S(1)} %collective-permute-done.3.refs_1_, bf16[36,512,128]{2,1,0:T(8,128)(2,1)S(1)} %basis4.1.refs_2_), custom_call_target="tpu_custom_call", output_to_operand_aliasing={{}: (3, {})} | custom-call | flops 169869312 | bytes 3145728 | tf_op jit(solution)/shard_map/basis12/pallas_call | solution.py:264
  46.2 0.0 collective-permute-done.10.w_odd_ref
  46.2 0.0 collective-permute-done.11.w_even_ref
  46.2 0.0 copy-done
  46.2 0.0 copy-done.7
  46.2 0.0 copy-done.9
  46.2 3.2 %pairs.1 = bf16[256,512]{1,0:T(8,128)(2,1)} custom-call(s32[4,12]{1,0:T(4,128)S(1)} %copy-done.7, s32[4]{0:T(128)S(1)} %copy-done.9, bf16[4,12,128,128]{3,2,1,0:T(8,128)(2,1)S(1)} %copy-done, bf16[36,512,128]{2,1,0:T(8,128)(2,1)S(1)} %basis12.1.basis_ref, bf16[16,512]{1,0:T(8,128)(2,1)S(1)} %stack_weights.1.w_own_ref, ...), custom_call_target="tpu_custom_call" | custom-call | tf_op jit(solution)/shard_map/pairs/pallas_call | solution.py:283
  (5 shorter events, 0.0 us)
Async XLA Ops:
  0.0 41.0 %copy-start.2 = (bf16[96,256]{1,0:T(8,128)(2,1)S(1)}, bf16[96,256]{1,0:T(8,128)(2,1)}, u32[]{:S(2)}) copy-start(bf16[96,256]{1,0:T(8,128)(2,1)} %freq_ref.5) | copy-start | bytes 147460
  0.0 5.5 %collective-permute-start = (bf16[96,512]{1,0:T(8,128)(2,1)}, bf16[96,512]{1,0:T(8,128)(2,1)S(1)}, u32[]{:S(2)}, u32[]{:S(2)}) collective-permute-start(bf16[96,512]{1,0:T(8,128)(2,1)} %refs_0_.1), channel_id=1, source_target_pairs={{1,2},{2,1},{5,6},{6,5},{9,10},{10,9},{13,14},{14,13},{17,18},{18,... | collective-permute-start | bytes 294920 | tf_op jit(solution)/shard_map/ppermute | solution.py:37
  0.8 7.0 %collective-permute-start.1 = (bf16[96,512]{1,0:T(8,128)(2,1)}, bf16[96,512]{1,0:T(8,128)(2,1)S(1)}, u32[]{:S(2)}, u32[]{:S(2)}) collective-permute-start(bf16[96,512]{1,0:T(8,128)(2,1)} %refs_0_.1), channel_id=1, source_target_pairs={{0,1},{1,0},{2,3},{3,2},{4,5},{5,4},{6,7},{7,6},{8,9},{9,8},{10,11... | collective-permute-start | bytes 294920 | tf_op jit(solution)/shard_map/ppermute | solution.py:38
  7.7 0.9 %copy-start.3 = (bf16[96,512]{1,0:T(8,128)(2,1)S(1)}, bf16[96,512]{1,0:T(8,128)(2,1)}, u32[]{:S(2)}) copy-start(bf16[96,512]{1,0:T(8,128)(2,1)} %refs_0_.1) | copy-start | bytes 294916
  8.7 33.7 %collective-permute-start.2 = (bf16[288,512]{1,0:T(8,128)(2,1)S(1)}, bf16[288,512]{1,0:T(8,128)(2,1)S(1)}, u32[]{:S(2)}, u32[]{:S(2)}) collective-permute-start(bf16[288,512]{1,0:T(8,128)(2,1)S(1)} %stack_features.1), channel_id=1, source_target_pairs={{4,8},{8,4},{12,16},{16,12},{20,24},{24,20},{5,9},{9,5},{13,17},{1... | collective-permute-start | bytes 884744 | tf_op jit(solution)/shard_map/ppermute | solution.py:37
  13.5 28.9 %collective-permute-start.3 = (bf16[288,512]{1,0:T(8,128)(2,1)S(1)}, bf16[288,512]{1,0:T(8,128)(2,1)S(1)}, u32[]{:S(2)}, u32[]{:S(2)}) collective-permute-start(bf16[288,512]{1,0:T(8,128)(2,1)S(1)} %stack_features.1), channel_id=1, source_target_pairs={{0,4},{4,0},{8,12},{12,8},{16,20},{20,16},{24,28},{28,24},{1,5},{5... | collective-permute-start | bytes 884744 | tf_op jit(solution)/shard_map/ppermute | solution.py:38
  13.6 1.0 %copy-start.5 = (f32[64,8,128]{2,1,0:T(8,128)S(1)}, f32[64,8,128]{2,1,0:T(8,128)}, u32[]{:S(2)}) copy-start(f32[64,8,128]{2,1,0:T(8,128)} %comp_ref.1) | copy-start | bytes 786436
  14.8 3.9 %collective-permute-start.4 = (bf16[16,512]{1,0:T(8,128)(2,1)S(1)}, bf16[16,512]{1,0:T(8,128)(2,1)S(1)}, u32[]{:S(2)}, u32[]{:S(2)}) collective-permute-start(bf16[16,512]{1,0:T(8,128)(2,1)S(1)} %get-tuple-element.10), channel_id=1, source_target_pairs={{1,2},{2,1},{5,6},{6,5},{9,10},{10,9},{13,14},{14,13},{17,18},{18,... | collective-permute-start | bytes 49160 | tf_op jit(solution)/shard_map/ppermute | solution.py:37
  15.5 4.3 %collective-permute-start.5 = (bf16[16,512]{1,0:T(8,128)(2,1)S(1)}, bf16[16,512]{1,0:T(8,128)(2,1)S(1)}, u32[]{:S(2)}, u32[]{:S(2)}) collective-permute-start(bf16[16,512]{1,0:T(8,128)(2,1)S(1)} %get-tuple-element.10), channel_id=1, source_target_pairs={{0,1},{1,0},{2,3},{3,2},{4,5},{5,4},{6,7},{7,6},{8,9},{9,8},{10,11... | collective-permute-start | bytes 49160 | tf_op jit(solution)/shard_map/ppermute | solution.py:38
  19.8 6.3 %collective-permute-start.6 = (bf16[160,128]{1,0:T(8,128)(2,1)S(1)}, bf16[160,128]{1,0:T(8,128)(2,1)S(1)}, u32[]{:S(2)}, u32[]{:S(2)}) collective-permute-start(bf16[160,128]{1,0:T(8,128)(2,1)S(1)} %get-tuple-element.11), channel_id=1, source_target_pairs={{4,8},{8,4},{12,16},{16,12},{20,24},{24,20},{5,9},{9,5},{13,17},{1... | collective-permute-start | bytes 122888 | tf_op jit(solution)/shard_map/ppermute | solution.py:37
  24.5 1.7 %collective-permute-start.7 = (bf16[160,128]{1,0:T(8,128)(2,1)S(1)}, bf16[160,128]{1,0:T(8,128)(2,1)S(1)}, u32[]{:S(2)}, u32[]{:S(2)}) collective-permute-start(bf16[160,128]{1,0:T(8,128)(2,1)S(1)} %get-tuple-element.12), channel_id=1, source_target_pairs={{0,4},{4,0},{8,12},{12,8},{16,20},{20,16},{24,28},{28,24},{1,5},{5... | collective-permute-start | bytes 122888 | tf_op jit(solution)/shard_map/ppermute | solution.py:38
  26.2 0.7 %copy-start.6 = (f32[25,64]{1,0:T(8,128)S(1)}, f32[25,64]{1,0:T(8,128)}, u32[]{:S(2)}) copy-start(f32[25,64]{1,0:T(8,128)} %stencil_ref.1) | copy-start | bytes 19204
  26.9 0.7 %copy-start.8 = (s32[512]{0:T(512)S(1)}, s32[512]{0:T(512)}, u32[]{:S(2)}) copy-start(s32[512]{0:T(512)} %param.12) | copy-start | bytes 6148
  29.2 7.5 %collective-permute-start.8 = (bf16[16,512]{1,0:T(8,128)(2,1)S(1)}, bf16[16,512]{1,0:T(8,128)(2,1)S(1)}, u32[]{:S(2)}, u32[]{:S(2)}) collective-permute-start(bf16[16,512]{1,0:T(8,128)(2,1)S(1)} %weight.1.own_ref), channel_id=1, source_target_pairs={{1,2},{2,1},{5,6},{6,5},{9,10},{10,9},{13,14},{14,13},{17,18},{18,... | collective-permute-start | bytes 49160 | tf_op jit(solution)/shard_map/ppermute | solution.py:37
  29.9 6.8 %collective-permute-start.9 = (bf16[16,512]{1,0:T(8,128)(2,1)S(1)}, bf16[16,512]{1,0:T(8,128)(2,1)S(1)}, u32[]{:S(2)}, u32[]{:S(2)}) collective-permute-start(bf16[16,512]{1,0:T(8,128)(2,1)S(1)} %weight.1.own_ref), channel_id=1, source_target_pairs={{0,1},{1,0},{2,3},{3,2},{4,5},{5,4},{6,7},{7,6},{8,9},{9,8},{10,11... | collective-permute-start | bytes 49160 | tf_op jit(solution)/shard_map/ppermute | solution.py:38
  34.2 0.8 %copy-start.1 = (bf16[96,256]{1,0:T(8,128)(2,1)S(1)}, bf16[96,256]{1,0:T(8,128)(2,1)}, u32[]{:S(2)}) copy-start(bf16[96,256]{1,0:T(8,128)(2,1)} %freq_ref.5) | copy-start | bytes 147460
  35.0 0.9 %copy-start.4 = (bf16[96,512]{1,0:T(8,128)(2,1)S(1)}, bf16[96,512]{1,0:T(8,128)(2,1)}, u32[]{:S(2)}) copy-start(bf16[96,512]{1,0:T(8,128)(2,1)} %refs_0_.1) | copy-start | bytes 294916
  36.7 9.4 %collective-permute-start.10 = (bf16[16,512]{1,0:T(8,128)(2,1)S(1)}, bf16[16,512]{1,0:T(8,128)(2,1)S(1)}, u32[]{:S(2)}, u32[]{:S(2)}) collective-permute-start(bf16[16,512]{1,0:T(8,128)(2,1)S(1)} %stack_weights.1.w_own_ref), channel_id=1, source_target_pairs={{4,8},{8,4},{12,16},{16,12},{20,24},{24,20},{5,9},{9,5},{13,17},{1... | collective-permute-start | bytes 49160 | tf_op jit(solution)/shard_map/ppermute | solution.py:37
  40.9 5.2 %collective-permute-start.11 = (bf16[16,512]{1,0:T(8,128)(2,1)S(1)}, bf16[16,512]{1,0:T(8,128)(2,1)S(1)}, u32[]{:S(2)}, u32[]{:S(2)}) collective-permute-start(bf16[16,512]{1,0:T(8,128)(2,1)S(1)} %stack_weights.1.w_own_ref), channel_id=1, source_target_pairs={{0,4},{4,0},{8,12},{12,8},{16,20},{20,16},{24,28},{28,24},{1,5},{5... | collective-permute-start | bytes 49160 | tf_op jit(solution)/shard_map/ppermute | solution.py:38
  42.4 3.8 %copy-start = (bf16[4,12,128,128]{3,2,1,0:T(8,128)(2,1)S(1)}, bf16[4,12,128,128]{3,2,1,0:T(8,128)(2,1)}, u32[]{:S(2)}) copy-start(bf16[4,12,128,128]{3,2,1,0:T(8,128)(2,1)} %pip_ref.1) | copy-start | bytes 4718596
  42.4 3.8 %copy-start.7 = (s32[4,12]{1,0:T(4,128)S(1)}, s32[4,12]{1,0:T(4,128)}, u32[]{:S(2)}) copy-start(s32[4,12]{1,0:T(4,128)} %src_ref.1) | copy-start | bytes 580
  42.4 3.8 %copy-start.9 = (s32[4]{0:T(128)S(1)}, s32[4]{0:T(128)}, u32[]{:S(2)}) copy-start(s32[4]{0:T(128)} %count_ref.1) | copy-start | bytes 52

commit v2 on v1

v2 whole, which is shorter than its diff:
```python
import functools
import math

import jax
import jax.numpy as jnp
from jax import lax
from jax.experimental import pallas as pl
from jax.experimental.pallas import tpu as pltpu
from jax.sharding import PartitionSpec as P

BF16 = jnp.bfloat16
F32 = jnp.float32
LONG = 1 << 36
RIM = 16

VMEM = pl.BlockSpec(memory_space=pltpu.VMEM)
SMEM = pl.BlockSpec(memory_space=pltpu.SMEM)
ANY = pl.BlockSpec(memory_space=pl.ANY)
HBM = pl.BlockSpec(memory_space=pltpu.HBM)

COS = (0.99999922, -19.73898252, 64.92872662, -85.27239701, 58.79403871, -21.07678212)
SIN = (6.2830558, -41.33121431, 81.36681529, -74.47800454, 32.7814008)


def params(limit=None, **kw):
    return pltpu.CompilerParams(vmem_limit_bytes=limit or (16 << 20), **kw)


def exchange(axis, odd_payload, even_payload):
    ra, dec = lax.axis_size("ra"), lax.axis_size("dec")
    here = (lambda r, d: r * dec + d) if axis == "ra" else (lambda d, r: r * dec + d)
    count, other = (ra, dec) if axis == "ra" else (dec, ra)

    def swap(payload, odd):
        pairs = [(here(i, k), here(i + 1, k)) for i in range(odd, count - 1, 2) for k in range(other)]
        busy = {i for pair in pairs for i in pair}
        for i in (0, count - 1):
            ends = [(here(i, k), here(i, k + 1)) for k in range(0, other - 1, 2)]
            pairs += [pair for pair in ends if not busy & set(pair)]
        return lax.ppermute(payload, ("ra", "dec"), sorted(pairs + [(b, a) for a, b in pairs]))

    if axis == "ra":
        even = swap(even_payload, 0)
        return swap(odd_payload, 1), even
    odd = swap(odd_payload, 1)
    return odd, swap(even_payload, 0)


def sides(axis):
    i, n = lax.axis_index(axis), lax.axis_size(axis)
    odd = lax.rem(i, 2) == 1
    return odd, jnp.logical_and(i > 0, jnp.logical_not(jnp.logical_and(odd, i == n - 1)))


def dot(a, b, ca, cb):
    return lax.dot_general(a, b, (((ca,), (cb,)), ((), ())), preferred_element_type=F32)


def rim_kernel(comp_hbm, feat_hbm, freq_hbm, stencil_hbm, cell_hbm, rim_ref, rows_ref, feat_ref, freq_ref, stencil_ref, cell_ref, comp_ref, sems):
    bands, nx, ny = comp_ref.shape
    pairs = ((comp_hbm, comp_ref), (feat_hbm, feat_ref), (freq_hbm, freq_ref), (stencil_hbm, stencil_ref), (cell_hbm, cell_ref))
    copies = [pltpu.make_async_copy(a, b, sems.at[i]) for i, (a, b) in enumerate(pairs)]
    for copy in copies:
        copy.start()
    row = lax.broadcasted_iota(jnp.int32, (RIM, ny), 0)
    lane = lax.broadcasted_iota(jnp.int32, (RIM, ny), 1)
    pick = ((row < 2) & (lane == row)) | ((row >= 2) & (row < 4) & (lane == row + ny - 4))
    copies[0].wait()
    for x in range(nx):
        rows_ref[x * bands : (x + 1) * bands, :] = comp_ref[:, x, :]
    rim_ref[...] = dot(pick.astype(F32).astype(BF16), rows_ref[...].astype(BF16), 1, 1).astype(BF16)
    for copy in copies[1:]:
        copy.wait()


def ready_kernel(bands, nx, ny, stencil_ref, cell_ref, feat_ref, rim_ref, taps_ref, hit_ref, feat_out_ref, st_ref):
    feat_out_ref[...] = feat_ref[...]
    st_ref[...] = jnp.zeros_like(st_ref)
    count = stencil_ref.shape[0]
    st_ref[0:count, 0:bands] = stencil_ref[...]
    by_band = st_ref[...].T
    for k in range(count):
        taps_ref[k * bands : (k + 1) * bands, :] = jnp.broadcast_to(by_band[0:bands, k : k + 1], (bands, ny))
    cell = cell_ref[...]
    slot = (cell // ny % nx) * bands + cell // (nx * ny)
    hit = lax.broadcasted_iota(jnp.int32, hit_ref.shape, 0) == slot
    hit_ref[...] = jnp.where(hit, 1.0, 0.0).astype(BF16)


def row_kernel(rows_ref, odd_ref, even_ref, taps_ref, hit_ref, to_odd_ref, to_even_ref):
    n = rows_ref.shape[0]
    two = to_odd_ref.shape[0] - 2 * RIM
    is_odd, _ = sides("ra")

    def put(ref, start):
        ref[0:two, :] = rows_ref[start : start + two, :].astype(BF16)
        ref[two : two + RIM, :] = odd_ref[:, start : start + two]
        ref[two + RIM :, :] = even_ref[:, start : start + two]

    @pl.when(is_odd)
    def _():
        put(to_odd_ref, n - two)
        put(to_even_ref, 0)

    @pl.when(jnp.logical_not(is_odd))
    def _():
        put(to_odd_ref, 0)
        put(to_even_ref, n - two)


def places(ny):
    dec_odd, has_odd = sides("dec")
    row = lax.broadcasted_iota(jnp.int32, (RIM, ny), 0)
    lane = lax.broadcasted_iota(jnp.int32, (RIM, ny), 1)
    after = ((row < 2) & (lane == row)).astype(F32)
    before = ((row >= 2) & (row < 4) & (lane == row + ny - 4)).astype(F32)
    odd = jnp.where(has_odd, jnp.where(dec_odd, after, before), 0.0)
    return odd.astype(BF16), jnp.where(dec_odd, before, after).astype(BF16)


def extend(ext_ref, start, cells, edge):
    size, ny = cells.shape
    at = lax.broadcasted_iota(jnp.int32, cells.shape, 1)
    ext_ref[2, start : start + size, :] = cells
    ext_ref[3, start : start + size, :] = pltpu.roll(jnp.where(at < 1, edge, cells), ny - 1, 1)
    ext_ref[4, start : start + size, :] = pltpu.roll(jnp.where(at < 2, edge, cells), ny - 2, 1)
    ext_ref[1, start : start + size, :] = pltpu.roll(jnp.where(at > ny - 2, edge, cells), 1, 1)
    ext_ref[0, start : start + size, :] = pltpu.roll(jnp.where(at > ny - 3, edge, cells), 2, 1)


def inner_kernel(bands, rows_ref, odd_ref, even_ref, taps_ref, to_odd_ref, out_ref, ext_ref):
    n, ny = rows_ref.shape
    nx = n // bands
    place_odd, place_even = places(ny)
    extend(ext_ref, 0, rows_ref[...], dot(odd_ref[...], place_odd, 0, 0) + dot(even_ref[...], place_even, 0, 0))
    for g in range(0, bands, 8):
        accs = [jnp.zeros((8, ny), F32) for _ in range(nx)]
        for c in range(5):
            for a in range(5):
                w = taps_ref[(5 * a + c) * bands + g : (5 * a + c) * bands + g + 8, :]
                for x in range(nx):
                    if 0 <= x + a - 2 < nx:
                        base = (x + a - 2) * bands + g
                        accs[x] = accs[x] + w * ext_ref[c, base : base + 8, :]
        for x in range(nx):
            out_ref[x * bands + g : x * bands + g + 8, :] = accs[x]


def weight_kernel(bands, inner_ref, odd_ref, even_ref, taps_ref, hit_ref, cell_ref, basis_in_ref, out_ref, basis_ref, ext_ref, sum_ref):
    n, ny = inner_ref.shape
    nx = n // bands
    two = 2 * bands
    ra_odd, has_odd = sides("ra")
    place_odd, place_even = places(ny)
    odd = jnp.where(has_odd, odd_ref[...].astype(F32), 0.0).astype(BF16)
    up = jnp.where(ra_odd, odd, even_ref[...])
    down = jnp.where(ra_odd, even_ref[...], odd)

    def halo(rows):
        return dot(rows[two : two + RIM], place_odd, 0, 0) + dot(rows[two + RIM :], place_even, 0, 0)

    extend(ext_ref, 0, down[:two].astype(F32), halo(down))
    extend(ext_ref, two, up[:two].astype(F32), halo(up))
    sum_ref[...] = inner_ref[...]
    for g in range(0, bands, 8):
        for x, parts in ((0, ((0, 0), (1, 1))), (1, ((0, 1),)), (nx - 2, ((4, 2),)), (nx - 1, ((3, 2), (4, 3)))):
            acc = sum_ref[x * bands + g : x * bands + g + 8, :]
            for a, e in parts:
                for c in range(5):
                    tap = (5 * a + c) * bands + g
                    acc = acc + taps_ref[tap : tap + 8, :] * ext_ref[c, e * bands + g : e * bands + g + 8, :]
            sum_ref[x * bands + g : x * bands + g + 8, :] = acc

    smooth = sum_ref[...]
    high = smooth.astype(BF16)
    low = (smooth - high.astype(F32)).astype(BF16)
    cell = cell_ref[...]
    found = dot(high, hit_ref[...], 0, 0) + dot(low, hit_ref[...], 0, 0)
    at = lax.broadcasted_iota(jnp.int32, found.shape, 0) == cell % ny
    value = jnp.sum(jnp.where(at, found, 0.0), axis=0, keepdims=True)
    out_ref[...] = jnp.broadcast_to(lax.rsqrt(value), out_ref.shape).astype(BF16)


def stack_weight_kernel(own_ref, odd_ref, even_ref, basis_in_ref, out_ref, basis_ref):
    at = lax.broadcasted_iota(jnp.int32, out_ref.shape, 0)
    _, has_odd = sides("dec")
    odd = jnp.where(has_odd, odd_ref[...].astype(F32), 0.0)
    out = jnp.where(at == 1, odd, own_ref[...].astype(F32))
    out_ref[...] = jnp.where(at == 2, even_ref[...].astype(F32), out).astype(BF16)


def stack_rows_kernel(a_ref, b_ref, c_ref, after_ref, out_ref):
    n = a_ref.shape[0]
    out_ref[0:n, :] = a_ref[...]
    out_ref[n : 2 * n, :] = b_ref[...]
    out_ref[2 * n :, :] = c_ref[...]


def sincos(theta):
    turns = theta * (0.5 / math.pi)
    magic = 12582912.0
    r = turns - ((turns + magic) - magic)
    z = r * r
    c = jnp.full_like(z, COS[-1])
    for k in COS[-2::-1]:
        c = c * z + k
    s = jnp.full_like(z, SIN[-1])
    for k in SIN[-2::-1]:
        s = s * z + k
    return c, s * r


def basis_kernel(first, tiles, nblk, freq_ref, *refs):
    feat_refs, out_ref, ft_ref = refs[: len(tiles)], refs[-2], refs[-1]
    feats, nfreq = freq_ref.shape
    blk = out_ref.shape[2]
    ft_ref[...] = freq_ref[...].astype(F32).T.astype(BF16)
    at = first
    for feat_ref, count in zip(feat_refs, tiles, strict=True):
        for t in range(count):
            for b in range(nblk):
                x = feat_ref[t * feats : (t + 1) * feats, b * blk : (b + 1) * blk]
                c, s = sincos(dot(ft_ref[...], x, 1, 0))
                out_ref[at, 0:nfreq, :] = c.astype(BF16)
                out_ref[at, nfreq:, :] = s.astype(BF16)
                at += 1


def pair_kernel(src_ref, count_ref, pip_ref, basis_ref, w_own_ref, w_odd_ref, w_even_ref, out_ref, w_ref, done_ref, sems):
    nblk, slots, blk, _ = pip_ref.shape
    nfreq = out_ref.shape[0]
    copies = []
    ra_odd, has_odd = sides("ra")
    dec_odd, _ = sides("dec")
    for i, ref in enumerate((w_own_ref, w_even_ref, w_odd_ref)):
        for j in range(3):
            for b in range(nblk):
                at = (3 * i + j) * nblk + b
                w = ref[j : j + 1, b * blk : (b + 1) * blk].astype(F32)
                w_ref[at : at + 1, :] = jnp.where(has_odd, w, 0.0) if i == 2 else w

    def side(step, odd, first):
        up = jnp.where(odd, first, 3 - first)
        return jnp.where(step == 1, 0, jnp.where(step == 2, up, 3 - up))

    for a in range(nblk):
        def place(p):
            s = src_ref[a, p]
            q = s // nblk
            return (3 * side(q // 3, ra_odd, 2) + side(q % 3, dec_odd, 1)) * nblk + s % nblk

        total = None
        for p in range(0, slots, 2):
            lhs, rhs = [], []
            for k in (p, p + 1):
                at = place(k)
                live = jnp.where(k < count_ref[a], 1.0, 0.0)
                lhs.append(basis_ref[at])
                rhs.append((pip_ref[a, k].astype(F32) * (w_ref[pl.ds(at, 1), :] * live)).astype(BF16))
            part = dot(jnp.concatenate(lhs, 1), jnp.concatenate(rhs, 1), 1, 1)
            total = part if total is None else total + part
        own = basis_ref[a].astype(F32)
        folded = own[:nfreq] * total[:nfreq] + own[nfreq:] * total[nfreq:]
        done_ref[a] = (folded * w_ref[a : a + 1, :]).astype(BF16)
        copies.append(pltpu.make_async_copy(done_ref.at[a], out_ref.at[:, a * blk : (a + 1) * blk], sems.at[a]))
        copies[-1].start()
    for copy in copies:
        copy.wait()


def vm(shape, dtype):
    return pltpu.VMEM(shape, dtype)


def per_device(completeness, stencil, features, frequencies, gal_cell, pip, pair_src, pair_count):
    bands, nx, ny = completeness.shape
    feats, galaxies = features.shape
    nfreq = frequencies.shape[1]
    nblk, slots, blk, _ = pip.shape
    n = bands * nx
    two = 2 * bands

    def call(body, out, args, anys=(), scratch=(), name=None, aliases=None, cost=1):
        return pl.pallas_call(
            body, out_shape=out, in_specs=[VMEM] * len(args) + [ANY] * len(anys), out_specs=jax.tree.map(lambda _: VMEM, out),
            scratch_shapes=scratch, compiler_params=params(), input_output_aliases=aliases or {}, name=name,
            cost_estimate=pl.CostEstimate(flops=cost, bytes_accessed=1, transcendentals=0),
        )(*args, *anys)

    cells = gal_cell.reshape(1, galaxies)
    given = [pltpu.with_memory_space_constraint(x, pltpu.HBM) for x in (completeness, features, frequencies, stencil, cells)]
    rim, rows, features, frequencies, stencil, cells = pl.pallas_call(
        rim_kernel,
        out_shape=(vm((RIM, n), BF16), vm((n, ny), F32)) + tuple(vm(x.shape, x.dtype) for x in given[1:]),
        in_specs=[HBM] * len(given), out_specs=(VMEM,) * 6, compiler_params=params(), name="rim",
        scratch_shapes=[pltpu.VMEM(completeness.shape, F32), pltpu.SemaphoreType.DMA((len(given),))],
    )(*given)
    d_odd, d_even = exchange("dec", rim, rim)
    taps, hit, own_features = call(
        functools.partial(ready_kernel, bands, nx, ny),
        (vm((stencil.shape[0] * bands, ny), F32), vm((n, galaxies), BF16), vm(features.shape, BF16)),
        (stencil, cells, features), (rim,), [pltpu.VMEM((32, 128), F32)], "ready",
    )
    f_odd, f_even = exchange("dec", own_features, own_features)

    to_odd, to_even = call(row_kernel, (vm((two + 2 * RIM, ny), BF16),) * 2, (rows, d_odd, d_even), (taps, hit), name="rows", cost=LONG)
    r_odd, r_even = exchange("ra", to_odd, to_even)
    inner = call(
        functools.partial(inner_kernel, bands), vm((n, ny), F32), (rows, d_odd, d_even, taps), (to_odd,),
        [pltpu.VMEM((5, n, ny), F32)], "inner",
    )
    column = call(stack_rows_kernel, vm((3 * feats, galaxies), BF16), (features, f_odd, f_even), (inner,), name="stack_features")
    c_odd, c_even = exchange("ra", column, column)

    def basis(first, tiles, arrays, buffer, after):
        shape = vm((9 * nblk, 2 * nfreq, blk), BF16)

        def body(freq_ref, *refs):
            outs = refs[-2:]
            basis_kernel(first, tiles, nblk, freq_ref, *refs[: len(arrays)], *outs)

        anys = (after,) if buffer is None else (after, buffer)
        return call(
            body, shape, (frequencies, *arrays), anys, [pltpu.VMEM((nfreq, feats), BF16)], "basis%d" % first,
            None if buffer is None else {len(arrays) + 2: 0},
        )

    table = basis(0, (1,), (features,), None, column)
    weight, table = call(
        functools.partial(weight_kernel, bands), (vm((RIM, galaxies), BF16), vm(table.shape, BF16)),
        (inner, r_odd, r_even, taps, hit, cells), (table,),
        [pltpu.VMEM((5, 2 * two, ny), F32), pltpu.VMEM((n, ny), F32)], "weight", {6: 1}, LONG,
    )
    w_odd, w_even = exchange("dec", weight, weight)
    table = basis(nblk, (1, 1), (f_odd, f_even), table, weight)
    table = basis(3 * nblk, (3,), (c_even,), table, weight)
    w_column, table = call(
        stack_weight_kernel, (vm((RIM, galaxies), BF16), vm(table.shape, BF16)), (weight, w_odd, w_even), (table,), name="stack_weights",
        aliases={3: 1},
    )
    x_odd, x_even = exchange("ra", w_column, w_column)
    table = basis(6 * nblk, (3,), (c_odd,), table, w_column)
    return pl.pallas_call(
        pair_kernel, out_shape=jax.ShapeDtypeStruct((nfreq, galaxies), BF16), in_specs=[SMEM, SMEM] + [VMEM] * 5, out_specs=ANY,
        scratch_shapes=[
            pltpu.VMEM((9 * nblk + 4, blk), F32), pltpu.VMEM((nblk, nfreq, blk), BF16), pltpu.SemaphoreType.DMA((nblk,)),
        ],
        compiler_params=params(), name="pairs",
    )(pair_src, pair_count, pip, table, w_column, x_odd, x_even)


def solution(mesh):
    in_specs = (
        P(None, "ra", "dec"),
        P(),
        P(None, ("ra", "dec")),
        P(),
        P(("ra", "dec")),
        P(("ra", "dec"), None, None, None),
        P(("ra", "dec"), None),
        P(("ra", "dec")),
    )
    out_specs = P(None, ("ra", "dec"))
    return jax.shard_map(per_device, mesh=mesh, in_specs=in_specs, out_specs=out_specs, check_vma=False)
```

time: 50.3 us -> 26.1 us (0.52)
  starting transfers between devices: 28.3 us -> 13 us
  local copies, waits for them, and re-layouts: 4.95 us -> 0.01 us
  waiting for transfers between devices: 4.96 us -> 0.89 us
    ppermute x12, starting transfers between devices: 28.3 us -> 13 us  [swap(): lax.ppermute(payload, ('ra', 'dec'), sorted(pairs + [(b, a) for a, b in p...]
    unnamed x20 -> x6, local copies, waits for them, and re-layouts: 4.95 us -> 0.01 us
    ppermute x12, waiting for transfers between devices: 4.96 us -> 0.89 us  [swap(): lax.ppermute(payload, ('ra', 'dec'), sorted(pairs + [(b, a) for a, b in p...]
    pallas_call x1, Pallas kernels: 0.26 us -> 1.27 us  [per_device(): pl.pallas_call(rim_kernel, out_shape=(vm((RIM, n), BF16), vm((n, ny), F32...]
    pallas_call x7 -> x10, Pallas kernels: 7.51 us -> 7.11 us  [call(): pl.pallas_call(body, out_shape=out, in_specs=[VMEM] * len(args) + [ANY] *...]
  transfers between devices with their start and end apart: 12 -> 12, of which waited for: 3 -> 2; matrix products, arithmetic and copies ran while one was open for 0% -> 0% of each run, Pallas kernels for 16% -> 28%
where the time goes in v2:
time: 26.1 us; the launch traced here: 25.6 us
  starting transfers between devices  13 us (50%)
  Pallas kernels  11.5 us (44%)
  waiting for transfers between devices  0.89 us (3%)
    ppermute x12, starting transfers between devices, swap(): lax.ppermute(payload, ('ra', 'dec'), sorted(pairs + [(b, a) for a, b in p...  13 us
    pallas_call x10, Pallas kernels, call(): pl.pallas_call(body, out_shape=out, in_specs=[VMEM] * len(args) + [ANY] *...  7.11 us
    pallas_call x1, Pallas kernels, per_device(): pl.pallas_call(pair_kernel, out_shape=jax.ShapeDtypeStruct((nfreq, galaxi...  3.14 us
    pallas_call x1, Pallas kernels, per_device(): pl.pallas_call(rim_kernel, out_shape=(vm((RIM, n), BF16), vm((n, ny), F32...  1.27 us
    ppermute x12, waiting for transfers between devices, swap(): lax.ppermute(payload, ('ra', 'dec'), sorted(pairs + [(b, a) for a, b in p...  0.89 us
  transfers between devices with their start and end apart: 12, of which 2 were waited for; matrix products, arithmetic and copies ran while one was open for 0% of the time, Pallas kernels for 28%

profile of v2, /device:TPU:1, one launch (start us, length us, event | category | flops | bytes accessed | tf_op | source)
XLA Modules:
  0.0 25.6 jit_solution(1023501071866548774)
XLA Ops:
  0.0 1.3 %rim.1 = (bf16[16,512]{1,0:T(8,128)(2,1)S(1)}, f32[512,128]{1,0:T(8,128)S(1)}, bf16[96,512]{1,0:T(8,128)(2,1)S(1)}, bf16[96,256]{1,0:T(8,128)(2,1)S(1)}, f32[25,64]{1,0:T(8,128)S(1)}, /*index=5*/s32[1,512]{1,0:T(1,128)S(1)}) custom-call(f32[64,8,128]{2,1,0:T(8,128)} %comp_hbm.1, bf16[96,512]{1,0:T(8,128)(2,1)} %feat_hbm.1, bf16[96,256]{1,0:T(8,128)(2,1)} %freq_hbm.1, ...), custom_call_target="tpu_custom_call" | custom-call | tf_op jit(solution)/shard_map/rim/pallas_call | solution.py:292
  1.3 0.1 collective-permute-start.2
  1.4 3.4 %collective-permute-start.3 = (bf16[16,512]{1,0:T(8,128)(2,1)S(1)}, bf16[16,512]{1,0:T(8,128)(2,1)S(1)}, u32[]{:S(2)}, u32[]{:S(2)}) collective-permute-start(bf16[16,512]{1,0:T(8,128)(2,1)S(1)} %get-tuple-element.24.rim_ref), channel_id=1, source_target_pairs={{0,1},{1,0},{2,3},{3,2},{4,5},{5,4},{6,7},{7,6},{8,9},{9,8},{10,11... | collective-permute-start | bytes 49160 | tf_op jit(solution)/shard_map/ppermute | solution.py:40
  4.8 0.5 %ready.1 = (f32[1600,128]{1,0:T(8,128)S(1)}, bf16[512,512]{1,0:T(8,128)(2,1)S(1)}, bf16[96,512]{1,0:T(8,128)(2,1)S(1)}) custom-call(f32[25,64]{1,0:T(8,128)S(1)} %get-tuple-element.22.stencil_ref, s32[1,512]{1,0:T(1,128)S(1)} %get-tuple-element.23.cell_ref, bf16[96,512]{1,0:T(8,128)(2,1)S(1)} %get-tuple-element.21.feat_ref.a_ref.refs_0_, ...), custom_call_target="tpu_custom_call" | custom-call | flops 1 | bytes 1 | tf_op jit(solution)/shard_map/ready/pallas_call | solution.py:284
  5.3 1.3 %collective-permute-start = (bf16[96,512]{1,0:T(8,128)(2,1)S(1)}, bf16[96,512]{1,0:T(8,128)(2,1)S(1)}, u32[]{:S(2)}, u32[]{:S(2)}) collective-permute-start(bf16[96,512]{1,0:T(8,128)(2,1)S(1)} %get-tuple-element.25), channel_id=1, source_target_pairs={{0,4},{1,2},{2,1},{3,7},{4,0},{5,6},{6,5},{7,3},{8,12},{9,10},{10,... | collective-permute-start | bytes 294920 | tf_op jit(solution)/shard_map/ppermute | solution.py:40
  6.6 0.8 %collective-permute-start.1 = (bf16[96,512]{1,0:T(8,128)(2,1)S(1)}, bf16[96,512]{1,0:T(8,128)(2,1)S(1)}, u32[]{:S(2)}, u32[]{:S(2)}) collective-permute-start(bf16[96,512]{1,0:T(8,128)(2,1)S(1)} %get-tuple-element.25), channel_id=1, source_target_pairs={{0,1},{1,0},{2,3},{3,2},{4,5},{5,4},{6,7},{7,6},{8,9},{9,8},{10,11... | collective-permute-start | bytes 294920 | tf_op jit(solution)/shard_map/ppermute | solution.py:40
  7.4 0.0 collective-permute-done.2.odd_ref
  7.4 0.0 collective-permute-done.3.even_ref
  7.4 2.1 %collective-permute-start.5 = (bf16[160,128]{1,0:T(8,128)(2,1)S(1)}, bf16[160,128]{1,0:T(8,128)(2,1)S(1)}, u32[]{:S(2)}, u32[]{:S(2)}) collective-permute-start(bf16[160,128]{1,0:T(8,128)(2,1)S(1)} %get-tuple-element.29.to_odd_ref), channel_id=1, source_target_pairs={{0,1},{1,0},{2,3},{3,2},{4,8},{5,9},{6,10},{7,11},{8,4},{9,5},{10,... | collective-permute-start | bytes 122888 | tf_op jit(solution)/shard_map/ppermute | solution.py:40
  9.4 0.4 %collective-permute-start.6 = (bf16[160,128]{1,0:T(8,128)(2,1)S(1)}, bf16[160,128]{1,0:T(8,128)(2,1)S(1)}, u32[]{:S(2)}, u32[]{:S(2)}) collective-permute-start(bf16[160,128]{1,0:T(8,128)(2,1)S(1)} %get-tuple-element.30), channel_id=1, source_target_pairs={{0,4},{1,5},{2,6},{3,7},{4,0},{5,1},{6,2},{7,3},{8,12},{9,13},{10,... | collective-permute-start | bytes 122888 | tf_op jit(solution)/shard_map/ppermute | solution.py:40
  9.8 1.0 %inner.1.after_ref.inner_ref = f32[512,128]{1,0:T(8,128)S(1)} custom-call(f32[512,128]{1,0:T(8,128)S(1)} %get-tuple-element.26.rows_ref, bf16[16,512]{1,0:T(8,128)(2,1)S(1)} %collective-permute-done.2.odd_ref, bf16[16,512]{1,0:T(8,128)(2,1)S(1)} %collective-permute-done.3.even_ref, f32[1600,128]{1,0:T(8,128)S(1)} %get-tuple-element.27.taps_ref, ...), custom_call_target="tpu_custom_call" | custom-call | flops 1 | bytes 1 | tf_op jit(solution)/shard_map/inner/pallas_call | solution.py:284
  10.8 0.0 collective-permute-done.b_ref.refs_0_
  10.8 0.2 collective-permute-done.1.c_ref.refs_1_
  11.0 0.9 %collective-permute-start.9 = (bf16[288,512]{1,0:T(8,128)(2,1)S(1)}, bf16[288,512]{1,0:T(8,128)(2,1)S(1)}, u32[]{:S(2)}, u32[]{:S(2)}) collective-permute-start(bf16[288,512]{1,0:T(8,128)(2,1)S(1)} %stack_features.1.refs_1_), channel_id=1, source_target_pairs={{0,4},{1,5},{2,6},{3,7},{4,0},{5,1},{6,2},{7,3},{8,12},{9,13},{10,... | collective-permute-start | bytes 884744 | tf_op jit(solution)/shard_map/ppermute | solution.py:40
  11.9 1.2 %collective-permute-start.4 = (bf16[288,512]{1,0:T(8,128)(2,1)S(1)}, bf16[288,512]{1,0:T(8,128)(2,1)S(1)}, u32[]{:S(2)}, u32[]{:S(2)}) collective-permute-start(bf16[288,512]{1,0:T(8,128)(2,1)S(1)} %stack_features.1.refs_1_), channel_id=1, source_target_pairs={{0,1},{1,0},{2,3},{3,2},{4,8},{5,9},{6,10},{7,11},{8,4},{9,5},{10,... | collective-permute-start | bytes 884744 | tf_op jit(solution)/shard_map/ppermute | solution.py:40
  13.1 0.6 %basis0.1.basis_in_ref = bf16[36,512,128]{2,1,0:T(8,128)(2,1)S(1)} custom-call(bf16[96,256]{1,0:T(8,128)(2,1)S(1)} %get-tuple-element.20.freq_ref, bf16[96,512]{1,0:T(8,128)(2,1)S(1)} %get-tuple-element.21.feat_ref.a_ref.refs_0_, bf16[288,512]{1,0:T(8,128)(2,1)S(1)} %stack_features.1.refs_1_), custom_call_target="tpu_custom_call" | custom-call | flops 1 | bytes 1 | tf_op jit(solution)/shard_map/basis0/pallas_call | solution.py:284
  13.7 0.0 collective-permute-done.5.odd_ref
  13.8 0.0 collective-permute-done.6.even_ref
  13.8 0.8 %weight.1 = (bf16[16,512]{1,0:T(8,128)(2,1)S(1)}, bf16[36,512,128]{2,1,0:T(8,128)(2,1)S(1)}) custom-call(f32[512,128]{1,0:T(8,128)S(1)} %inner.1.after_ref.inner_ref, bf16[160,128]{1,0:T(8,128)(2,1)S(1)} %collective-permute-done.5.odd_ref, bf16[160,128]{1,0:T(8,128)(2,1)S(1)} %collective-permute-done.6.even_ref, ...), custom_call_target="tpu_custom_call", output_to_operand_aliasing={{1}: (6, {})} | custom-call | flops 68719476736 | bytes 1 | tf_op jit(solution)/shard_map/weight/pallas_call | solution.py:284
  14.5 0.1 collective-permute-start.7
  14.6 0.8 %collective-permute-start.8 = (bf16[16,512]{1,0:T(8,128)(2,1)S(1)}, bf16[16,512]{1,0:T(8,128)(2,1)S(1)}, u32[]{:S(2)}, u32[]{:S(2)}) collective-permute-start(bf16[16,512]{1,0:T(8,128)(2,1)S(1)} %get-tuple-element.31.refs_2_.refs_1_.own_ref), channel_id=1, source_target_pairs={{0,1},{1,0},{2,3},{3,2},{4,5},{5,4},{6,7},{7,6},{8,9},{9,8},{10,11... | collective-permute-start | bytes 49160 | tf_op jit(solution)/shard_map/ppermute | solution.py:40
  15.5 1.1 %basis4.1.refs_2_ = bf16[36,512,128]{2,1,0:T(8,128)(2,1)S(1)} custom-call(bf16[96,256]{1,0:T(8,128)(2,1)S(1)} %get-tuple-element.20.freq_ref, bf16[96,512]{1,0:T(8,128)(2,1)S(1)} %collective-permute-done.b_ref.refs_0_, bf16[96,512]{1,0:T(8,128)(2,1)S(1)} %collective-permute-done.1.c_ref.refs_1_, ...), custom_call_target="tpu_custom_call", output_to_operand_aliasing={{}: (4, {})} | custom-call | flops 1 | bytes 1 | tf_op jit(solution)/shard_map/basis4/pallas_call | solution.py:284
  16.5 0.0 collective-permute-done.9.refs_0_
  16.5 1.5 %basis12.1.basis_in_ref = bf16[36,512,128]{2,1,0:T(8,128)(2,1)S(1)} custom-call(bf16[96,256]{1,0:T(8,128)(2,1)S(1)} %get-tuple-element.20.freq_ref, bf16[288,512]{1,0:T(8,128)(2,1)S(1)} %collective-permute-done.9.refs_0_, bf16[16,512]{1,0:T(8,128)(2,1)S(1)} %get-tuple-element.31.refs_2_.refs_1_.own_ref, ...), custom_call_target="tpu_custom_call", output_to_operand_aliasing={{}: (3, {})} | custom-call | flops 1 | bytes 1 | tf_op jit(solution)/shard_map/basis12/pallas_call | solution.py:284
  18.1 0.0 collective-permute-done.7.odd_ref
  18.1 0.0 collective-permute-done.8.even_ref
  18.1 1.9 %collective-permute-start.10 = (bf16[16,512]{1,0:T(8,128)(2,1)S(1)}, bf16[16,512]{1,0:T(8,128)(2,1)S(1)}, u32[]{:S(2)}, u32[]{:S(2)}) collective-permute-start(bf16[16,512]{1,0:T(8,128)(2,1)S(1)} %get-tuple-element.33.refs_1_.w_own_ref), channel_id=1, source_target_pairs={{0,1},{1,0},{2,3},{3,2},{4,8},{5,9},{6,10},{7,11},{8,4},{9,5},{10,... | collective-permute-start | bytes 49160 | tf_op jit(solution)/shard_map/ppermute | solution.py:40
  20.0 0.2 collective-permute-start.11
  20.2 0.7 %collective-permute-done.4.refs_0_ = bf16[288,512]{1,0:T(8,128)(2,1)S(1)} collective-permute-done((bf16[288,512]{1,0:T(8,128)(2,1)S(1)}, bf16[288,512]{1,0:T(8,128)(2,1)S(1)}, u32[]{:S(2)}, u32[]{:S(2)}) %collective-permute-start.4) | collective-permute-done | bytes 294944 | tf_op jit(solution)/shard_map/ppermute | solution.py:40
  20.9 0.0 copy-start
  20.9 0.0 copy-start.1
  20.9 0.0 copy-start.2
  20.9 1.5 %basis24.1.basis_ref = bf16[36,512,128]{2,1,0:T(8,128)(2,1)S(1)} custom-call(bf16[96,256]{1,0:T(8,128)(2,1)S(1)} %get-tuple-element.20.freq_ref, bf16[288,512]{1,0:T(8,128)(2,1)S(1)} %collective-permute-done.4.refs_0_, bf16[16,512]{1,0:T(8,128)(2,1)S(1)} %get-tuple-element.33.refs_1_.w_own_ref, ...), custom_call_target="tpu_custom_call", output_to_operand_aliasing={{}: (3, {})} | custom-call | flops 1 | bytes 1 | tf_op jit(solution)/shard_map/basis24/pallas_call | solution.py:284
  22.4 0.0 collective-permute-done.10.w_odd_ref
  22.4 0.0 collective-permute-done.11.w_even_ref
  22.5 0.0 copy-done
  22.5 0.0 copy-done.1
  22.5 0.0 copy-done.2
  22.5 3.1 %pairs.1 = bf16[256,512]{1,0:T(8,128)(2,1)} custom-call(s32[4,12]{1,0:T(4,128)S(1)} %copy-done.1, s32[4]{0:T(128)S(1)} %copy-done.2, bf16[4,12,128,128]{3,2,1,0:T(8,128)(2,1)S(1)} %copy-done, bf16[36,512,128]{2,1,0:T(8,128)(2,1)S(1)} %basis24.1.basis_ref, bf16[16,512]{1,0:T(8,128)(2,1)S(1)} %get-tuple-element.33.refs_1_.w_own_ref, ...), custom_call_target="tpu_custom_call" | custom-call | tf_op jit(solution)/shard_map/pairs/pallas_call | solution.py:343
  (3 shorter events, 0.1 us)
Async XLA Ops:
  1.3 6.1 %collective-permute-start.2 = (bf16[16,512]{1,0:T(8,128)(2,1)S(1)}, bf16[16,512]{1,0:T(8,128)(2,1)S(1)}, u32[]{:S(2)}, u32[]{:S(2)}) collective-permute-start(bf16[16,512]{1,0:T(8,128)(2,1)S(1)} %get-tuple-element.24.rim_ref), channel_id=1, source_target_pairs={{0,4},{1,2},{2,1},{3,7},{4,0},{5,6},{6,5},{7,3},{8,12},{9,10},{10,... | collective-permute-start | bytes 49160 | tf_op jit(solution)/shard_map/ppermute | solution.py:40
  1.4 6.0 %collective-permute-start.3 = (bf16[16,512]{1,0:T(8,128)(2,1)S(1)}, bf16[16,512]{1,0:T(8,128)(2,1)S(1)}, u32[]{:S(2)}, u32[]{:S(2)}) collective-permute-start(bf16[16,512]{1,0:T(8,128)(2,1)S(1)} %get-tuple-element.24.rim_ref), channel_id=1, source_target_pairs={{0,1},{1,0},{2,3},{3,2},{4,5},{5,4},{6,7},{7,6},{8,9},{9,8},{10,11... | collective-permute-start | bytes 49160 | tf_op jit(solution)/shard_map/ppermute | solution.py:40
  5.3 5.5 %collective-permute-start = (bf16[96,512]{1,0:T(8,128)(2,1)S(1)}, bf16[96,512]{1,0:T(8,128)(2,1)S(1)}, u32[]{:S(2)}, u32[]{:S(2)}) collective-permute-start(bf16[96,512]{1,0:T(8,128)(2,1)S(1)} %get-tuple-element.25), channel_id=1, source_target_pairs={{0,4},{1,2},{2,1},{3,7},{4,0},{5,6},{6,5},{7,3},{8,12},{9,10},{10,... | collective-permute-start | bytes 294920 | tf_op jit(solution)/shard_map/ppermute | solution.py:40
  6.6 4.4 %collective-permute-start.1 = (bf16[96,512]{1,0:T(8,128)(2,1)S(1)}, bf16[96,512]{1,0:T(8,128)(2,1)S(1)}, u32[]{:S(2)}, u32[]{:S(2)}) collective-permute-start(bf16[96,512]{1,0:T(8,128)(2,1)S(1)} %get-tuple-element.25), channel_id=1, source_target_pairs={{0,1},{1,0},{2,3},{3,2},{4,5},{5,4},{6,7},{7,6},{8,9},{9,8},{10,11... | collective-permute-start | bytes 294920 | tf_op jit(solution)/shard_map/ppermute | solution.py:40
  7.4 6.4 %collective-permute-start.5 = (bf16[160,128]{1,0:T(8,128)(2,1)S(1)}, bf16[160,128]{1,0:T(8,128)(2,1)S(1)}, u32[]{:S(2)}, u32[]{:S(2)}) collective-permute-start(bf16[160,128]{1,0:T(8,128)(2,1)S(1)} %get-tuple-element.29.to_odd_ref), channel_id=1, source_target_pairs={{0,1},{1,0},{2,3},{3,2},{4,8},{5,9},{6,10},{7,11},{8,4},{9,5},{10,... | collective-permute-start | bytes 122888 | tf_op jit(solution)/shard_map/ppermute | solution.py:40
  9.4 4.3 %collective-permute-start.6 = (bf16[160,128]{1,0:T(8,128)(2,1)S(1)}, bf16[160,128]{1,0:T(8,128)(2,1)S(1)}, u32[]{:S(2)}, u32[]{:S(2)}) collective-permute-start(bf16[160,128]{1,0:T(8,128)(2,1)S(1)} %get-tuple-element.30), channel_id=1, source_target_pairs={{0,4},{1,5},{2,6},{3,7},{4,0},{5,1},{6,2},{7,3},{8,12},{9,13},{10,... | collective-permute-start | bytes 122888 | tf_op jit(solution)/shard_map/ppermute | solution.py:40
  11.0 5.5 %collective-permute-start.9 = (bf16[288,512]{1,0:T(8,128)(2,1)S(1)}, bf16[288,512]{1,0:T(8,128)(2,1)S(1)}, u32[]{:S(2)}, u32[]{:S(2)}) collective-permute-start(bf16[288,512]{1,0:T(8,128)(2,1)S(1)} %stack_features.1.refs_1_), channel_id=1, source_target_pairs={{0,4},{1,5},{2,6},{3,7},{4,0},{5,1},{6,2},{7,3},{8,12},{9,13},{10,... | collective-permute-start | bytes 884744 | tf_op jit(solution)/shard_map/ppermute | solution.py:40
  11.9 9.0 %collective-permute-start.4 = (bf16[288,512]{1,0:T(8,128)(2,1)S(1)}, bf16[288,512]{1,0:T(8,128)(2,1)S(1)}, u32[]{:S(2)}, u32[]{:S(2)}) collective-permute-start(bf16[288,512]{1,0:T(8,128)(2,1)S(1)} %stack_features.1.refs_1_), channel_id=1, source_target_pairs={{0,1},{1,0},{2,3},{3,2},{4,8},{5,9},{6,10},{7,11},{8,4},{9,5},{10,... | collective-permute-start | bytes 884744 | tf_op jit(solution)/shard_map/ppermute | solution.py:40
  14.5 3.6 %collective-permute-start.7 = (bf16[16,512]{1,0:T(8,128)(2,1)S(1)}, bf16[16,512]{1,0:T(8,128)(2,1)S(1)}, u32[]{:S(2)}, u32[]{:S(2)}) collective-permute-start(bf16[16,512]{1,0:T(8,128)(2,1)S(1)} %get-tuple-element.31.refs_2_.refs_1_.own_ref), channel_id=1, source_target_pairs={{0,4},{1,2},{2,1},{3,7},{4,0},{5,6},{6,5},{7,3},{8,12},{9,10},{10,... | collective-permute-start | bytes 49160 | tf_op jit(solution)/shard_map/ppermute | solution.py:40
  14.6 3.5 %collective-permute-start.8 = (bf16[16,512]{1,0:T(8,128)(2,1)S(1)}, bf16[16,512]{1,0:T(8,128)(2,1)S(1)}, u32[]{:S(2)}, u32[]{:S(2)}) collective-permute-start(bf16[16,512]{1,0:T(8,128)(2,1)S(1)} %get-tuple-element.31.refs_2_.refs_1_.own_ref), channel_id=1, source_target_pairs={{0,1},{1,0},{2,3},{3,2},{4,5},{5,4},{6,7},{7,6},{8,9},{9,8},{10,11... | collective-permute-start | bytes 49160 | tf_op jit(solution)/shard_map/ppermute | solution.py:40
  18.1 4.3 %collective-permute-start.10 = (bf16[16,512]{1,0:T(8,128)(2,1)S(1)}, bf16[16,512]{1,0:T(8,128)(2,1)S(1)}, u32[]{:S(2)}, u32[]{:S(2)}) collective-permute-start(bf16[16,512]{1,0:T(8,128)(2,1)S(1)} %get-tuple-element.33.refs_1_.w_own_ref), channel_id=1, source_target_pairs={{0,1},{1,0},{2,3},{3,2},{4,8},{5,9},{6,10},{7,11},{8,4},{9,5},{10,... | collective-permute-start | bytes 49160 | tf_op jit(solution)/shard_map/ppermute | solution.py:40
  20.0 2.4 %collective-permute-start.11 = (bf16[16,512]{1,0:T(8,128)(2,1)S(1)}, bf16[16,512]{1,0:T(8,128)(2,1)S(1)}, u32[]{:S(2)}, u32[]{:S(2)}) collective-permute-start(bf16[16,512]{1,0:T(8,128)(2,1)S(1)} %get-tuple-element.33.refs_1_.w_own_ref), channel_id=1, source_target_pairs={{0,4},{1,5},{2,6},{3,7},{4,0},{5,1},{6,2},{7,3},{8,12},{9,13},{10,... | collective-permute-start | bytes 49160 | tf_op jit(solution)/shard_map/ppermute | solution.py:40
  20.9 1.6 %copy-start = (bf16[4,12,128,128]{3,2,1,0:T(8,128)(2,1)S(1)}, bf16[4,12,128,128]{3,2,1,0:T(8,128)(2,1)}, u32[]{:S(2)}) copy-start(bf16[4,12,128,128]{3,2,1,0:T(8,128)(2,1)} %pip_ref.1) | copy-start | bytes 4718596
  20.9 1.6 %copy-start.1 = (s32[4,12]{1,0:T(4,128)S(1)}, s32[4,12]{1,0:T(4,128)}, u32[]{:S(2)}) copy-start(s32[4,12]{1,0:T(4,128)} %src_ref.1) | copy-start | bytes 580
  20.9 1.6 %copy-start.2 = (s32[4]{0:T(128)S(1)}, s32[4]{0:T(128)}, u32[]{:S(2)}) copy-start(s32[4]{0:T(128)} %count_ref.1) | copy-start | bytes 52

commit v3 on v2

v3 whole, which is shorter than its diff:
```python
import functools
import math

import jax
import jax.numpy as jnp
from jax import lax
from jax.experimental import pallas as pl
from jax.experimental.pallas import tpu as pltpu
from jax.sharding import PartitionSpec as P

BF16 = jnp.bfloat16
F32 = jnp.float32
LONG = 1 << 36
FIRST = 6
RIM = 16

VMEM = pl.BlockSpec(memory_space=pltpu.VMEM)
SMEM = pl.BlockSpec(memory_space=pltpu.SMEM)
ANY = pl.BlockSpec(memory_space=pl.ANY)
HBM = pl.BlockSpec(memory_space=pltpu.HBM)

COS = (0.99999922, -19.73898252, 64.92872662, -85.27239701, 58.79403871, -21.07678212)
SIN = (6.2830558, -41.33121431, 81.36681529, -74.47800454, 32.7814008)


def params(limit=None, **kw):
    return pltpu.CompilerParams(vmem_limit_bytes=limit or (16 << 20), **kw)


def exchange(axis, odd_payload, even_payload):
    ra, dec = lax.axis_size("ra"), lax.axis_size("dec")
    here = (lambda r, d: r * dec + d) if axis == "ra" else (lambda d, r: r * dec + d)
    count, other = (ra, dec) if axis == "ra" else (dec, ra)

    def swap(payload, odd):
        pairs = [(here(i, k), here(i + 1, k)) for i in range(odd, count - 1, 2) for k in range(other)]
        busy = {i for pair in pairs for i in pair}
        for i in (0, count - 1):
            ends = [(here(i, k), here(i, k + 1)) for k in range(0, other - 1, 2)]
            pairs += [pair for pair in ends if not busy & set(pair)]
        return lax.ppermute(payload, ("ra", "dec"), sorted(pairs + [(b, a) for a, b in pairs]))

    if axis == "ra":
        even = swap(even_payload, 0)
        return swap(odd_payload, 1), even
    odd = swap(odd_payload, 1)
    return odd, swap(even_payload, 0)


def sides(axis):
    i, n = lax.axis_index(axis), lax.axis_size(axis)
    odd = lax.rem(i, 2) == 1
    return odd, jnp.logical_and(i > 0, jnp.logical_not(jnp.logical_and(odd, i == n - 1)))


def dot(a, b, ca, cb):
    return lax.dot_general(a, b, (((ca,), (cb,)), ((), ())), preferred_element_type=F32)


def rim_kernel(*refs):
    count = (len(refs) - 3) // 2
    given, (rim_ref, rows_ref), kept = refs[:count], refs[count : count + 2], refs[count + 2 : -2]
    comp_ref, sems = refs[-2:]
    bands, nx, ny = comp_ref.shape
    copies = [pltpu.make_async_copy(a, b, sems.at[i]) for i, (a, b) in enumerate(zip(given, (comp_ref, *kept), strict=True))]
    for copy in copies:
        copy.start()
    row = lax.broadcasted_iota(jnp.int32, (RIM, ny), 0)
    lane = lax.broadcasted_iota(jnp.int32, (RIM, ny), 1)
    pick = ((row < 2) & (lane == row)) | ((row >= 2) & (row < 4) & (lane == row + ny - 4))
    copies[0].wait()
    for x in range(nx):
        rows_ref[x * bands : (x + 1) * bands, :] = comp_ref[:, x, :]
    rim_ref[...] = dot(pick.astype(F32).astype(BF16), rows_ref[...].astype(BF16), 1, 1).astype(BF16)
    for copy in copies[1:]:
        copy.wait()


def list_slots(nblk, src_ref, count_ref, code_ref, tile_ref):
    own, slots = src_ref.shape
    blocks, half = 9 * nblk, own * FIRST
    ra_odd, _ = sides("ra")
    dec_odd, _ = sides("dec")
    ra_up, dec_up = jnp.where(ra_odd, 2, 1), jnp.where(dec_odd, 1, 2)
    for i, ra_at in enumerate((3 - ra_up, 0, ra_up)):
        for j, dec_at in enumerate((3 - dec_up, 0, dec_up)):
            tile_ref[3 * i + j] = (3 * ra_at + dec_at) * nblk
    for i in range(half + own * slots):
        code_ref[i] = blocks * 65536
    steps = jnp.int32(0)
    for a in range(own):
        early, late = jnp.int32(0), jnp.int32(0)
        for p in range(slots):
            s = src_ref[a, p]
            at = tile_ref[lax.div(s, nblk)] + lax.rem(s, nblk)
            live = p < count_ref[a]
            soon = jnp.logical_and(at < 6 * nblk, early < FIRST)
            to = jnp.where(soon, a * FIRST + early, half + a * slots + late)
            code_ref[jnp.where(live, to, half + own * slots + 1)] = p + at * (256 + 65536)
            early = early + jnp.where(jnp.logical_and(live, soon), 1, 0)
            late = late + jnp.where(jnp.logical_and(live, jnp.logical_not(soon)), 1, 0)
        steps = jnp.maximum(steps, lax.div(late + 1, 2))
    code_ref[half + own * slots] = steps


def ready_kernel(bands, nx, ny, stencil_ref, cell_ref, rim_ref, taps_ref, lane_taps_ref, hit_ref, st_ref):
    st_ref[...] = jnp.zeros_like(st_ref)
    count = stencil_ref.shape[0]
    st_ref[0:count, 0:bands] = stencil_ref[...]
    st_ref[0:count, bands : 2 * bands] = stencil_ref[...]
    by_band = st_ref[...].T
    for k in range(count):
        taps_ref[k * bands : (k + 1) * bands, :] = jnp.broadcast_to(by_band[0:bands, k : k + 1], (bands, ny))
    along = jnp.concatenate([st_ref[...]] * (nx // 2), 1)
    lane_taps_ref[...] = jnp.zeros_like(lane_taps_ref)
    for a in range(5):
        for row, c in ((0, 0), (1, 0), (2, 4), (3, 3), (8, 1), (11, 4)):
            lane_taps_ref[16 * a + row : 16 * a + row + 1, :] = along[5 * a + c : 5 * a + c + 1, :]
    cell = cell_ref[...]
    slot = (cell // ny % nx) * bands + cell // (nx * ny)
    hit = lax.broadcasted_iota(jnp.int32, hit_ref.shape, 0) == slot
    hit_ref[...] = jnp.where(hit, 1.0, 0.0).astype(BF16)


def row_kernel(rows_ref, odd_ref, even_ref, after_ref, to_odd_ref, to_even_ref):
    n = rows_ref.shape[0]
    two = to_odd_ref.shape[0] - 2 * RIM
    is_odd, _ = sides("ra")

    def put(ref, start):
        ref[0:two, :] = rows_ref[start : start + two, :].astype(BF16)
        ref[two : two + RIM, :] = odd_ref[:, start : start + two]
        ref[two + RIM :, :] = even_ref[:, start : start + two]

    @pl.when(is_odd)
    def _():
        put(to_odd_ref, n - two)
        put(to_even_ref, 0)

    @pl.when(jnp.logical_not(is_odd))
    def _():
        put(to_odd_ref, 0)
        put(to_even_ref, n - two)


def picks():
    dec_odd, has_odd = sides("dec")
    row = lax.broadcasted_iota(jnp.int32, (RIM, RIM), 0)
    lane = lax.broadcasted_iota(jnp.int32, (RIM, RIM), 1)

    def ones(*spots):
        return functools.reduce(jnp.logical_or, [(row == r) & (lane == k) for r, k in spots]).astype(F32)

    before, after = ones((0, 2), (1, 3), (8, 3)), ones((2, 0), (3, 0), (11, 1))
    odd = jnp.where(has_odd, jnp.where(dec_odd, after, before), 0.0)
    return odd.astype(BF16), jnp.where(dec_odd, before, after).astype(BF16)


def edge_sums(lane_taps_ref, bands, columns):
    width = columns.shape[1]
    size = lane_taps_ref.shape[1]
    total = jnp.zeros((RIM, size), F32)
    for a in range(5):
        moved = columns if a == 0 else pltpu.roll(columns, width - a * bands, 1)
        total = total + lane_taps_ref[16 * a : 16 * a + 16, :] * moved[:, 0:size]
    return total[0:8] + total[8:16]


def extend(ext_ref, cells):
    ny = cells.shape[1]
    at = lax.broadcasted_iota(jnp.int32, cells.shape, 1)
    ext_ref[2] = cells
    ext_ref[3] = jnp.where(at > ny - 2, 0.0, pltpu.roll(cells, ny - 1, 1))
    ext_ref[4] = jnp.where(at > ny - 3, 0.0, pltpu.roll(cells, ny - 2, 1))
    ext_ref[1] = jnp.where(at < 1, 0.0, pltpu.roll(cells, 1, 1))
    ext_ref[0] = jnp.where(at < 2, 0.0, pltpu.roll(cells, 2, 1))


def split(x):
    high = x.astype(BF16)
    return high, (x - high.astype(F32)).astype(BF16)


def at_column(table, hits, cell):
    high, low = split(table)
    found = dot(high, hits, 0, 0) + dot(low, hits, 0, 0)
    at = lax.broadcasted_iota(jnp.int32, found.shape, 0) == cell % table.shape[1]
    return jnp.sum(jnp.where(at, found, 0.0), axis=0, keepdims=True)


def at_edge(edges, hits, cell, ny):
    found = dot(jnp.concatenate(split(edges), 0), hits, 1, 0)
    found = found[0:8] + found[8:16]
    y = cell % ny
    row = jnp.where(y < 2, y, jnp.where(y > ny - 3, y - (ny - 4), 8))
    return jnp.sum(jnp.where(lax.broadcasted_iota(jnp.int32, found.shape, 0) == row, found, 0.0), axis=0, keepdims=True)


def inner_kernel(bands, rows_ref, taps_ref, out_ref, ext_ref):
    n, ny = rows_ref.shape
    nx = n // bands
    extend(ext_ref, rows_ref[...])
    for g in range(0, bands, 8):
        accs = [jnp.zeros((8, ny), F32) for _ in range(nx)]
        for c in range(5):
            for a in range(5):
                w = taps_ref[(5 * a + c) * bands + g : (5 * a + c) * bands + g + 8, :]
                for x in range(nx):
                    if 0 <= x + a - 2 < nx:
                        base = (x + a - 2) * bands + g
                        accs[x] = accs[x] + w * ext_ref[c, base : base + 8, :]
        for x in range(nx):
            out_ref[x * bands + g : x * bands + g + 8, :] = accs[x]


def side_sums(ext_ref, taps_ref, bands, up, put):
    parts = (((4, 0),), ((3, 0), (4, 1))) if up else (((0, 0), (1, 1)), ((0, 1),))
    for g in range(0, bands, 8):
        for x, terms in enumerate(parts):
            acc = None
            for a, e in terms:
                for c in range(5):
                    tap = (5 * a + c) * bands + g
                    term = taps_ref[tap : tap + 8, :] * ext_ref[c, e * bands + g : e * bands + g + 8, :]
                    acc = term if acc is None else acc + term
            put(x * bands + g, acc)


def even_side_kernel(bands, inner_ref, odd_ref, even_ref, rows_ref, taps_ref, lane_taps_ref, hit_ref, cell_ref, out_ref, ext_ref, sum_ref):
    n, ny = inner_ref.shape
    two = 2 * bands
    ra_odd, _ = sides("ra")
    sum_ref[...] = inner_ref[...]
    extend(ext_ref, rows_ref[0:two, :].astype(F32))

    def add_from(start):
        def put(at, value):
            sum_ref[start + at : start + at + 8, :] += value

        return put

    pl.when(ra_odd)(lambda: side_sums(ext_ref, taps_ref, bands, False, add_from(0)))
    pl.when(jnp.logical_not(ra_odd))(lambda: side_sums(ext_ref, taps_ref, bands, True, add_from(n - two)))

    odd, even = picks()
    own = dot(odd, odd_ref[...], 1, 0) + dot(even, even_ref[...], 1, 0)
    beside = dot(odd, rows_ref[two : two + RIM, :], 1, 0) + dot(even, rows_ref[two + RIM :, :], 1, 0)
    columns = jnp.concatenate([jnp.where(ra_odd, beside, 0.0), own, jnp.where(ra_odd, 0.0, beside)], 1)
    edges = edge_sums(lane_taps_ref, bands, columns)
    cell = cell_ref[...]
    value = at_column(sum_ref[...], hit_ref[...], cell) + at_edge(edges, hit_ref[...], cell, ny)
    out_ref[...] = jnp.broadcast_to(value, out_ref.shape)


def weight_kernel(bands, even_side_ref, rows_ref, taps_ref, lane_taps_ref, hit_ref, cell_ref, basis_in_ref, out_ref, basis_ref, ext_ref, sum_ref):
    two, ny = sum_ref.shape
    n = hit_ref.shape[0]
    ra_odd, has_odd = sides("ra")
    extend(ext_ref, jnp.where(has_odd, rows_ref[0:two, :].astype(F32), 0.0))

    def put(at, value):
        sum_ref[at : at + 8, :] = value

    pl.when(ra_odd)(lambda: side_sums(ext_ref, taps_ref, bands, True, put))
    pl.when(jnp.logical_not(ra_odd))(lambda: side_sums(ext_ref, taps_ref, bands, False, put))

    odd, even = picks()
    beside = dot(odd, rows_ref[two : two + RIM, :], 1, 0) + dot(even, rows_ref[two + RIM :, :], 1, 0)
    beside = jnp.where(has_odd, beside, 0.0)
    columns = jnp.concatenate([jnp.where(ra_odd, 0.0, beside), jnp.zeros((RIM, n), F32), jnp.where(ra_odd, beside, 0.0)], 1)
    edges = edge_sums(lane_taps_ref, bands, columns)
    edges = jnp.where(ra_odd, edges[:, n - two :], edges[:, 0:two])
    hits = hit_ref[pl.ds(pl.multiple_of(jnp.where(ra_odd, n - two, 0), two), two), :]
    cell = cell_ref[...]
    value = even_side_ref[0:1, :] + at_column(sum_ref[...], hits, cell) + at_edge(edges, hits, cell, ny)
    out_ref[...] = jnp.broadcast_to(lax.rsqrt(value), out_ref.shape).astype(BF16)


def stack_weight_kernel(own_ref, odd_ref, even_ref, basis_in_ref, out_ref, basis_ref):
    at = lax.broadcasted_iota(jnp.int32, out_ref.shape, 0)
    _, has_odd = sides("dec")
    odd = jnp.where(has_odd, odd_ref[...].astype(F32), 0.0)
    out = jnp.where(at == 1, odd, own_ref[...].astype(F32))
    out_ref[...] = jnp.where(at == 2, even_ref[...].astype(F32), out).astype(BF16)


def stack_rows_kernel(a_ref, b_ref, c_ref, after_ref, out_ref):
    n = a_ref.shape[0]
    out_ref[0:n, :] = a_ref[...]
    out_ref[n : 2 * n, :] = b_ref[...]
    out_ref[2 * n :, :] = c_ref[...]


def sincos(theta):
    turns = theta * (0.5 / math.pi)
    magic = 12582912.0
    r = turns - ((turns + magic) - magic)
    z = r * r
    c = jnp.full_like(z, COS[-1])
    for k in COS[-2::-1]:
        c = c * z + k
    s = jnp.full_like(z, SIN[-1])
    for k in SIN[-2::-1]:
        s = s * z + k
    return c, s * r


def basis_kernel(first, tiles, nblk, freq_ref, feat_ref, out_ref, ft_ref):
    feats, nfreq = freq_ref.shape
    blk = out_ref.shape[2]
    ft_ref[...] = freq_ref[...].astype(F32).T.astype(BF16)
    for t in tiles:
        for b in range(nblk):
            c, s = sincos(dot(ft_ref[...], feat_ref[t * feats : (t + 1) * feats, b * blk : (b + 1) * blk], 1, 0))
            out_ref[first + t * nblk + b, 0:nfreq, :] = c.astype(BF16)
            out_ref[first + t * nblk + b, nfreq:, :] = s.astype(BF16)


def own_basis_kernel(nblk, src_ref, count_ref, freq_ref, feat_ref, after_ref, out_ref, code_ref, ft_ref, tile_ref):
    list_slots(nblk, src_ref, count_ref, code_ref, tile_ref)
    basis_kernel(0, (0,), nblk, freq_ref, feat_ref, out_ref, ft_ref)


def pair_sums(code_ref, pip_ref, basis_ref, w_ref, at, a):
    lhs, rhs = [], []
    for k in range(2):
        code = code_ref[at + k]
        lhs.append(basis_ref[lax.rem(lax.div(code, 256), 256)])
        w = w_ref[pl.ds(lax.div(code, 65536), 1), :]
        rhs.append((pip_ref[a, lax.rem(code, 256)].astype(F32) * w).astype(BF16))
    return dot(jnp.concatenate(lhs, 1), jnp.concatenate(rhs, 1), 1, 1)


def spread_weights(w_ref, refs, blk):
    nblk = refs[0][0].shape[1] // blk
    w_ref[9 * nblk :, :] = jnp.zeros((w_ref.shape[0] - 9 * nblk, blk), F32)
    for i, (ref, there) in enumerate(refs):
        for j in range(3):
            for b in range(nblk):
                at = (3 * i + j) * nblk + b
                w = ref[j : j + 1, b * blk : (b + 1) * blk].astype(F32)
                w_ref[at : at + 1, :] = w if there is None else jnp.where(there, w, 0.0)


def early_kernel(code_ref, pip_ref, basis_ref, w_own_ref, w_even_ref, after_ref, sum_ref, w_ref):
    nblk, _, blk, _ = pip_ref.shape
    spread_weights(w_ref, ((w_own_ref, None), (w_even_ref, None)), blk)
    for a in range(nblk):
        total = None
        for p in range(0, FIRST, 2):
            part = pair_sums(code_ref, pip_ref, basis_ref, w_ref, a * FIRST + p, a)
            total = part if total is None else total + part
        sum_ref[a] = total


def pair_kernel(code_ref, pip_ref, basis_ref, early_ref, w_own_ref, w_even_ref, w_odd_ref, out_ref, w_ref, sum_ref, done_ref, sems):
    nblk, slots, blk, _ = pip_ref.shape
    nfreq = out_ref.shape[0]
    half, steps = nblk * FIRST, (slots - FIRST) // 2
    copies = []
    _, has_odd = sides("ra")
    spread_weights(w_ref, ((w_own_ref, None), (w_even_ref, None), (w_odd_ref, has_odd)), blk)
    many = code_ref[half + nblk * slots]

    @pl.when(many > steps)
    def _():
        sum_ref[...] = jnp.zeros_like(sum_ref)

        def step(t, _):
            for a in range(nblk):
                sum_ref[a] += pair_sums(code_ref, pip_ref, basis_ref, w_ref, half + a * slots + 2 * t, a)
            return _

        lax.fori_loop(steps, many, step, 0)

    @pl.when(many <= steps)
    def _():
        sum_ref[...] = jnp.zeros_like(sum_ref)

    for a in range(nblk):
        total = early_ref[a] + sum_ref[a]
        for t in range(steps):
            total = total + pair_sums(code_ref, pip_ref, basis_ref, w_ref, half + a * slots + 2 * t, a)
        own = basis_ref[a].astype(F32)
        folded = own[:nfreq] * total[:nfreq] + own[nfreq:] * total[nfreq:]
        done_ref[a] = (folded * w_ref[a : a + 1, :]).astype(BF16)
        copies.append(pltpu.make_async_copy(done_ref.at[a], out_ref.at[:, a * blk : (a + 1) * blk], sems.at[a]))
        copies[-1].start()
    for copy in copies:
        copy.wait()


def vm(shape, dtype):
    return pltpu.VMEM(shape, dtype)


def sm(shape):
    return pltpu.SMEM(shape, jnp.int32)


def per_device(completeness, stencil, features, frequencies, gal_cell, pip, pair_src, pair_count):
    bands, nx, ny = completeness.shape
    feats, galaxies = features.shape
    nfreq = frequencies.shape[1]
    nblk, slots, blk, _ = pip.shape
    n = bands * nx
    two = 2 * bands

    def call(body, out, args, anys=(), scratch=(), name=None, aliases=None, cost=1, scalars=()):
        return pl.pallas_call(
            body, out_shape=out, in_specs=[SMEM] * len(scalars) + [VMEM] * len(args) + [ANY] * len(anys),
            out_specs=jax.tree.map(lambda x: SMEM if x.memory_space == pltpu.SMEM else VMEM, out),
            scratch_shapes=scratch, compiler_params=params(), input_output_aliases=aliases or {}, name=name,
            cost_estimate=pl.CostEstimate(flops=cost, bytes_accessed=1, transcendentals=0),
        )(*scalars, *args, *anys)

    cells = gal_cell.reshape(1, galaxies)
    given = (completeness, features, frequencies, stencil, cells, pair_src, pair_count)
    kept = tuple(vm(x.shape, x.dtype) for x in given[1:5]) + tuple(sm(x.shape) for x in given[5:])
    rim, rows, features, frequencies, stencil, cells, pair_src, pair_count = pl.pallas_call(
        rim_kernel, out_shape=(vm((RIM, n), BF16), vm((n, ny), F32)) + kept,
        in_specs=[HBM] * len(given), out_specs=(VMEM,) * 6 + (SMEM,) * 2, compiler_params=params(), name="rim",
        scratch_shapes=[pltpu.VMEM(completeness.shape, F32), pltpu.SemaphoreType.DMA((len(given),))],
    )(*[pltpu.with_memory_space_constraint(x, pltpu.HBM) for x in given])
    d_odd, d_even = exchange("dec", rim, rim)
    f_odd, f_even = exchange("dec", features, features)
    taps, lane_taps, hit = call(
        functools.partial(ready_kernel, bands, nx, ny),
        (vm((stencil.shape[0] * bands, ny), F32), vm((5 * RIM, n), F32), vm((n, galaxies), BF16)),
        (stencil, cells), (rim,), [pltpu.VMEM((32, 128), F32)], "ready",
    )
    inner = call(
        functools.partial(inner_kernel, bands), vm((n, ny), F32), (rows, taps), (), [pltpu.VMEM((5, n, ny), F32)], "inner",
    )
    to_odd, to_even = call(
        row_kernel, (vm((two + 2 * RIM, ny), BF16),) * 2, (rows, d_odd, d_even), (inner,), name="rows", cost=LONG
    )
    r_odd, r_even = exchange("ra", to_odd, to_even)
    even_side = call(
        functools.partial(even_side_kernel, bands), vm((8, galaxies), F32),
        (inner, d_odd, d_even, r_even, taps, lane_taps, hit, cells), (),
        [pltpu.VMEM((5, two, ny), F32), pltpu.VMEM((n, ny), F32)], "even_side",
    )
    column = call(stack_rows_kernel, vm((3 * feats, galaxies), BF16), (features, f_odd, f_even), (even_side,), name="stack_features")
    c_odd, c_even = exchange("ra", column, column)

    blocks = vm((9 * nblk, 2 * nfreq, blk), BF16)
    scratch = [pltpu.VMEM((nfreq, feats), BF16)]
    table, code = call(
        functools.partial(own_basis_kernel, nblk), (blocks, sm((nblk * (FIRST + slots) + 2,))), (frequencies, features), (column,),
        scratch + [pltpu.SMEM((9,), jnp.int32)], "own_basis", scalars=(pair_src, pair_count),
    )

    def basis(part, tiles, array, buffer, after):
        def body(freq_ref, feat_ref, *refs):
            basis_kernel(3 * part * nblk, tiles, nblk, freq_ref, feat_ref, *refs[-2:])

        return call(body, blocks, (frequencies, array), (after, buffer), scratch, "basis%d" % part, {3: 0})

    weight, table = call(
        functools.partial(weight_kernel, bands), (vm((RIM, galaxies), BF16), blocks),
        (even_side, r_odd, taps, lane_taps, hit, cells), (table,),
        [pltpu.VMEM((5, two, ny), F32), pltpu.VMEM((two, ny), F32)], "weight", {6: 1}, LONG,
    )
    w_odd, w_even = exchange("dec", weight, weight)
    table = basis(0, (1, 2), column, table, weight)
    table = basis(1, (0, 1, 2), c_even, table, weight)
    w_column, table = call(
        stack_weight_kernel, (vm((RIM, galaxies), BF16), vm(table.shape, BF16)), (weight, w_odd, w_even), (table,), name="stack_weights",
        aliases={3: 1},
    )
    x_odd, x_even = exchange("ra", w_column, w_column)
    early = call(
        early_kernel, vm((nblk, 2 * nfreq, blk), F32), (pip, table, w_column, x_even), (w_column,),
        [pltpu.VMEM((9 * nblk + 4, blk), F32)], "early_pairs", scalars=(code,),
    )
    table = basis(2, (0, 1, 2), c_odd, table, early)
    return pl.pallas_call(
        pair_kernel, out_shape=jax.ShapeDtypeStruct((nfreq, galaxies), BF16), in_specs=[SMEM] + [VMEM] * 6, out_specs=ANY,
        scratch_shapes=[
            pltpu.VMEM((9 * nblk + 4, blk), F32), pltpu.VMEM((nblk, 2 * nfreq, blk), F32),
            pltpu.VMEM((nblk, nfreq, blk), BF16), pltpu.SemaphoreType.DMA((nblk,)),
        ],
        compiler_params=params(), name="pairs",
    )(code, pip, table, early, w_column, x_even, x_odd)


def solution(mesh):
    in_specs = (
        P(None, "ra", "dec"),
        P(),
        P(None, ("ra", "dec")),
        P(),
        P(("ra", "dec")),
        P(("ra", "dec"), None, None, None),
        P(("ra", "dec"), None),
        P(("ra", "dec")),
    )
    out_specs = P(None, ("ra", "dec"))
    return jax.shard_map(per_device, mesh=mesh, in_specs=in_specs, out_specs=out_specs, check_vma=False)
```

time: 26.1 us -> 24.5 us (0.939)
  waiting for transfers between devices: 0.89 us -> 0.03 us
  starting transfers between devices: 13 us -> 12.3 us
    pallas_call x10 -> x12, Pallas kernels: 7.11 us -> 8.43 us  [call(): pl.pallas_call(body, out_shape=out, in_specs=[SMEM] * len(scalars) + [VME...]
    pallas_call x1, Pallas kernels: 3.14 us -> 1.84 us  [per_device(): pl.pallas_call(pair_kernel, out_shape=jax.ShapeDtypeStruct((nfreq, galaxi...]
    ppermute x12, waiting for transfers between devices: 0.89 us -> 0.03 us  [swap(): lax.ppermute(payload, ('ra', 'dec'), sorted(pairs + [(b, a) for a, b in p...]
    ppermute x12, starting transfers between devices: 13 us -> 12.3 us  [swap(): lax.ppermute(payload, ('ra', 'dec'), sorted(pairs + [(b, a) for a, b in p...]
  transfers between devices with their start and end apart: 12 -> 12, of which waited for: 2 -> 0; matrix products, arithmetic and copies ran while one was open for 0% -> 0% of each run, Pallas kernels for 28% -> 35%
where the time goes in v3:
time: 24.5 us; the launch traced here: 24.1 us
  starting transfers between devices  12.3 us (50%)
  Pallas kernels  11.6 us (47%)
    ppermute x12, starting transfers between devices, swap(): lax.ppermute(payload, ('ra', 'dec'), sorted(pairs + [(b, a) for a, b in p...  12.3 us
    pallas_call x12, Pallas kernels, call(): pl.pallas_call(body, out_shape=out, in_specs=[SMEM] * len(scalars) + [VME...  8.43 us
    pallas_call x1, Pallas kernels, per_device(): pl.pallas_call(pair_kernel, out_shape=jax.ShapeDtypeStruct((nfreq, galaxi...  1.84 us
    pallas_call x1, Pallas kernels, per_device(): pl.pallas_call(rim_kernel, out_shape=(vm((RIM, n), BF16), vm((n, ny), F32...  1.3 us
  transfers between devices with their start and end apart: 12, of which 0 were waited for; matrix products, arithmetic and copies ran while one was open for 0% of the time, Pallas kernels for 35%

profile of v3, /device:TPU:1, one launch (start us, length us, event | category | flops | bytes accessed | tf_op | source)
XLA Modules:
  0.0 24.1 jit_solution(11796681449801425264)
XLA Ops:
  0.0 1.3 %rim.1 = (bf16[16,512]{1,0:T(8,128)(2,1)S(1)}, f32[512,128]{1,0:T(8,128)S(1)}, bf16[96,512]{1,0:T(8,128)(2,1)S(1)}, bf16[96,256]{1,0:T(8,128)(2,1)S(1)}, f32[25,...) custom-call(f32[64,8,128]{2,1,0:T(8,128)} %refs_0_.1, bf16[96,512]{1,0:T(8,128)(2,1)} %refs_1_.1, ...), custom_call_target="tpu_custom_call" | custom-call | tf_op jit(solution)/shard_map/rim/pallas_call | solution.py:420
  1.3 0.1 collective-permute-start.2
  1.4 3.4 %collective-permute-start.3 = (bf16[16,512]{1,0:T(8,128)(2,1)S(1)}, bf16[16,512]{1,0:T(8,128)(2,1)S(1)}, u32[]{:S(2)}, u32[]{:S(2)}) collective-permute-start(bf16[16,512]{1,0:T(8,128)(2,1)S(1)} %get-tuple-element.31.rim_ref), channel_id=1, source_target_pairs={{0,1},{1,0},{2,3},{3,2},{4,5},{5,4},{6,7},{7,6},{8,9},{9,8},{10,11... | collective-permute-start | bytes 49160 | tf_op jit(solution)/shard_map/ppermute | solution.py:41
  4.8 1.2 %collective-permute-start = (bf16[96,512]{1,0:T(8,128)(2,1)S(1)}, bf16[96,512]{1,0:T(8,128)(2,1)S(1)}, u32[]{:S(2)}, u32[]{:S(2)}) collective-permute-start(bf16[96,512]{1,0:T(8,128)(2,1)S(1)} %get-tuple-element.27.a_ref.feat_ref), channel_id=1, source_target_pairs={{0,4},{1,2},{2,1},{3,7},{4,0},{5,6},{6,5},{7,3},{8,12},{9,10},{10,... | collective-permute-start | bytes 294920 | tf_op jit(solution)/shard_map/ppermute | solution.py:41
  6.0 0.8 %collective-permute-start.1 = (bf16[96,512]{1,0:T(8,128)(2,1)S(1)}, bf16[96,512]{1,0:T(8,128)(2,1)S(1)}, u32[]{:S(2)}, u32[]{:S(2)}) collective-permute-start(bf16[96,512]{1,0:T(8,128)(2,1)S(1)} %get-tuple-element.27.a_ref.feat_ref), channel_id=1, source_target_pairs={{0,1},{1,0},{2,3},{3,2},{4,5},{5,4},{6,7},{7,6},{8,9},{9,8},{10,11... | collective-permute-start | bytes 294920 | tf_op jit(solution)/shard_map/ppermute | solution.py:41
  6.8 0.6 %ready.1 = (f32[1600,128]{1,0:T(8,128)S(1)}, f32[80,512]{1,0:T(8,128)S(1)}, bf16[512,512]{1,0:T(8,128)(2,1)S(1)}) custom-call(f32[25,64]{1,0:T(8,128)S(1)} %get-tuple-element.29.stencil_ref, s32[1,512]{1,0:T(1,128)S(1)} %get-tuple-element.30.cell_ref, bf16[16,512]{1,0:T(8,128)(2,1)S(1)} %get-tuple-element.31.rim_ref), custom_call_target="tpu_custom_call" | custom-call | flops 1 | bytes 1 | tf_op jit(solution)/shard_map/ready/pallas_call | solution.py:410
  7.4 0.8 %inner.1.after_ref.inner_ref = f32[512,128]{1,0:T(8,128)S(1)} custom-call(f32[512,128]{1,0:T(8,128)S(1)} %get-tuple-element.28.rows_ref, f32[1600,128]{1,0:T(8,128)S(1)} %get-tuple-element.32.taps_ref), custom_call_target="tpu_custom_call" | custom-call | flops 1 | bytes 1 | tf_op jit(solution)/shard_map/inner/pallas_call | solution.py:410
  8.2 0.0 collective-permute-done.2.odd_ref
  8.2 0.0 collective-permute-done.3.even_ref
  8.3 1.0 %collective-permute-start.4 = (bf16[160,128]{1,0:T(8,128)(2,1)S(1)}, bf16[160,128]{1,0:T(8,128)(2,1)S(1)}, u32[]{:S(2)}, u32[]{:S(2)}) collective-permute-start(bf16[160,128]{1,0:T(8,128)(2,1)S(1)} %get-tuple-element.33), channel_id=1, source_target_pairs={{0,4},{1,5},{2,6},{3,7},{4,0},{5,1},{6,2},{7,3},{8,12},{9,13},{10,... | collective-permute-start | bytes 122888 | tf_op jit(solution)/shard_map/ppermute | solution.py:41
  9.2 1.2 %collective-permute-start.6 = (bf16[160,128]{1,0:T(8,128)(2,1)S(1)}, bf16[160,128]{1,0:T(8,128)(2,1)S(1)}, u32[]{:S(2)}, u32[]{:S(2)}) collective-permute-start(bf16[160,128]{1,0:T(8,128)(2,1)S(1)} %get-tuple-element.37), channel_id=1, source_target_pairs={{0,1},{1,0},{2,3},{3,2},{4,8},{5,9},{6,10},{7,11},{8,4},{9,5},{10,... | collective-permute-start | bytes 122888 | tf_op jit(solution)/shard_map/ppermute | solution.py:41
  10.4 0.0 collective-permute-done.4.rows_ref
  10.4 0.6 %even_side.1.after_ref.even_side_ref = f32[8,512]{1,0:T(8,128)S(1)} custom-call(f32[512,128]{1,0:T(8,128)S(1)} %inner.1.after_ref.inner_ref, bf16[16,512]{1,0:T(8,128)(2,1)S(1)} %collective-permute-done.2.odd_ref, bf16[16,512]{1,0:T(8,128)(2,1)S(1)} %collective-permute-done.3.even_ref, bf16[160,128]{1,0:T(8,128)(2,1)S(1)} %collective-permute-done.4.rows_ref, ...), custom_call_target="tpu_custom_call" | custom-call | flops 1 | bytes 1 | tf_op jit(solution)/shard_map/even_side/pallas_call | solution.py:410
  11.0 0.0 collective-permute-done.b_ref
  11.0 0.0 collective-permute-done.1.c_ref
  11.0 0.3 %collective-permute-start.9 = (bf16[288,512]{1,0:T(8,128)(2,1)S(1)}, bf16[288,512]{1,0:T(8,128)(2,1)S(1)}, u32[]{:S(2)}, u32[]{:S(2)}) collective-permute-start(bf16[288,512]{1,0:T(8,128)(2,1)S(1)} %stack_features.1.after_ref.feat_ref), channel_id=1, source_target_pairs={{0,4},{1,5},{2,6},{3,7},{4,0},{5,1},{6,2},{7,3},{8,12},{9,13},{10,... | collective-permute-start | bytes 884744 | tf_op jit(solution)/shard_map/ppermute | solution.py:41
  11.3 1.4 %collective-permute-start.5 = (bf16[288,512]{1,0:T(8,128)(2,1)S(1)}, bf16[288,512]{1,0:T(8,128)(2,1)S(1)}, u32[]{:S(2)}, u32[]{:S(2)}) collective-permute-start(bf16[288,512]{1,0:T(8,128)(2,1)S(1)} %stack_features.1.after_ref.feat_ref), channel_id=1, source_target_pairs={{0,1},{1,0},{2,3},{3,2},{4,8},{5,9},{6,10},{7,11},{8,4},{9,5},{10,... | collective-permute-start | bytes 884744 | tf_op jit(solution)/shard_map/ppermute | solution.py:41
  12.7 0.7 %own_basis.1 = (bf16[36,512,128]{2,1,0:T(8,128)(2,1)S(1)}, s32[74]{0:T(128)S(4)}) custom-call(s32[4,12]{1,0:T(4,128)S(4)} %get-tuple-element.24.src_ref, s32[4]{0:T(128)S(4)} %get-tuple-element.25.count_ref, bf16[96,256]{1,0:T(8,128)(2,1)S(1)} %get-tuple-element.26.freq_ref, bf16[96,512]{1,0:T(8,128)(2,1)S(1)} %get-tuple-element.27.a_ref.feat_ref, ...), custom_call_target="tpu_custom_call" | custom-call | flops 1 | bytes 1 | tf_op jit(solution)/shard_map/own_basis/pallas_call | solution.py:410
  13.4 0.0 collective-permute-done.6.rows_ref
  13.4 0.5 %weight.1 = (bf16[16,512]{1,0:T(8,128)(2,1)S(1)}, bf16[36,512,128]{2,1,0:T(8,128)(2,1)S(1)}) custom-call(f32[8,512]{1,0:T(8,128)S(1)} %even_side.1.after_ref.even_side_ref, bf16[160,128]{1,0:T(8,128)(2,1)S(1)} %collective-permute-done.6.rows_ref, f32[1600,128]{1,0:T(8,128)S(1)} %get-tuple-element.32.taps_ref, ...), custom_call_target="tpu_custom_call", output_to_operand_aliasing={{1}: (6, {})} | custom-call | flops 68719476736 | bytes 1 | tf_op jit(solution)/shard_map/weight/pallas_call | solution.py:410
  13.9 0.1 collective-permute-start.7
  14.0 0.7 %collective-permute-start.8 = (bf16[16,512]{1,0:T(8,128)(2,1)S(1)}, bf16[16,512]{1,0:T(8,128)(2,1)S(1)}, u32[]{:S(2)}, u32[]{:S(2)}) collective-permute-start(bf16[16,512]{1,0:T(8,128)(2,1)S(1)} %get-tuple-element.39.refs_0_.own_ref), channel_id=1, source_target_pairs={{0,1},{1,0},{2,3},{3,2},{4,5},{5,4},{6,7},{7,6},{8,9},{9,8},{10,11... | collective-permute-start | bytes 49160 | tf_op jit(solution)/shard_map/ppermute | solution.py:41
  14.7 1.1 %basis0.1.refs_1_ = bf16[36,512,128]{2,1,0:T(8,128)(2,1)S(1)} custom-call(bf16[96,256]{1,0:T(8,128)(2,1)S(1)} %get-tuple-element.26.freq_ref, bf16[288,512]{1,0:T(8,128)(2,1)S(1)} %stack_features.1.after_ref.feat_ref, bf16[16,512]{1,0:T(8,128)(2,1)S(1)} %get-tuple-element.39.refs_0_.own_ref, ...), custom_call_target="tpu_custom_call", output_to_operand_aliasing={{}: (3, {})} | custom-call | flops 1 | bytes 1 | tf_op jit(solution)/shard_map/basis0/pallas_call | solution.py:410
  15.8 0.0 collective-permute-done.9.feat_ref
  15.8 1.5 %basis1.1.basis_in_ref = bf16[36,512,128]{2,1,0:T(8,128)(2,1)S(1)} custom-call(bf16[96,256]{1,0:T(8,128)(2,1)S(1)} %get-tuple-element.26.freq_ref, bf16[288,512]{1,0:T(8,128)(2,1)S(1)} %collective-permute-done.9.feat_ref, bf16[16,512]{1,0:T(8,128)(2,1)S(1)} %get-tuple-element.39.refs_0_.own_ref, ...), custom_call_target="tpu_custom_call", output_to_operand_aliasing={{}: (3, {})} | custom-call | flops 1 | bytes 1 | tf_op jit(solution)/shard_map/basis1/pallas_call | solution.py:410
  17.3 0.0 copy-start
  17.3 0.0 collective-permute-done.7.odd_ref
  17.3 0.0 collective-permute-done.8.even_ref
  17.4 1.4 %collective-permute-start.10 = (bf16[16,512]{1,0:T(8,128)(2,1)S(1)}, bf16[16,512]{1,0:T(8,128)(2,1)S(1)}, u32[]{:S(2)}, u32[]{:S(2)}) collective-permute-start(bf16[16,512]{1,0:T(8,128)(2,1)S(1)} %get-tuple-element.42.w_own_ref.after_ref), channel_id=1, source_target_pairs={{0,4},{1,5},{2,6},{3,7},{4,0},{5,1},{6,2},{7,3},{8,12},{9,13},{10,... | collective-permute-start | bytes 49160 | tf_op jit(solution)/shard_map/ppermute | solution.py:41
  18.8 0.9 %collective-permute-start.11 = (bf16[16,512]{1,0:T(8,128)(2,1)S(1)}, bf16[16,512]{1,0:T(8,128)(2,1)S(1)}, u32[]{:S(2)}, u32[]{:S(2)}) collective-permute-start(bf16[16,512]{1,0:T(8,128)(2,1)S(1)} %get-tuple-element.42.w_own_ref.after_ref), channel_id=1, source_target_pairs={{0,1},{1,0},{2,3},{3,2},{4,8},{5,9},{6,10},{7,11},{8,4},{9,5},{10,... | collective-permute-start | bytes 49160 | tf_op jit(solution)/shard_map/ppermute | solution.py:41
  19.6 0.0 collective-permute-done.10.w_even_ref
  19.6 0.0 copy-done
  19.7 1.0 %early_pairs.1.refs_0_.early_ref = f32[4,512,128]{2,1,0:T(8,128)S(1)} custom-call(s32[74]{0:T(128)S(4)} %get-tuple-element.36.code_ref, bf16[4,12,128,128]{3,2,1,0:T(8,128)(2,1)S(1)} %copy-done, bf16[36,512,128]{2,1,0:T(8,128)(2,1)S(1)} %get-tuple-element.41.basis_ref.refs_1_, bf16[16,512]{1,0:T(8,128)(2,1)S(1)} %get-tuple-element.42.w_own_ref.after_ref, ...), custom_call_target="tpu_custom_call" | custom-call | flops 1 | bytes 1 | tf_op jit(solution)/shard_map/early_pairs/pallas_call | solution.py:410
  20.7 0.0 collective-permute-done.5.feat_ref
  20.7 1.5 %basis2.1.basis_ref = bf16[36,512,128]{2,1,0:T(8,128)(2,1)S(1)} custom-call(bf16[96,256]{1,0:T(8,128)(2,1)S(1)} %get-tuple-element.26.freq_ref, bf16[288,512]{1,0:T(8,128)(2,1)S(1)} %collective-permute-done.5.feat_ref, f32[4,512,128]{2,1,0:T(8,128)S(1)} %early_pairs.1.refs_0_.early_ref, ...), custom_call_target="tpu_custom_call", output_to_operand_aliasing={{}: (3, {})} | custom-call | flops 1 | bytes 1 | tf_op jit(solution)/shard_map/basis2/pallas_call | solution.py:410
  22.2 0.0 collective-permute-done.11.w_odd_ref
  22.2 1.8 %pairs.1 = bf16[256,512]{1,0:T(8,128)(2,1)} custom-call(s32[74]{0:T(128)S(4)} %get-tuple-element.36.code_ref, bf16[4,12,128,128]{3,2,1,0:T(8,128)(2,1)S(1)} %copy-done, bf16[36,512,128]{2,1,0:T(8,128)(2,1)S(1)} %basis2.1.basis_ref, f32[4,512,128]{2,1,0:T(8,128)S(1)} %early_pairs.1.refs_0_.early_ref, ...), custom_call_target="tpu_custom_call" | custom-call | tf_op jit(solution)/shard_map/pairs/pallas_call | solution.py:478
  (3 shorter events, 0.1 us)
Async XLA Ops:
  1.3 6.9 %collective-permute-start.2 = (bf16[16,512]{1,0:T(8,128)(2,1)S(1)}, bf16[16,512]{1,0:T(8,128)(2,1)S(1)}, u32[]{:S(2)}, u32[]{:S(2)}) collective-permute-start(bf16[16,512]{1,0:T(8,128)(2,1)S(1)} %get-tuple-element.31.rim_ref), channel_id=1, source_target_pairs={{0,4},{1,2},{2,1},{3,7},{4,0},{5,6},{6,5},{7,3},{8,12},{9,10},{10,... | collective-permute-start | bytes 49160 | tf_op jit(solution)/shard_map/ppermute | solution.py:41
  1.4 6.8 %collective-permute-start.3 = (bf16[16,512]{1,0:T(8,128)(2,1)S(1)}, bf16[16,512]{1,0:T(8,128)(2,1)S(1)}, u32[]{:S(2)}, u32[]{:S(2)}) collective-permute-start(bf16[16,512]{1,0:T(8,128)(2,1)S(1)} %get-tuple-element.31.rim_ref), channel_id=1, source_target_pairs={{0,1},{1,0},{2,3},{3,2},{4,5},{5,4},{6,7},{7,6},{8,9},{9,8},{10,11... | collective-permute-start | bytes 49160 | tf_op jit(solution)/shard_map/ppermute | solution.py:41
  4.8 6.2 %collective-permute-start = (bf16[96,512]{1,0:T(8,128)(2,1)S(1)}, bf16[96,512]{1,0:T(8,128)(2,1)S(1)}, u32[]{:S(2)}, u32[]{:S(2)}) collective-permute-start(bf16[96,512]{1,0:T(8,128)(2,1)S(1)} %get-tuple-element.27.a_ref.feat_ref), channel_id=1, source_target_pairs={{0,4},{1,2},{2,1},{3,7},{4,0},{5,6},{6,5},{7,3},{8,12},{9,10},{10,... | collective-permute-start | bytes 294920 | tf_op jit(solution)/shard_map/ppermute | solution.py:41
  6.0 5.0 %collective-permute-start.1 = (bf16[96,512]{1,0:T(8,128)(2,1)S(1)}, bf16[96,512]{1,0:T(8,128)(2,1)S(1)}, u32[]{:S(2)}, u32[]{:S(2)}) collective-permute-start(bf16[96,512]{1,0:T(8,128)(2,1)S(1)} %get-tuple-element.27.a_ref.feat_ref), channel_id=1, source_target_pairs={{0,1},{1,0},{2,3},{3,2},{4,5},{5,4},{6,7},{7,6},{8,9},{9,8},{10,11... | collective-permute-start | bytes 294920 | tf_op jit(solution)/shard_map/ppermute | solution.py:41
  8.3 2.1 %collective-permute-start.4 = (bf16[160,128]{1,0:T(8,128)(2,1)S(1)}, bf16[160,128]{1,0:T(8,128)(2,1)S(1)}, u32[]{:S(2)}, u32[]{:S(2)}) collective-permute-start(bf16[160,128]{1,0:T(8,128)(2,1)S(1)} %get-tuple-element.33), channel_id=1, source_target_pairs={{0,4},{1,5},{2,6},{3,7},{4,0},{5,1},{6,2},{7,3},{8,12},{9,13},{10,... | collective-permute-start | bytes 122888 | tf_op jit(solution)/shard_map/ppermute | solution.py:41
  9.2 4.2 %collective-permute-start.6 = (bf16[160,128]{1,0:T(8,128)(2,1)S(1)}, bf16[160,128]{1,0:T(8,128)(2,1)S(1)}, u32[]{:S(2)}, u32[]{:S(2)}) collective-permute-start(bf16[160,128]{1,0:T(8,128)(2,1)S(1)} %get-tuple-element.37), channel_id=1, source_target_pairs={{0,1},{1,0},{2,3},{3,2},{4,8},{5,9},{6,10},{7,11},{8,4},{9,5},{10,... | collective-permute-start | bytes 122888 | tf_op jit(solution)/shard_map/ppermute | solution.py:41
  11.0 4.7 %collective-permute-start.9 = (bf16[288,512]{1,0:T(8,128)(2,1)S(1)}, bf16[288,512]{1,0:T(8,128)(2,1)S(1)}, u32[]{:S(2)}, u32[]{:S(2)}) collective-permute-start(bf16[288,512]{1,0:T(8,128)(2,1)S(1)} %stack_features.1.after_ref.feat_ref), channel_id=1, source_target_pairs={{0,4},{1,5},{2,6},{3,7},{4,0},{5,1},{6,2},{7,3},{8,12},{9,13},{10,... | collective-permute-start | bytes 884744 | tf_op jit(solution)/shard_map/ppermute | solution.py:41
  11.3 9.3 %collective-permute-start.5 = (bf16[288,512]{1,0:T(8,128)(2,1)S(1)}, bf16[288,512]{1,0:T(8,128)(2,1)S(1)}, u32[]{:S(2)}, u32[]{:S(2)}) collective-permute-start(bf16[288,512]{1,0:T(8,128)(2,1)S(1)} %stack_features.1.after_ref.feat_ref), channel_id=1, source_target_pairs={{0,1},{1,0},{2,3},{3,2},{4,8},{5,9},{6,10},{7,11},{8,4},{9,5},{10,... | collective-permute-start | bytes 884744 | tf_op jit(solution)/shard_map/ppermute | solution.py:41
  13.9 3.4 %collective-permute-start.7 = (bf16[16,512]{1,0:T(8,128)(2,1)S(1)}, bf16[16,512]{1,0:T(8,128)(2,1)S(1)}, u32[]{:S(2)}, u32[]{:S(2)}) collective-permute-start(bf16[16,512]{1,0:T(8,128)(2,1)S(1)} %get-tuple-element.39.refs_0_.own_ref), channel_id=1, source_target_pairs={{0,4},{1,2},{2,1},{3,7},{4,0},{5,6},{6,5},{7,3},{8,12},{9,10},{10,... | collective-permute-start | bytes 49160 | tf_op jit(solution)/shard_map/ppermute | solution.py:41
  14.0 3.3 %collective-permute-start.8 = (bf16[16,512]{1,0:T(8,128)(2,1)S(1)}, bf16[16,512]{1,0:T(8,128)(2,1)S(1)}, u32[]{:S(2)}, u32[]{:S(2)}) collective-permute-start(bf16[16,512]{1,0:T(8,128)(2,1)S(1)} %get-tuple-element.39.refs_0_.own_ref), channel_id=1, source_target_pairs={{0,1},{1,0},{2,3},{3,2},{4,5},{5,4},{6,7},{7,6},{8,9},{9,8},{10,11... | collective-permute-start | bytes 49160 | tf_op jit(solution)/shard_map/ppermute | solution.py:41
  17.3 2.3 %copy-start = (bf16[4,12,128,128]{3,2,1,0:T(8,128)(2,1)S(1)}, bf16[4,12,128,128]{3,2,1,0:T(8,128)(2,1)}, u32[]{:S(2)}) copy-start(bf16[4,12,128,128]{3,2,1,0:T(8,128)(2,1)} %pip_ref.3) | copy-start | bytes 4718596
  17.4 2.3 %collective-permute-start.10 = (bf16[16,512]{1,0:T(8,128)(2,1)S(1)}, bf16[16,512]{1,0:T(8,128)(2,1)S(1)}, u32[]{:S(2)}, u32[]{:S(2)}) collective-permute-start(bf16[16,512]{1,0:T(8,128)(2,1)S(1)} %get-tuple-element.42.w_own_ref.after_ref), channel_id=1, source_target_pairs={{0,4},{1,5},{2,6},{3,7},{4,0},{5,1},{6,2},{7,3},{8,12},{9,13},{10,... | collective-permute-start | bytes 49160 | tf_op jit(solution)/shard_map/ppermute | solution.py:41
  18.8 3.5 %collective-permute-start.11 = (bf16[16,512]{1,0:T(8,128)(2,1)S(1)}, bf16[16,512]{1,0:T(8,128)(2,1)S(1)}, u32[]{:S(2)}, u32[]{:S(2)}) collective-permute-start(bf16[16,512]{1,0:T(8,128)(2,1)S(1)} %get-tuple-element.42.w_own_ref.after_ref), channel_id=1, source_target_pairs={{0,1},{1,0},{2,3},{3,2},{4,8},{5,9},{6,10},{7,11},{8,4},{9,5},{10,... | collective-permute-start | bytes 49160 | tf_op jit(solution)/shard_map/ppermute | solution.py:41

commit v4 on v3

--- a/solution.py
+++ b/solution.py
@@ -65,13 +65,14 @@
     copies = [pltpu.make_async_copy(a, b, sems.at[i]) for i, (a, b) in enumerate(zip(given, (comp_ref, *kept), strict=True))]
     for copy in copies:
         copy.start()
-    row = lax.broadcasted_iota(jnp.int32, (RIM, ny), 0)
-    lane = lax.broadcasted_iota(jnp.int32, (RIM, ny), 1)
+    row = lax.broadcasted_iota(jnp.int32, (8, ny), 0)
+    lane = lax.broadcasted_iota(jnp.int32, (8, ny), 1)
     pick = ((row < 2) & (lane == row)) | ((row >= 2) & (row < 4) & (lane == row + ny - 4))
     copies[0].wait()
     for x in range(nx):
         rows_ref[x * bands : (x + 1) * bands, :] = comp_ref[:, x, :]
-    rim_ref[...] = dot(pick.astype(F32).astype(BF16), rows_ref[...].astype(BF16), 1, 1).astype(BF16)
+    rim = dot(pick.astype(F32).astype(BF16), rows_ref[...].astype(BF16), 1, 1)
+    rim_ref[...] = jnp.concatenate([rim[0:4, at : at + 128] for at in range(0, bands * nx, 128)], 0).astype(BF16)
     for copy in copies[1:]:
         copy.wait()
 
@@ -82,9 +83,11 @@
     ra_odd, _ = sides("ra")
     dec_odd, _ = sides("dec")
     ra_up, dec_up = jnp.where(ra_odd, 2, 1), jnp.where(dec_odd, 1, 2)
-    for i, ra_at in enumerate((3 - ra_up, 0, ra_up)):
-        for j, dec_at in enumerate((3 - dec_up, 0, dec_up)):
-            tile_ref[3 * i + j] = (3 * ra_at + dec_at) * nblk
+    ra, dec = lax.axis_index("ra"), lax.axis_index("dec")
+    last_ra, last_dec = lax.axis_size("ra") - 1, lax.axis_size("dec") - 1
+    for i, (ra_at, ra_in) in enumerate(((3 - ra_up, ra > 0), (0, ra >= 0), (ra_up, ra < last_ra))):
+        for j, (dec_at, dec_in) in enumerate(((3 - dec_up, dec > 0), (0, dec >= 0), (dec_up, dec < last_dec))):
+            tile_ref[3 * i + j] = jnp.where(jnp.logical_and(ra_in, dec_in), (3 * ra_at + dec_at) * nblk, -blocks)
     for i in range(half + own * slots):
         code_ref[i] = blocks * 65536
     steps = jnp.int32(0)
@@ -93,7 +96,7 @@
         for p in range(slots):
             s = src_ref[a, p]
             at = tile_ref[lax.div(s, nblk)] + lax.rem(s, nblk)
-            live = p < count_ref[a]
+            live = jnp.logical_and(p < count_ref[a], at >= 0)
             soon = jnp.logical_and(at < 6 * nblk, early < FIRST)
             to = jnp.where(soon, a * FIRST + early, half + a * slots + late)
             code_ref[jnp.where(live, to, half + own * slots + 1)] = p + at * (256 + 65536)
@@ -103,7 +106,21 @@
     code_ref[half + own * slots] = steps
 
 
-def ready_kernel(bands, nx, ny, stencil_ref, cell_ref, rim_ref, taps_ref, lane_taps_ref, hit_ref, st_ref):
+def leads():
+    return jnp.logical_and(lax.axis_index("ra") < 2, lax.axis_index("dec") == 0)
+
+
+def ahead_kernel(bands, nx, ny, rim_in_ref, stencil_ref, cell_ref, rim_ref, taps_ref, lane_taps_ref, hit_ref, st_ref):
+    rim_ref[...] = rim_in_ref[...]
+    pl.when(leads())(lambda: ready(bands, nx, ny, stencil_ref, cell_ref, taps_ref, lane_taps_ref, hit_ref, st_ref))
+
+
+def ready_kernel(bands, nx, ny, stencil_ref, cell_ref, rim_ref, taps_in_ref, lane_taps_in_ref, hit_in_ref, taps_ref, lane_taps_ref, hit_ref, st_ref):
+    late = jnp.logical_not(leads())
+    pl.when(late)(lambda: ready(bands, nx, ny, stencil_ref, cell_ref, taps_ref, lane_taps_ref, hit_ref, st_ref))
+
+
+def ready(bands, nx, ny, stencil_ref, cell_ref, taps_ref, lane_taps_ref, hit_ref, st_ref):
     st_ref[...] = jnp.zeros_like(st_ref)
     count = stencil_ref.shape[0]
     st_ref[0:count, 0:bands] = stencil_ref[...]
@@ -124,13 +141,14 @@
 
 def row_kernel(rows_ref, odd_ref, even_ref, after_ref, to_odd_ref, to_even_ref):
     n = rows_ref.shape[0]
-    two = to_odd_ref.shape[0] - 2 * RIM
+    two = to_odd_ref.shape[0] - RIM
     is_odd, _ = sides("ra")
 
     def put(ref, start):
         ref[0:two, :] = rows_ref[start : start + two, :].astype(BF16)
-        ref[two : two + RIM, :] = odd_ref[:, start : start + two]
-        ref[two + RIM :, :] = even_ref[:, start : start + two]
+        at = start // 128 * 4
+        edges = [r[...].astype(F32)[at : at + 4] for r in (odd_ref, even_ref)]
+        ref[two:, :] = jnp.concatenate([*edges, jnp.zeros((RIM - 8, 128), F32)], 0).astype(BF16)
 
     @pl.when(is_odd)
     def _():
@@ -143,17 +161,16 @@
         put(to_even_ref, n - two)
 
 
-def picks():
+def beside(odd, even):
     dec_odd, has_odd = sides("dec")
-    row = lax.broadcasted_iota(jnp.int32, (RIM, RIM), 0)
-    lane = lax.broadcasted_iota(jnp.int32, (RIM, RIM), 1)
-
-    def ones(*spots):
-        return functools.reduce(jnp.logical_or, [(row == r) & (lane == k) for r, k in spots]).astype(F32)
-
-    before, after = ones((0, 2), (1, 3), (8, 3)), ones((2, 0), (3, 0), (11, 1))
-    odd = jnp.where(has_odd, jnp.where(dec_odd, after, before), 0.0)
-    return odd.astype(BF16), jnp.where(dec_odd, before, after).astype(BF16)
+    odd = jnp.where(has_odd, odd, 0.0)
+    before, after = jnp.where(dec_odd, even, odd), jnp.where(dec_odd, odd, even)
+    none = jnp.zeros_like(before)
+    return jnp.concatenate([before[2:4], after[0:1], after[0:1], none, before[3:4], none[0:2], after[1:2], none], 0)
+
+
+def columns_of(rim):
+    return jnp.concatenate([rim[at : at + 4] for at in range(0, RIM, 4)], 1)
 
 
 def edge_sums(lane_taps_ref, bands, columns):
@@ -242,10 +259,10 @@
     pl.when(ra_odd)(lambda: side_sums(ext_ref, taps_ref, bands, False, add_from(0)))
     pl.when(jnp.logical_not(ra_odd))(lambda: side_sums(ext_ref, taps_ref, bands, True, add_from(n - two)))
 
-    odd, even = picks()
-    own = dot(odd, odd_ref[...], 1, 0) + dot(even, even_ref[...], 1, 0)
-    beside = dot(odd, rows_ref[two : two + RIM, :], 1, 0) + dot(even, rows_ref[two + RIM :, :], 1, 0)
-    columns = jnp.concatenate([jnp.where(ra_odd, beside, 0.0), own, jnp.where(ra_odd, 0.0, beside)], 1)
+    own = beside(columns_of(odd_ref[...].astype(F32)), columns_of(even_ref[...].astype(F32)))
+    rims = rows_ref[two : two + RIM, :].astype(F32)
+    side = beside(rims[0:4], rims[4:8])
+    columns = jnp.concatenate([jnp.where(ra_odd, side, 0.0), own, jnp.where(ra_odd, 0.0, side)], 1)
     edges = edge_sums(lane_taps_ref, bands, columns)
     cell = cell_ref[...]
     value = at_column(sum_ref[...], hit_ref[...], cell) + at_edge(edges, hit_ref[...], cell, ny)
@@ -264,24 +281,25 @@
     pl.when(ra_odd)(lambda: side_sums(ext_ref, taps_ref, bands, True, put))
     pl.when(jnp.logical_not(ra_odd))(lambda: side_sums(ext_ref, taps_ref, bands, False, put))
 
-    odd, even = picks()
-    beside = dot(odd, rows_ref[two : two + RIM, :], 1, 0) + dot(even, rows_ref[two + RIM :, :], 1, 0)
-    beside = jnp.where(has_odd, beside, 0.0)
-    columns = jnp.concatenate([jnp.where(ra_odd, 0.0, beside), jnp.zeros((RIM, n), F32), jnp.where(ra_odd, beside, 0.0)], 1)
+    rims = rows_ref[two : two + RIM, :].astype(F32)
+    side = jnp.where(has_odd, beside(rims[0:4], rims[4:8]), 0.0)
+    columns = jnp.concatenate([jnp.where(ra_odd, 0.0, side), jnp.zeros((RIM, n), F32), jnp.where(ra_odd, side, 0.0)], 1)
     edges = edge_sums(lane_taps_ref, bands, columns)
     edges = jnp.where(ra_odd, edges[:, n - two :], edges[:, 0:two])
     hits = hit_ref[pl.ds(pl.multiple_of(jnp.where(ra_odd, n - two, 0), two), two), :]
     cell = cell_ref[...]
     value = even_side_ref[0:1, :] + at_column(sum_ref[...], hits, cell) + at_edge(edges, hits, cell, ny)
-    out_ref[...] = jnp.broadcast_to(lax.rsqrt(value), out_ref.shape).astype(BF16)
-
-
-def stack_weight_kernel(own_ref, odd_ref, even_ref, basis_in_ref, out_ref, basis_ref):
-    at = lax.broadcasted_iota(jnp.int32, out_ref.shape, 0)
+    weights = lax.rsqrt(value)
+    blk = out_ref.shape[1]
+    rows = [weights[:, at : at + blk] for at in range(0, weights.shape[1], blk)]
+    out_ref[...] = jnp.concatenate([*rows, jnp.zeros((out_ref.shape[0] - len(rows), blk), F32)], 0).astype(BF16)
+
+
+def stack_weight_kernel(nblk, own_ref, odd_ref, even_ref, basis_in_ref, out_ref, basis_ref):
     _, has_odd = sides("dec")
-    odd = jnp.where(has_odd, odd_ref[...].astype(F32), 0.0)
-    out = jnp.where(at == 1, odd, own_ref[...].astype(F32))
-    out_ref[...] = jnp.where(at == 2, even_ref[...].astype(F32), out).astype(BF16)
+    own, odd, even = (ref[...].astype(F32)[0:nblk] for ref in (own_ref, odd_ref, even_ref))
+    none = jnp.zeros((out_ref.shape[0] - 3 * nblk, out_ref.shape[1]), F32)
+    out_ref[...] = jnp.concatenate([own, jnp.where(has_odd, odd, 0.0), even, none], 0).astype(BF16)
 
 
 def stack_rows_kernel(a_ref, b_ref, c_ref, after_ref, out_ref):
@@ -309,11 +327,24 @@
     feats, nfreq = freq_ref.shape
     blk = out_ref.shape[2]
     ft_ref[...] = freq_ref[...].astype(F32).T.astype(BF16)
-    for t in tiles:
+
+    def work(t):
         for b in range(nblk):
             c, s = sincos(dot(ft_ref[...], feat_ref[t * feats : (t + 1) * feats, b * blk : (b + 1) * blk], 1, 0))
             out_ref[first + t * nblk + b, 0:nfreq, :] = c.astype(BF16)
             out_ref[first + t * nblk + b, nfreq:, :] = s.astype(BF16)
+
+    def inside():
+        for t in tiles:
+            if t != 1:
+                work(t)
+        if 1 in tiles:
+            pl.when(sides("dec")[1])(functools.partial(work, 1))
+
+    if first == 6 * nblk:
+        pl.when(sides("ra")[1])(inside)
+    else:
+        inside()
 
 
 def own_basis_kernel(nblk, src_ref, count_ref, freq_ref, feat_ref, after_ref, out_ref, code_ref, ft_ref, tile_ref):
@@ -331,20 +362,17 @@
     return dot(jnp.concatenate(lhs, 1), jnp.concatenate(rhs, 1), 1, 1)
 
 
-def spread_weights(w_ref, refs, blk):
-    nblk = refs[0][0].shape[1] // blk
-    w_ref[9 * nblk :, :] = jnp.zeros((w_ref.shape[0] - 9 * nblk, blk), F32)
-    for i, (ref, there) in enumerate(refs):
-        for j in range(3):
-            for b in range(nblk):
-                at = (3 * i + j) * nblk + b
-                w = ref[j : j + 1, b * blk : (b + 1) * blk].astype(F32)
-                w_ref[at : at + 1, :] = w if there is None else jnp.where(there, w, 0.0)
+def spread_weights(w_ref, *refs):
+    rows = w_ref.shape[0] // 9 * 3
+    w_ref[3 * rows :, :] = jnp.zeros((w_ref.shape[0] - 3 * rows, w_ref.shape[1]), F32)
+    for i, ref in enumerate(refs):
+        w = ref[...].astype(F32)[0:rows]
+        w_ref[i * rows : (i + 1) * rows, :] = w if i < 2 else jnp.where(sides("ra")[1], w, 0.0)
 
 
 def early_kernel(code_ref, pip_ref, basis_ref, w_own_ref, w_even_ref, after_ref, sum_ref, w_ref):
     nblk, _, blk, _ = pip_ref.shape
-    spread_weights(w_ref, ((w_own_ref, None), (w_even_ref, None)), blk)
+    spread_weights(w_ref, w_own_ref, w_even_ref)
     for a in range(nblk):
         total = None
         for p in range(0, FIRST, 2):
@@ -357,14 +385,26 @@
     nblk, slots, blk, _ = pip_ref.shape
     nfreq = out_ref.shape[0]
     half, steps = nblk * FIRST, (slots - FIRST) // 2
-    copies = []
-    _, has_odd = sides("ra")
-    spread_weights(w_ref, ((w_own_ref, None), (w_even_ref, None), (w_odd_ref, has_odd)), blk)
+    spread_weights(w_ref, w_own_ref, w_even_ref, w_odd_ref)
     many = code_ref[half + nblk * slots]
+
+    def finish(start_ref, count):
+        copies = []
+        for a in range(nblk):
+            total = start_ref[a]
+            for t in range(count):
+                total = total + pair_sums(code_ref, pip_ref, basis_ref, w_ref, half + a * slots + 2 * t, a)
+            own = basis_ref[a].astype(F32)
+            folded = own[:nfreq] * total[:nfreq] + own[nfreq:] * total[nfreq:]
+            done_ref[a] = (folded * w_ref[a : a + 1, :]).astype(BF16)
+            copies.append(pltpu.make_async_copy(done_ref.at[a], out_ref.at[:, a * blk : (a + 1) * blk], sems.at[a]))
+            copies[-1].start()
+        for copy in copies:
+            copy.wait()
 
     @pl.when(many > steps)
     def _():
-        sum_ref[...] = jnp.zeros_like(sum_ref)
+        sum_ref[...] = early_ref[...]
 
         def step(t, _):
             for a in range(nblk):
@@ -372,22 +412,11 @@
             return _
 
         lax.fori_loop(steps, many, step, 0)
-
-    @pl.when(many <= steps)
-    def _():
-        sum_ref[...] = jnp.zeros_like(sum_ref)
-
-    for a in range(nblk):
-        total = early_ref[a] + sum_ref[a]
-        for t in range(steps):
-            total = total + pair_sums(code_ref, pip_ref, basis_ref, w_ref, half + a * slots + 2 * t, a)
-        own = basis_ref[a].astype(F32)
-        folded = own[:nfreq] * total[:nfreq] + own[nfreq:] * total[nfreq:]
-        done_ref[a] = (folded * w_ref[a : a + 1, :]).astype(BF16)
-        copies.append(pltpu.make_async_copy(done_ref.at[a], out_ref.at[:, a * blk : (a + 1) * blk], sems.at[a]))
-        copies[-1].start()
-    for copy in copies:
-        copy.wait()
+        finish(sum_ref, steps)
+
+    pl.when(many == steps)(lambda: finish(early_ref, steps))
+    pl.when(jnp.logical_and(many > 0, many < steps))(lambda: finish(early_ref, steps - 1))
+    pl.when(many == 0)(lambda: finish(early_ref, 0))
 
 
 def vm(shape, dtype):
@@ -418,22 +447,26 @@
     given = (completeness, features, frequencies, stencil, cells, pair_src, pair_count)
     kept = tuple(vm(x.shape, x.dtype) for x in given[1:5]) + tuple(sm(x.shape) for x in given[5:])
     rim, rows, features, frequencies, stencil, cells, pair_src, pair_count = pl.pallas_call(
-        rim_kernel, out_shape=(vm((RIM, n), BF16), vm((n, ny), F32)) + kept,
+        rim_kernel, out_shape=(vm((RIM, 128), BF16), vm((n, ny), F32)) + kept,
         in_specs=[HBM] * len(given), out_specs=(VMEM,) * 6 + (SMEM,) * 2, compiler_params=params(), name="rim",
         scratch_shapes=[pltpu.VMEM(completeness.shape, F32), pltpu.SemaphoreType.DMA((len(given),))],
     )(*[pltpu.with_memory_space_constraint(x, pltpu.HBM) for x in given])
+    tables = (vm((stencil.shape[0] * bands, ny), F32), vm((5 * RIM, n), F32), vm((n, galaxies), BF16))
+    rim, taps, lane_taps, hit = call(
+        functools.partial(ahead_kernel, bands, nx, ny), (vm((RIM, 128), BF16), *tables), (rim, stencil, cells), (),
+        [pltpu.VMEM((32, 128), F32)], "ahead",
+    )
     d_odd, d_even = exchange("dec", rim, rim)
     f_odd, f_even = exchange("dec", features, features)
     taps, lane_taps, hit = call(
-        functools.partial(ready_kernel, bands, nx, ny),
-        (vm((stencil.shape[0] * bands, ny), F32), vm((5 * RIM, n), F32), vm((n, galaxies), BF16)),
-        (stencil, cells), (rim,), [pltpu.VMEM((32, 128), F32)], "ready",
+        functools.partial(ready_kernel, bands, nx, ny), tables, (stencil, cells), (rim, taps, lane_taps, hit),
+        [pltpu.VMEM((32, 128), F32)], "ready", {3: 0, 4: 1, 5: 2},
     )
     inner = call(
         functools.partial(inner_kernel, bands), vm((n, ny), F32), (rows, taps), (), [pltpu.VMEM((5, n, ny), F32)], "inner",
     )
     to_odd, to_even = call(
-        row_kernel, (vm((two + 2 * RIM, ny), BF16),) * 2, (rows, d_odd, d_even), (inner,), name="rows", cost=LONG
+        row_kernel, (vm((two + RIM, ny), BF16),) * 2, (rows, d_odd, d_even), (inner,), name="rows", cost=LONG
     )
     r_odd, r_even = exchange("ra", to_odd, to_even)
     even_side = call(
@@ -458,7 +491,7 @@
         return call(body, blocks, (frequencies, array), (after, buffer), scratch, "basis%d" % part, {3: 0})
 
     weight, table = call(
-        functools.partial(weight_kernel, bands), (vm((RIM, galaxies), BF16), blocks),
+        functools.partial(weight_kernel, bands), (vm((3 * nblk + 15 & -16, blk), BF16), blocks),
         (even_side, r_odd, taps, lane_taps, hit, cells), (table,),
         [pltpu.VMEM((5, two, ny), F32), pltpu.VMEM((two, ny), F32)], "weight", {6: 1}, LONG,
     )
@@ -466,7 +499,7 @@
     table = basis(0, (1, 2), column, table, weight)
     table = basis(1, (0, 1, 2), c_even, table, weight)
     w_column, table = call(
-        stack_weight_kernel, (vm((RIM, galaxies), BF16), vm(table.shape, BF16)), (weight, w_odd, w_even), (table,), name="stack_weights",
+        functools.partial(stack_weight_kernel, nblk), (vm(weight.shape, BF16), blocks), (weight, w_odd, w_even), (table,), name="stack_weights",
         aliases={3: 1},
     )
     x_odd, x_even = exchange("ra", w_column, w_column)

time: 24.5 us -> 23.5 us (0.959); the launches traced: 24.1 us -> 23.5 us
  Pallas kernels: 11.6 us -> 10 us
  waiting for transfers between devices: 0.03 us -> 0.7 us
  starting transfers between devices: 12.3 us -> 12.6 us
    pallas_call x12 -> x13, Pallas kernels: 8.43 us -> 6.96 us  [call(): pl.pallas_call(body, out_shape=out, in_specs=[SMEM] * len(scalars) + [VME...]
    ppermute x12, waiting for transfers between devices: 0.03 us -> 0.7 us  [swap(): lax.ppermute(payload, ('ra', 'dec'), sorted(pairs + [(b, a) for a, b in p...]
    ppermute x12, starting transfers between devices: 12.3 us -> 12.6 us  [swap(): lax.ppermute(payload, ('ra', 'dec'), sorted(pairs + [(b, a) for a, b in p...]
  transfers between devices with their start and end apart: 12 -> 12, of which waited for: 0 -> 2; matrix products, arithmetic and copies ran while one was open for 0% -> 0% of each run, Pallas kernels for 35% -> 27%
where the time goes in v4:
time: 23.5 us
  starting transfers between devices  12.6 us (54%)
  Pallas kernels  10 us (43%)
  waiting for transfers between devices  0.7 us (3%)
    ppermute x12, starting transfers between devices, swap(): lax.ppermute(payload, ('ra', 'dec'), sorted(pairs + [(b, a) for a, b in p...  12.6 us
    pallas_call x13, Pallas kernels, call(): pl.pallas_call(body, out_shape=out, in_specs=[SMEM] * len(scalars) + [VME...  6.96 us
    pallas_call x1, Pallas kernels, per_device(): pl.pallas_call(pair_kernel, out_shape=jax.ShapeDtypeStruct((nfreq, galaxi...  1.74 us
    pallas_call x1, Pallas kernels, per_device(): pl.pallas_call(rim_kernel, out_shape=(vm((RIM, 128), BF16), vm((n, ny), F...  1.3 us
    ppermute x12, waiting for transfers between devices, swap(): lax.ppermute(payload, ('ra', 'dec'), sorted(pairs + [(b, a) for a, b in p...  0.7 us
  transfers between devices with their start and end apart: 12, of which 2 were waited for; matrix products, arithmetic and copies ran while one was open for 0% of the time, Pallas kernels for 27%

profile of v4, /device:TPU:1, one launch (start us, length us, event | category | flops | bytes accessed | tf_op | source)
XLA Modules:
  0.0 23.5 jit_solution(4006647694551872457)
XLA Ops:
  0.0 1.3 %rim.1 = (bf16[16,128]{1,0:T(8,128)(2,1)S(1)}, f32[512,128]{1,0:T(8,128)S(1)}, bf16[96,512]{1,0:T(8,128)(2,1)S(1)}, bf16[96,256]{1,0:T(8,128)(2,1)S(1)}, f32[25,...) custom-call(f32[64,8,128]{2,1,0:T(8,128)} %refs_0_.1, bf16[96,512]{1,0:T(8,128)(2,1)} %refs_1_.1, ...), custom_call_target="tpu_custom_call" | custom-call | tf_op jit(solution)/shard_map/rim/pallas_call | solution.py:449
  1.3 0.7 %ahead.1 = (bf16[16,128]{1,0:T(8,128)(2,1)S(1)}, f32[1600,128]{1,0:T(8,128)S(1)}, f32[80,512]{1,0:T(8,128)S(1)}, bf16[512,512]{1,0:T(8,128)(2,1)S(1)}) custom-call(bf16[16,128]{1,0:T(8,128)(2,1)S(1)} %get-tuple-element.35.rim_in_ref, f32[25,64]{1,0:T(8,128)S(1)} %get-tuple-element.33.stencil_ref, s32[1,512]{1,0:T(1,128)S(1)} %get-tuple-element.34.cell_ref), custom_call_target="tpu_custom_call" | custom-call | flops 1 | bytes 1 | tf_op jit(solution)/shard_map/ahead/pallas_call | solution.py:439
  2.0 0.1 collective-permute-start.2
  2.1 2.7 %collective-permute-start.3 = (bf16[16,128]{1,0:T(8,128)(2,1)S(1)}, bf16[16,128]{1,0:T(8,128)(2,1)S(1)}, u32[]{:S(2)}, u32[]{:S(2)}) collective-permute-start(bf16[16,128]{1,0:T(8,128)(2,1)S(1)} %get-tuple-element.36.rim_ref), channel_id=1, source_target_pairs={{0,1},{1,0},{2,3},{3,2},{4,5},{5,4},{6,7},{7,6},{8,9},{9,8},{10,11... | collective-permute-start | bytes 12296 | tf_op jit(solution)/shard_map/ppermute | solution.py:41
  4.8 1.2 %collective-permute-start = (bf16[96,512]{1,0:T(8,128)(2,1)S(1)}, bf16[96,512]{1,0:T(8,128)(2,1)S(1)}, u32[]{:S(2)}, u32[]{:S(2)}) collective-permute-start(bf16[96,512]{1,0:T(8,128)(2,1)S(1)} %get-tuple-element.31.a_ref.feat_ref), channel_id=1, source_target_pairs={{0,4},{1,2},{2,1},{3,7},{4,0},{5,6},{6,5},{7,3},{8,12},{9,10},{10,... | collective-permute-start | bytes 294920 | tf_op jit(solution)/shard_map/ppermute | solution.py:41
  6.1 0.8 %collective-permute-start.1 = (bf16[96,512]{1,0:T(8,128)(2,1)S(1)}, bf16[96,512]{1,0:T(8,128)(2,1)S(1)}, u32[]{:S(2)}, u32[]{:S(2)}) collective-permute-start(bf16[96,512]{1,0:T(8,128)(2,1)S(1)} %get-tuple-element.31.a_ref.feat_ref), channel_id=1, source_target_pairs={{0,1},{1,0},{2,3},{3,2},{4,5},{5,4},{6,7},{7,6},{8,9},{9,8},{10,11... | collective-permute-start | bytes 294920 | tf_op jit(solution)/shard_map/ppermute | solution.py:41
  6.8 0.7 %inner.1.after_ref.inner_ref = f32[512,128]{1,0:T(8,128)S(1)} custom-call(f32[512,128]{1,0:T(8,128)S(1)} %get-tuple-element.32.rows_ref, f32[1600,128]{1,0:T(8,128)S(1)} %get-tuple-element.40.taps_ref), custom_call_target="tpu_custom_call" | custom-call | flops 1 | bytes 1 | tf_op jit(solution)/shard_map/inner/pallas_call | solution.py:439
  7.6 0.0 collective-permute-done.2.odd_ref
  7.6 0.0 collective-permute-done.3.even_ref
  7.6 1.0 %collective-permute-start.4 = (bf16[144,128]{1,0:T(8,128)(2,1)S(1)}, bf16[144,128]{1,0:T(8,128)(2,1)S(1)}, u32[]{:S(2)}, u32[]{:S(2)}) collective-permute-start(bf16[144,128]{1,0:T(8,128)(2,1)S(1)} %get-tuple-element.41), channel_id=1, source_target_pairs={{0,4},{1,5},{2,6},{3,7},{4,0},{5,1},{6,2},{7,3},{8,12},{9,13},{10,... | collective-permute-start | bytes 110600 | tf_op jit(solution)/shard_map/ppermute | solution.py:41
  8.6 1.8 %collective-permute-start.6 = (bf16[144,128]{1,0:T(8,128)(2,1)S(1)}, bf16[144,128]{1,0:T(8,128)(2,1)S(1)}, u32[]{:S(2)}, u32[]{:S(2)}) collective-permute-start(bf16[144,128]{1,0:T(8,128)(2,1)S(1)} %get-tuple-element.45), channel_id=1, source_target_pairs={{0,1},{1,0},{2,3},{3,2},{4,8},{5,9},{6,10},{7,11},{8,4},{9,5},{10,... | collective-permute-start | bytes 110600 | tf_op jit(solution)/shard_map/ppermute | solution.py:41
  10.4 0.0 collective-permute-done.4.rows_ref
  10.4 0.5 %even_side.1.after_ref.even_side_ref = f32[8,512]{1,0:T(8,128)S(1)} custom-call(f32[512,128]{1,0:T(8,128)S(1)} %inner.1.after_ref.inner_ref, bf16[16,128]{1,0:T(8,128)(2,1)S(1)} %collective-permute-done.2.odd_ref, bf16[16,128]{1,0:T(8,128)(2,1)S(1)} %collective-permute-done.3.even_ref, bf16[144,128]{1,0:T(8,128)(2,1)S(1)} %collective-permute-done.4.rows_ref, ...), custom_call_target="tpu_custom_call" | custom-call | flops 1 | bytes 1 | tf_op jit(solution)/shard_map/even_side/pallas_call | solution.py:439
  11.0 0.0 collective-permute-done.b_ref
  11.0 0.0 collective-permute-done.1.c_ref
  11.0 0.3 %collective-permute-start.9 = (bf16[288,512]{1,0:T(8,128)(2,1)S(1)}, bf16[288,512]{1,0:T(8,128)(2,1)S(1)}, u32[]{:S(2)}, u32[]{:S(2)}) collective-permute-start(bf16[288,512]{1,0:T(8,128)(2,1)S(1)} %stack_features.1.after_ref.feat_ref), channel_id=1, source_target_pairs={{0,4},{1,5},{2,6},{3,7},{4,0},{5,1},{6,2},{7,3},{8,12},{9,13},{10,... | collective-permute-start | bytes 884744 | tf_op jit(solution)/shard_map/ppermute | solution.py:41
  11.4 1.3 %collective-permute-start.5 = (bf16[288,512]{1,0:T(8,128)(2,1)S(1)}, bf16[288,512]{1,0:T(8,128)(2,1)S(1)}, u32[]{:S(2)}, u32[]{:S(2)}) collective-permute-start(bf16[288,512]{1,0:T(8,128)(2,1)S(1)} %stack_features.1.after_ref.feat_ref), channel_id=1, source_target_pairs={{0,1},{1,0},{2,3},{3,2},{4,8},{5,9},{6,10},{7,11},{8,4},{9,5},{10,... | collective-permute-start | bytes 884744 | tf_op jit(solution)/shard_map/ppermute | solution.py:41
  12.7 0.7 %own_basis.1 = (bf16[36,512,128]{2,1,0:T(8,128)(2,1)S(1)}, s32[74]{0:T(128)S(4)}) custom-call(s32[4,12]{1,0:T(4,128)S(4)} %get-tuple-element.28.src_ref, s32[4]{0:T(128)S(4)} %get-tuple-element.29.count_ref, bf16[96,256]{1,0:T(8,128)(2,1)S(1)} %get-tuple-element.30.freq_ref, bf16[96,512]{1,0:T(8,128)(2,1)S(1)} %get-tuple-element.31.a_ref.feat_ref, ...), custom_call_target="tpu_custom_call" | custom-call | flops 1 | bytes 1 | tf_op jit(solution)/shard_map/own_basis/pallas_call | solution.py:439
  13.4 0.0 collective-permute-done.6.rows_ref
  13.4 0.5 %weight.1 = (bf16[16,128]{1,0:T(8,128)(2,1)S(1)}, bf16[36,512,128]{2,1,0:T(8,128)(2,1)S(1)}) custom-call(f32[8,512]{1,0:T(8,128)S(1)} %even_side.1.after_ref.even_side_ref, bf16[144,128]{1,0:T(8,128)(2,1)S(1)} %collective-permute-done.6.rows_ref, f32[1600,128]{1,0:T(8,128)S(1)} %get-tuple-element.40.taps_ref, ...), custom_call_target="tpu_custom_call", output_to_operand_aliasing={{1}: (6, {})} | custom-call | flops 68719476736 | bytes 1 | tf_op jit(solution)/shard_map/weight/pallas_call | solution.py:439
  13.8 0.1 collective-permute-start.7
  13.9 0.7 %collective-permute-start.8 = (bf16[16,128]{1,0:T(8,128)(2,1)S(1)}, bf16[16,128]{1,0:T(8,128)(2,1)S(1)}, u32[]{:S(2)}, u32[]{:S(2)}) collective-permute-start(bf16[16,128]{1,0:T(8,128)(2,1)S(1)} %get-tuple-element.47.refs_0_.own_ref), channel_id=1, source_target_pairs={{0,1},{1,0},{2,3},{3,2},{4,5},{5,4},{6,7},{7,6},{8,9},{9,8},{10,11... | collective-permute-start | bytes 12296 | tf_op jit(solution)/shard_map/ppermute | solution.py:41
  14.6 0.6 %basis0.1.refs_1_ = bf16[36,512,128]{2,1,0:T(8,128)(2,1)S(1)} custom-call(bf16[96,256]{1,0:T(8,128)(2,1)S(1)} %get-tuple-element.30.freq_ref, bf16[288,512]{1,0:T(8,128)(2,1)S(1)} %stack_features.1.after_ref.feat_ref, bf16[16,128]{1,0:T(8,128)(2,1)S(1)} %get-tuple-element.47.refs_0_.own_ref, ...), custom_call_target="tpu_custom_call", output_to_operand_aliasing={{}: (3, {})} | custom-call | flops 1 | bytes 1 | tf_op jit(solution)/shard_map/basis0/pallas_call | solution.py:439
  15.3 0.0 collective-permute-done.9.feat_ref
  15.3 1.1 %basis1.1.basis_in_ref = bf16[36,512,128]{2,1,0:T(8,128)(2,1)S(1)} custom-call(bf16[96,256]{1,0:T(8,128)(2,1)S(1)} %get-tuple-element.30.freq_ref, bf16[288,512]{1,0:T(8,128)(2,1)S(1)} %collective-permute-done.9.feat_ref, bf16[16,128]{1,0:T(8,128)(2,1)S(1)} %get-tuple-element.47.refs_0_.own_ref, ...), custom_call_target="tpu_custom_call", output_to_operand_aliasing={{}: (3, {})} | custom-call | flops 1 | bytes 1 | tf_op jit(solution)/shard_map/basis1/pallas_call | solution.py:439
  16.4 0.0 copy-start
  16.4 0.0 collective-permute-done.7.odd_ref
  16.4 0.4 %collective-permute-done.8.even_ref = bf16[16,128]{1,0:T(8,128)(2,1)S(1)} collective-permute-done((bf16[16,128]{1,0:T(8,128)(2,1)S(1)}, bf16[16,128]{1,0:T(8,128)(2,1)S(1)}, u32[]{:S(2)}, u32[]{:S(2)}) %collective-permute-start.8) | collective-permute-done | bytes 4128 | tf_op jit(solution)/shard_map/ppermute | solution.py:41
  16.8 1.6 %collective-permute-start.10 = (bf16[16,128]{1,0:T(8,128)(2,1)S(1)}, bf16[16,128]{1,0:T(8,128)(2,1)S(1)}, u32[]{:S(2)}, u32[]{:S(2)}) collective-permute-start(bf16[16,128]{1,0:T(8,128)(2,1)S(1)} %get-tuple-element.50.w_own_ref.after_ref), channel_id=1, source_target_pairs={{0,4},{1,5},{2,6},{3,7},{4,0},{5,1},{6,2},{7,3},{8,12},{9,13},{10,... | collective-permute-start | bytes 12296 | tf_op jit(solution)/shard_map/ppermute | solution.py:41
  18.5 0.9 %collective-permute-start.11 = (bf16[16,128]{1,0:T(8,128)(2,1)S(1)}, bf16[16,128]{1,0:T(8,128)(2,1)S(1)}, u32[]{:S(2)}, u32[]{:S(2)}) collective-permute-start(bf16[16,128]{1,0:T(8,128)(2,1)S(1)} %get-tuple-element.50.w_own_ref.after_ref), channel_id=1, source_target_pairs={{0,1},{1,0},{2,3},{3,2},{4,8},{5,9},{6,10},{7,11},{8,4},{9,5},{10,... | collective-permute-start | bytes 12296 | tf_op jit(solution)/shard_map/ppermute | solution.py:41
  19.4 0.0 collective-permute-done.10.w_even_ref
  19.4 0.0 copy-done
  19.4 1.0 %early_pairs.1.refs_0_.early_ref = f32[4,512,128]{2,1,0:T(8,128)S(1)} custom-call(s32[74]{0:T(128)S(4)} %get-tuple-element.44.code_ref, bf16[4,12,128,128]{3,2,1,0:T(8,128)(2,1)S(1)} %copy-done, bf16[36,512,128]{2,1,0:T(8,128)(2,1)S(1)} %get-tuple-element.49.basis_ref.refs_1_, bf16[16,128]{1,0:T(8,128)(2,1)S(1)} %get-tuple-element.50.w_own_ref.after_ref, ...), custom_call_target="tpu_custom_call" | custom-call | flops 1 | bytes 1 | tf_op jit(solution)/shard_map/early_pairs/pallas_call | solution.py:439
  20.4 0.0 collective-permute-done.5.feat_ref
  20.4 1.1 %basis2.1.basis_ref = bf16[36,512,128]{2,1,0:T(8,128)(2,1)S(1)} custom-call(bf16[96,256]{1,0:T(8,128)(2,1)S(1)} %get-tuple-element.30.freq_ref, bf16[288,512]{1,0:T(8,128)(2,1)S(1)} %collective-permute-done.5.feat_ref, f32[4,512,128]{2,1,0:T(8,128)S(1)} %early_pairs.1.refs_0_.early_ref, ...), custom_call_target="tpu_custom_call", output_to_operand_aliasing={{}: (3, {})} | custom-call | flops 1 | bytes 1 | tf_op jit(solution)/shard_map/basis2/pallas_call | solution.py:439
  21.5 0.2 collective-permute-done.11.w_odd_ref
  21.8 1.7 %pairs.1 = bf16[256,512]{1,0:T(8,128)(2,1)} custom-call(s32[74]{0:T(128)S(4)} %get-tuple-element.44.code_ref, bf16[4,12,128,128]{3,2,1,0:T(8,128)(2,1)S(1)} %copy-done, bf16[36,512,128]{2,1,0:T(8,128)(2,1)S(1)} %basis2.1.basis_ref, f32[4,512,128]{2,1,0:T(8,128)S(1)} %early_pairs.1.refs_0_.early_ref, ...), custom_call_target="tpu_custom_call" | custom-call | tf_op jit(solution)/shard_map/pairs/pallas_call | solution.py:511
  (4 shorter events, 0.1 us)
Async XLA Ops:
  2.0 5.6 %collective-permute-start.2 = (bf16[16,128]{1,0:T(8,128)(2,1)S(1)}, bf16[16,128]{1,0:T(8,128)(2,1)S(1)}, u32[]{:S(2)}, u32[]{:S(2)}) collective-permute-start(bf16[16,128]{1,0:T(8,128)(2,1)S(1)} %get-tuple-element.36.rim_ref), channel_id=1, source_target_pairs={{0,4},{1,2},{2,1},{3,7},{4,0},{5,6},{6,5},{7,3},{8,12},{9,10},{10,... | collective-permute-start | bytes 12296 | tf_op jit(solution)/shard_map/ppermute | solution.py:41
  2.1 5.5 %collective-permute-start.3 = (bf16[16,128]{1,0:T(8,128)(2,1)S(1)}, bf16[16,128]{1,0:T(8,128)(2,1)S(1)}, u32[]{:S(2)}, u32[]{:S(2)}) collective-permute-start(bf16[16,128]{1,0:T(8,128)(2,1)S(1)} %get-tuple-element.36.rim_ref), channel_id=1, source_target_pairs={{0,1},{1,0},{2,3},{3,2},{4,5},{5,4},{6,7},{7,6},{8,9},{9,8},{10,11... | collective-permute-start | bytes 12296 | tf_op jit(solution)/shard_map/ppermute | solution.py:41
  4.8 6.1 %collective-permute-start = (bf16[96,512]{1,0:T(8,128)(2,1)S(1)}, bf16[96,512]{1,0:T(8,128)(2,1)S(1)}, u32[]{:S(2)}, u32[]{:S(2)}) collective-permute-start(bf16[96,512]{1,0:T(8,128)(2,1)S(1)} %get-tuple-element.31.a_ref.feat_ref), channel_id=1, source_target_pairs={{0,4},{1,2},{2,1},{3,7},{4,0},{5,6},{6,5},{7,3},{8,12},{9,10},{10,... | collective-permute-start | bytes 294920 | tf_op jit(solution)/shard_map/ppermute | solution.py:41
  6.1 4.9 %collective-permute-start.1 = (bf16[96,512]{1,0:T(8,128)(2,1)S(1)}, bf16[96,512]{1,0:T(8,128)(2,1)S(1)}, u32[]{:S(2)}, u32[]{:S(2)}) collective-permute-start(bf16[96,512]{1,0:T(8,128)(2,1)S(1)} %get-tuple-element.31.a_ref.feat_ref), channel_id=1, source_target_pairs={{0,1},{1,0},{2,3},{3,2},{4,5},{5,4},{6,7},{7,6},{8,9},{9,8},{10,11... | collective-permute-start | bytes 294920 | tf_op jit(solution)/shard_map/ppermute | solution.py:41
  7.6 2.8 %collective-permute-start.4 = (bf16[144,128]{1,0:T(8,128)(2,1)S(1)}, bf16[144,128]{1,0:T(8,128)(2,1)S(1)}, u32[]{:S(2)}, u32[]{:S(2)}) collective-permute-start(bf16[144,128]{1,0:T(8,128)(2,1)S(1)} %get-tuple-element.41), channel_id=1, source_target_pairs={{0,4},{1,5},{2,6},{3,7},{4,0},{5,1},{6,2},{7,3},{8,12},{9,13},{10,... | collective-permute-start | bytes 110600 | tf_op jit(solution)/shard_map/ppermute | solution.py:41
  8.6 4.8 %collective-permute-start.6 = (bf16[144,128]{1,0:T(8,128)(2,1)S(1)}, bf16[144,128]{1,0:T(8,128)(2,1)S(1)}, u32[]{:S(2)}, u32[]{:S(2)}) collective-permute-start(bf16[144,128]{1,0:T(8,128)(2,1)S(1)} %get-tuple-element.45), channel_id=1, source_target_pairs={{0,1},{1,0},{2,3},{3,2},{4,8},{5,9},{6,10},{7,11},{8,4},{9,5},{10,... | collective-permute-start | bytes 110600 | tf_op jit(solution)/shard_map/ppermute | solution.py:41
  11.0 4.3 %collective-permute-start.9 = (bf16[288,512]{1,0:T(8,128)(2,1)S(1)}, bf16[288,512]{1,0:T(8,128)(2,1)S(1)}, u32[]{:S(2)}, u32[]{:S(2)}) collective-permute-start(bf16[288,512]{1,0:T(8,128)(2,1)S(1)} %stack_features.1.after_ref.feat_ref), channel_id=1, source_target_pairs={{0,4},{1,5},{2,6},{3,7},{4,0},{5,1},{6,2},{7,3},{8,12},{9,13},{10,... | collective-permute-start | bytes 884744 | tf_op jit(solution)/shard_map/ppermute | solution.py:41
  11.4 9.1 %collective-permute-start.5 = (bf16[288,512]{1,0:T(8,128)(2,1)S(1)}, bf16[288,512]{1,0:T(8,128)(2,1)S(1)}, u32[]{:S(2)}, u32[]{:S(2)}) collective-permute-start(bf16[288,512]{1,0:T(8,128)(2,1)S(1)} %stack_features.1.after_ref.feat_ref), channel_id=1, source_target_pairs={{0,1},{1,0},{2,3},{3,2},{4,8},{5,9},{6,10},{7,11},{8,4},{9,5},{10,... | collective-permute-start | bytes 884744 | tf_op jit(solution)/shard_map/ppermute | solution.py:41
  13.8 2.6 %collective-permute-start.7 = (bf16[16,128]{1,0:T(8,128)(2,1)S(1)}, bf16[16,128]{1,0:T(8,128)(2,1)S(1)}, u32[]{:S(2)}, u32[]{:S(2)}) collective-permute-start(bf16[16,128]{1,0:T(8,128)(2,1)S(1)} %get-tuple-element.47.refs_0_.own_ref), channel_id=1, source_target_pairs={{0,4},{1,2},{2,1},{3,7},{4,0},{5,6},{6,5},{7,3},{8,12},{9,10},{10,... | collective-permute-start | bytes 12296 | tf_op jit(solution)/shard_map/ppermute | solution.py:41
  13.9 2.9 %collective-permute-start.8 = (bf16[16,128]{1,0:T(8,128)(2,1)S(1)}, bf16[16,128]{1,0:T(8,128)(2,1)S(1)}, u32[]{:S(2)}, u32[]{:S(2)}) collective-permute-start(bf16[16,128]{1,0:T(8,128)(2,1)S(1)} %get-tuple-element.47.refs_0_.own_ref), channel_id=1, source_target_pairs={{0,1},{1,0},{2,3},{3,2},{4,5},{5,4},{6,7},{7,6},{8,9},{9,8},{10,11... | collective-permute-start | bytes 12296 | tf_op jit(solution)/shard_map/ppermute | solution.py:41
  16.4 3.0 %copy-start = (bf16[4,12,128,128]{3,2,1,0:T(8,128)(2,1)S(1)}, bf16[4,12,128,128]{3,2,1,0:T(8,128)(2,1)}, u32[]{:S(2)}) copy-start(bf16[4,12,128,128]{3,2,1,0:T(8,128)(2,1)} %pip_ref.3) | copy-start | bytes 4718596
  16.8 2.6 %collective-permute-start.10 = (bf16[16,128]{1,0:T(8,128)(2,1)S(1)}, bf16[16,128]{1,0:T(8,128)(2,1)S(1)}, u32[]{:S(2)}, u32[]{:S(2)}) collective-permute-start(bf16[16,128]{1,0:T(8,128)(2,1)S(1)} %get-tuple-element.50.w_own_ref.after_ref), channel_id=1, source_target_pairs={{0,4},{1,5},{2,6},{3,7},{4,0},{5,1},{6,2},{7,3},{8,12},{9,13},{10,... | collective-permute-start | bytes 12296 | tf_op jit(solution)/shard_map/ppermute | solution.py:41
  18.5 3.3 %collective-permute-start.11 = (bf16[16,128]{1,0:T(8,128)(2,1)S(1)}, bf16[16,128]{1,0:T(8,128)(2,1)S(1)}, u32[]{:S(2)}, u32[]{:S(2)}) collective-permute-start(bf16[16,128]{1,0:T(8,128)(2,1)S(1)} %get-tuple-element.50.w_own_ref.after_ref), channel_id=1, source_target_pairs={{0,1},{1,0},{2,3},{3,2},{4,8},{5,9},{6,10},{7,11},{8,4},{9,5},{10,... | collective-permute-start | bytes 12296 | tf_op jit(solution)/shard_map/ppermute | solution.py:41

commit v5 on v4

--- a/solution.py
+++ b/solution.py
@@ -27,24 +27,24 @@
     return pltpu.CompilerParams(vmem_limit_bytes=limit or (16 << 20), **kw)
 
 
-def exchange(axis, odd_payload, even_payload):
+def swap(axis, odd, payload):
     ra, dec = lax.axis_size("ra"), lax.axis_size("dec")
     here = (lambda r, d: r * dec + d) if axis == "ra" else (lambda d, r: r * dec + d)
     count, other = (ra, dec) if axis == "ra" else (dec, ra)
-
-    def swap(payload, odd):
-        pairs = [(here(i, k), here(i + 1, k)) for i in range(odd, count - 1, 2) for k in range(other)]
-        busy = {i for pair in pairs for i in pair}
-        for i in (0, count - 1):
-            ends = [(here(i, k), here(i, k + 1)) for k in range(0, other - 1, 2)]
-            pairs += [pair for pair in ends if not busy & set(pair)]
-        return lax.ppermute(payload, ("ra", "dec"), sorted(pairs + [(b, a) for a, b in pairs]))
-
+    pairs = [(here(i, k), here(i + 1, k)) for i in range(odd, count - 1, 2) for k in range(other)]
+    busy = {i for pair in pairs for i in pair}
+    for i in (0, count - 1):
+        ends = [(here(i, k), here(i, k + 1)) for k in range(0, other - 1, 2)]
+        pairs += [pair for pair in ends if not busy & set(pair)]
+    return lax.ppermute(payload, ("ra", "dec"), sorted(pairs + [(b, a) for a, b in pairs]))
+
+
+def exchange(axis, odd_payload, even_payload):
     if axis == "ra":
-        even = swap(even_payload, 0)
-        return swap(odd_payload, 1), even
-    odd = swap(odd_payload, 1)
-    return odd, swap(even_payload, 0)
+        even = swap(axis, 0, even_payload)
+        return swap(axis, 1, odd_payload), even
+    odd = swap(axis, 1, odd_payload)
+    return odd, swap(axis, 0, even_payload)
 
 
 def sides(axis):
@@ -58,22 +58,32 @@
 
 
 def rim_kernel(*refs):
-    count = (len(refs) - 3) // 2
-    given, (rim_ref, rows_ref), kept = refs[:count], refs[count : count + 2], refs[count + 2 : -2]
+    count = (len(refs) - 4) // 2
+    given, (rim_ref, rows_ref, hit_ref), kept = refs[:count], refs[count : count + 3], refs[count + 3 : -2]
     comp_ref, sems = refs[-2:]
     bands, nx, ny = comp_ref.shape
-    copies = [pltpu.make_async_copy(a, b, sems.at[i]) for i, (a, b) in enumerate(zip(given, (comp_ref, *kept), strict=True))]
+    parts = [pl.ds(at, bands // 4) for at in range(0, bands, bands // 4)]
+    others = list(zip(given[1:], kept, strict=True))
+    pairs = others[:1] + [(given[0].at[part], comp_ref.at[part]) for part in parts] + others[1:]
+    copies = [pltpu.make_async_copy(a, b, sems.at[i]) for i, (a, b) in enumerate(pairs)]
     for copy in copies:
         copy.start()
     row = lax.broadcasted_iota(jnp.int32, (8, ny), 0)
     lane = lax.broadcasted_iota(jnp.int32, (8, ny), 1)
     pick = ((row < 2) & (lane == row)) | ((row >= 2) & (row < 4) & (lane == row + ny - 4))
     copies[0].wait()
-    for x in range(nx):
-        rows_ref[x * bands : (x + 1) * bands, :] = comp_ref[:, x, :]
+    cell = kept[0][...]
+    slot = (cell // ny % nx) * bands + cell // (nx * ny)
+    hit = lax.broadcasted_iota(jnp.int32, hit_ref.shape, 0) == slot
+    hit_ref[...] = jnp.where(hit, 1.0, 0.0).astype(BF16)
+    for copy, part in zip(copies[1:], parts):
+        copy.wait()
+        for x in range(nx):
+            at = x * bands + part.start
+            rows_ref[at : at + part.size, :] = comp_ref[part.start : part.start + part.size, x, :]
     rim = dot(pick.astype(F32).astype(BF16), rows_ref[...].astype(BF16), 1, 1)
     rim_ref[...] = jnp.concatenate([rim[0:4, at : at + 128] for at in range(0, bands * nx, 128)], 0).astype(BF16)
-    for copy in copies[1:]:
+    for copy in copies[len(parts) + 1 :]:
         copy.wait()
 
 
@@ -110,17 +120,17 @@
     return jnp.logical_and(lax.axis_index("ra") < 2, lax.axis_index("dec") == 0)
 
 
-def ahead_kernel(bands, nx, ny, rim_in_ref, stencil_ref, cell_ref, rim_ref, taps_ref, lane_taps_ref, hit_ref, st_ref):
+def ahead_kernel(bands, nx, ny, rim_in_ref, stencil_ref, rim_ref, taps_ref, lane_taps_ref, st_ref):
     rim_ref[...] = rim_in_ref[...]
-    pl.when(leads())(lambda: ready(bands, nx, ny, stencil_ref, cell_ref, taps_ref, lane_taps_ref, hit_ref, st_ref))
-
-
-def ready_kernel(bands, nx, ny, stencil_ref, cell_ref, rim_ref, taps_in_ref, lane_taps_in_ref, hit_in_ref, taps_ref, lane_taps_ref, hit_ref, st_ref):
+    pl.when(leads())(lambda: ready(bands, nx, ny, stencil_ref, taps_ref, lane_taps_ref, st_ref))
+
+
+def ready_kernel(bands, nx, ny, stencil_ref, rim_ref, taps_in_ref, lane_taps_in_ref, taps_ref, lane_taps_ref, st_ref):
     late = jnp.logical_not(leads())
-    pl.when(late)(lambda: ready(bands, nx, ny, stencil_ref, cell_ref, taps_ref, lane_taps_ref, hit_ref, st_ref))
-
-
-def ready(bands, nx, ny, stencil_ref, cell_ref, taps_ref, lane_taps_ref, hit_ref, st_ref):
+    pl.when(late)(lambda: ready(bands, nx, ny, stencil_ref, taps_ref, lane_taps_ref, st_ref))
+
+
+def ready(bands, nx, ny, stencil_ref, taps_ref, lane_taps_ref, st_ref):
     st_ref[...] = jnp.zeros_like(st_ref)
     count = stencil_ref.shape[0]
     st_ref[0:count, 0:bands] = stencil_ref[...]
@@ -133,10 +143,6 @@
     for a in range(5):
         for row, c in ((0, 0), (1, 0), (2, 4), (3, 3), (8, 1), (11, 4)):
             lane_taps_ref[16 * a + row : 16 * a + row + 1, :] = along[5 * a + c : 5 * a + c + 1, :]
-    cell = cell_ref[...]
-    slot = (cell // ny % nx) * bands + cell // (nx * ny)
-    hit = lax.broadcasted_iota(jnp.int32, hit_ref.shape, 0) == slot
-    hit_ref[...] = jnp.where(hit, 1.0, 0.0).astype(BF16)
 
 
 def row_kernel(rows_ref, odd_ref, even_ref, after_ref, to_odd_ref, to_even_ref):
@@ -444,23 +450,23 @@
         )(*scalars, *args, *anys)
 
     cells = gal_cell.reshape(1, galaxies)
-    given = (completeness, features, frequencies, stencil, cells, pair_src, pair_count)
+    given = (completeness, cells, stencil, features, frequencies, pair_src, pair_count)
     kept = tuple(vm(x.shape, x.dtype) for x in given[1:5]) + tuple(sm(x.shape) for x in given[5:])
-    rim, rows, features, frequencies, stencil, cells, pair_src, pair_count = pl.pallas_call(
-        rim_kernel, out_shape=(vm((RIM, 128), BF16), vm((n, ny), F32)) + kept,
-        in_specs=[HBM] * len(given), out_specs=(VMEM,) * 6 + (SMEM,) * 2, compiler_params=params(), name="rim",
-        scratch_shapes=[pltpu.VMEM(completeness.shape, F32), pltpu.SemaphoreType.DMA((len(given),))],
+    rim, rows, hit, cells, stencil, features, frequencies, pair_src, pair_count = pl.pallas_call(
+        rim_kernel, out_shape=(vm((RIM, 128), BF16), vm((n, ny), F32), vm((n, galaxies), BF16)) + kept,
+        in_specs=[HBM] * len(given), out_specs=(VMEM,) * 7 + (SMEM,) * 2, compiler_params=params(), name="rim",
+        scratch_shapes=[pltpu.VMEM(completeness.shape, F32), pltpu.SemaphoreType.DMA((len(given) + 3,))],
     )(*[pltpu.with_memory_space_constraint(x, pltpu.HBM) for x in given])
-    tables = (vm((stencil.shape[0] * bands, ny), F32), vm((5 * RIM, n), F32), vm((n, galaxies), BF16))
-    rim, taps, lane_taps, hit = call(
-        functools.partial(ahead_kernel, bands, nx, ny), (vm((RIM, 128), BF16), *tables), (rim, stencil, cells), (),
+    tables = (vm((stencil.shape[0] * bands, ny), F32), vm((5 * RIM, n), F32))
+    rim, taps, lane_taps = call(
+        functools.partial(ahead_kernel, bands, nx, ny), (vm((RIM, 128), BF16), *tables), (rim, stencil), (),
         [pltpu.VMEM((32, 128), F32)], "ahead",
     )
     d_odd, d_even = exchange("dec", rim, rim)
     f_odd, f_even = exchange("dec", features, features)
-    taps, lane_taps, hit = call(
-        functools.partial(ready_kernel, bands, nx, ny), tables, (stencil, cells), (rim, taps, lane_taps, hit),
-        [pltpu.VMEM((32, 128), F32)], "ready", {3: 0, 4: 1, 5: 2},
+    taps, lane_taps = call(
+        functools.partial(ready_kernel, bands, nx, ny), tables, (stencil,), (rim, taps, lane_taps),
+        [pltpu.VMEM((32, 128), F32)], "ready", {2: 0, 3: 1},
     )
     inner = call(
         functools.partial(inner_kernel, bands), vm((n, ny), F32), (rows, taps), (), [pltpu.VMEM((5, n, ny), F32)], "inner",

time: 23.5 us -> 23.2 us (0.987)
  Pallas kernels: 10 us -> 9.52 us
    pallas_call x1, Pallas kernels: 1.74 us -> 1.46 us  [per_device(): pl.pallas_call(pair_kernel, out_shape=jax.ShapeDtypeStruct((nfreq, galaxi...]
  transfers between devices with their start and end apart: 12 -> 12, of which waited for: 2 -> 3; matrix products, arithmetic and copies ran while one was open for 0% -> 0% of each run, Pallas kernels for 27% -> 27%
where the time goes in v5:
time: 23.2 us; the launch traced here: 23 us
  starting transfers between devices  12.8 us (55%)
  Pallas kernels  9.52 us (41%)
  waiting for transfers between devices  0.54 us (2%)
    ppermute x12, starting transfers between devices, swap(): lax.ppermute(payload, ('ra', 'dec'), sorted(pairs + [(b, a) for a, b in p...  12.8 us
    pallas_call x13, Pallas kernels, call(): pl.pallas_call(body, out_shape=out, in_specs=[SMEM] * len(scalars) + [VME...  6.81 us
    pallas_call x1, Pallas kernels, per_device(): pl.pallas_call(pair_kernel, out_shape=jax.ShapeDtypeStruct((nfreq, galaxi...  1.46 us
    pallas_call x1, Pallas kernels, per_device(): pl.pallas_call(rim_kernel, out_shape=(vm((RIM, 128), BF16), vm((n, ny), F...  1.25 us
    ppermute x12, waiting for transfers between devices, swap(): lax.ppermute(payload, ('ra', 'dec'), sorted(pairs + [(b, a) for a, b in p...  0.54 us
  transfers between devices with their start and end apart: 12, of which 3 were waited for; matrix products, arithmetic and copies ran while one was open for 0% of the time, Pallas kernels for 27%

profile of v5, /device:TPU:1, one launch (start us, length us, event | category | flops | bytes accessed | tf_op | source)
XLA Modules:
  0.0 23.0 jit_solution(8787160134947682670)
XLA Ops:
  0.0 1.3 %rim.1 = (bf16[16,128]{1,0:T(8,128)(2,1)S(1)}, f32[512,128]{1,0:T(8,128)S(1)}, bf16[512,512]{1,0:T(8,128)(2,1)S(1)}, s32[1,512]{1,0:T(1,128)S(1)}, f32[25,64]{1,...) custom-call(f32[64,8,128]{2,1,0:T(8,128)} %refs_0_.1, ...), custom_call_target="tpu_custom_call" | custom-call | tf_op jit(solution)/shard_map/rim/pallas_call | solution.py:455
  1.3 0.5 %ahead.1 = (bf16[16,128]{1,0:T(8,128)(2,1)S(1)}, f32[1600,128]{1,0:T(8,128)S(1)}, f32[80,512]{1,0:T(8,128)S(1)}) custom-call(bf16[16,128]{1,0:T(8,128)(2,1)S(1)} %get-tuple-element.33.rim_in_ref, f32[25,64]{1,0:T(8,128)S(1)} %get-tuple-element.32.stencil_ref), custom_call_target="tpu_custom_call" | custom-call | flops 1 | bytes 1 | tf_op jit(solution)/shard_map/ahead/pallas_call | solution.py:445
  1.8 0.1 collective-permute-start.2
  1.9 2.9 %collective-permute-start.3 = (bf16[16,128]{1,0:T(8,128)(2,1)S(1)}, bf16[16,128]{1,0:T(8,128)(2,1)S(1)}, u32[]{:S(2)}, u32[]{:S(2)}) collective-permute-start(bf16[16,128]{1,0:T(8,128)(2,1)S(1)} %get-tuple-element.34.rim_ref), channel_id=1, source_target_pairs={{0,1},{1,0},{2,3},{3,2},{4,5},{5,4},{6,7},{7,6},{8,9},{9,8},{10,11... | collective-permute-start | bytes 12296 | tf_op jit(solution)/shard_map/ppermute | solution.py:39
  4.8 1.2 %collective-permute-start = (bf16[96,512]{1,0:T(8,128)(2,1)S(1)}, bf16[96,512]{1,0:T(8,128)(2,1)S(1)}, u32[]{:S(2)}, u32[]{:S(2)}) collective-permute-start(bf16[96,512]{1,0:T(8,128)(2,1)S(1)} %get-tuple-element.30.a_ref.feat_ref), channel_id=1, source_target_pairs={{0,4},{1,2},{2,1},{3,7},{4,0},{5,6},{6,5},{7,3},{8,12},{9,10},{10,... | collective-permute-start | bytes 294920 | tf_op jit(solution)/shard_map/ppermute | solution.py:39
  6.0 0.8 %collective-permute-start.1 = (bf16[96,512]{1,0:T(8,128)(2,1)S(1)}, bf16[96,512]{1,0:T(8,128)(2,1)S(1)}, u32[]{:S(2)}, u32[]{:S(2)}) collective-permute-start(bf16[96,512]{1,0:T(8,128)(2,1)S(1)} %get-tuple-element.30.a_ref.feat_ref), channel_id=1, source_target_pairs={{0,1},{1,0},{2,3},{3,2},{4,5},{5,4},{6,7},{7,6},{8,9},{9,8},{10,11... | collective-permute-start | bytes 294920 | tf_op jit(solution)/shard_map/ppermute | solution.py:39
  6.8 0.7 %inner.1.after_ref.inner_ref = f32[512,128]{1,0:T(8,128)S(1)} custom-call(f32[512,128]{1,0:T(8,128)S(1)} %get-tuple-element.31.rows_ref, f32[1600,128]{1,0:T(8,128)S(1)} %get-tuple-element.37.taps_ref), custom_call_target="tpu_custom_call" | custom-call | flops 1 | bytes 1 | tf_op jit(solution)/shard_map/inner/pallas_call | solution.py:445
  7.5 0.0 collective-permute-done.2.odd_ref
  7.5 0.0 collective-permute-done.3.even_ref
  7.6 1.0 %collective-permute-start.4 = (bf16[144,128]{1,0:T(8,128)(2,1)S(1)}, bf16[144,128]{1,0:T(8,128)(2,1)S(1)}, u32[]{:S(2)}, u32[]{:S(2)}) collective-permute-start(bf16[144,128]{1,0:T(8,128)(2,1)S(1)} %get-tuple-element.38), channel_id=1, source_target_pairs={{0,4},{1,5},{2,6},{3,7},{4,0},{5,1},{6,2},{7,3},{8,12},{9,13},{10,... | collective-permute-start | bytes 110600 | tf_op jit(solution)/shard_map/ppermute | solution.py:39
  8.5 1.7 %collective-permute-start.6 = (bf16[144,128]{1,0:T(8,128)(2,1)S(1)}, bf16[144,128]{1,0:T(8,128)(2,1)S(1)}, u32[]{:S(2)}, u32[]{:S(2)}) collective-permute-start(bf16[144,128]{1,0:T(8,128)(2,1)S(1)} %get-tuple-element.43), channel_id=1, source_target_pairs={{0,1},{1,0},{2,3},{3,2},{4,8},{5,9},{6,10},{7,11},{8,4},{9,5},{10,... | collective-permute-start | bytes 110600 | tf_op jit(solution)/shard_map/ppermute | solution.py:39
  10.2 0.0 collective-permute-done.4.rows_ref
  10.2 0.5 %even_side.1.after_ref.even_side_ref = f32[8,512]{1,0:T(8,128)S(1)} custom-call(f32[512,128]{1,0:T(8,128)S(1)} %inner.1.after_ref.inner_ref, bf16[16,128]{1,0:T(8,128)(2,1)S(1)} %collective-permute-done.2.odd_ref, bf16[16,128]{1,0:T(8,128)(2,1)S(1)} %collective-permute-done.3.even_ref, bf16[144,128]{1,0:T(8,128)(2,1)S(1)} %collective-permute-done.4.rows_ref, ...), custom_call_target="tpu_custom_call" | custom-call | flops 1 | bytes 1 | tf_op jit(solution)/shard_map/even_side/pallas_call | solution.py:445
  10.8 0.0 collective-permute-done.b_ref
  10.8 0.0 collective-permute-done.1.c_ref
  10.8 0.5 %collective-permute-start.9 = (bf16[288,512]{1,0:T(8,128)(2,1)S(1)}, bf16[288,512]{1,0:T(8,128)(2,1)S(1)}, u32[]{:S(2)}, u32[]{:S(2)}) collective-permute-start(bf16[288,512]{1,0:T(8,128)(2,1)S(1)} %stack_features.1.after_ref.feat_ref), channel_id=1, source_target_pairs={{0,4},{1,5},{2,6},{3,7},{4,0},{5,1},{6,2},{7,3},{8,12},{9,13},{10,... | collective-permute-start | bytes 884744 | tf_op jit(solution)/shard_map/ppermute | solution.py:39
  11.3 1.2 %collective-permute-start.5 = (bf16[288,512]{1,0:T(8,128)(2,1)S(1)}, bf16[288,512]{1,0:T(8,128)(2,1)S(1)}, u32[]{:S(2)}, u32[]{:S(2)}) collective-permute-start(bf16[288,512]{1,0:T(8,128)(2,1)S(1)} %stack_features.1.after_ref.feat_ref), channel_id=1, source_target_pairs={{0,1},{1,0},{2,3},{3,2},{4,8},{5,9},{6,10},{7,11},{8,4},{9,5},{10,... | collective-permute-start | bytes 884744 | tf_op jit(solution)/shard_map/ppermute | solution.py:39
  12.5 0.7 %own_basis.1 = (bf16[36,512,128]{2,1,0:T(8,128)(2,1)S(1)}, s32[74]{0:T(128)S(4)}) custom-call(s32[4,12]{1,0:T(4,128)S(4)} %get-tuple-element.27.src_ref, s32[4]{0:T(128)S(4)} %get-tuple-element.28.count_ref, bf16[96,256]{1,0:T(8,128)(2,1)S(1)} %get-tuple-element.29.freq_ref, bf16[96,512]{1,0:T(8,128)(2,1)S(1)} %get-tuple-element.30.a_ref.feat_ref, ...), custom_call_target="tpu_custom_call" | custom-call | flops 1 | bytes 1 | tf_op jit(solution)/shard_map/own_basis/pallas_call | solution.py:445
  13.2 0.0 collective-permute-done.6.rows_ref
  13.2 0.5 %weight.1 = (bf16[16,128]{1,0:T(8,128)(2,1)S(1)}, bf16[36,512,128]{2,1,0:T(8,128)(2,1)S(1)}) custom-call(f32[8,512]{1,0:T(8,128)S(1)} %even_side.1.after_ref.even_side_ref, bf16[144,128]{1,0:T(8,128)(2,1)S(1)} %collective-permute-done.6.rows_ref, f32[1600,128]{1,0:T(8,128)S(1)} %get-tuple-element.37.taps_ref, ...), custom_call_target="tpu_custom_call", output_to_operand_aliasing={{1}: (6, {})} | custom-call | flops 68719476736 | bytes 1 | tf_op jit(solution)/shard_map/weight/pallas_call | solution.py:445
  13.6 0.1 collective-permute-start.7
  13.7 0.9 %collective-permute-start.8 = (bf16[16,128]{1,0:T(8,128)(2,1)S(1)}, bf16[16,128]{1,0:T(8,128)(2,1)S(1)}, u32[]{:S(2)}, u32[]{:S(2)}) collective-permute-start(bf16[16,128]{1,0:T(8,128)(2,1)S(1)} %get-tuple-element.45.refs_0_.own_ref), channel_id=1, source_target_pairs={{0,1},{1,0},{2,3},{3,2},{4,5},{5,4},{6,7},{7,6},{8,9},{9,8},{10,11... | collective-permute-start | bytes 12296 | tf_op jit(solution)/shard_map/ppermute | solution.py:39
  14.6 0.6 %basis0.1.refs_1_ = bf16[36,512,128]{2,1,0:T(8,128)(2,1)S(1)} custom-call(bf16[96,256]{1,0:T(8,128)(2,1)S(1)} %get-tuple-element.29.freq_ref, bf16[288,512]{1,0:T(8,128)(2,1)S(1)} %stack_features.1.after_ref.feat_ref, bf16[16,128]{1,0:T(8,128)(2,1)S(1)} %get-tuple-element.45.refs_0_.own_ref, ...), custom_call_target="tpu_custom_call", output_to_operand_aliasing={{}: (3, {})} | custom-call | flops 1 | bytes 1 | tf_op jit(solution)/shard_map/basis0/pallas_call | solution.py:445
  15.2 0.0 collective-permute-done.9.feat_ref
  15.2 1.1 %basis1.1.basis_in_ref = bf16[36,512,128]{2,1,0:T(8,128)(2,1)S(1)} custom-call(bf16[96,256]{1,0:T(8,128)(2,1)S(1)} %get-tuple-element.29.freq_ref, bf16[288,512]{1,0:T(8,128)(2,1)S(1)} %collective-permute-done.9.feat_ref, bf16[16,128]{1,0:T(8,128)(2,1)S(1)} %get-tuple-element.45.refs_0_.own_ref, ...), custom_call_target="tpu_custom_call", output_to_operand_aliasing={{}: (3, {})} | custom-call | flops 1 | bytes 1 | tf_op jit(solution)/shard_map/basis1/pallas_call | solution.py:445
  16.3 0.0 copy-start
  16.3 0.0 collective-permute-done.7.odd_ref
  16.3 0.3 %collective-permute-done.8.even_ref = bf16[16,128]{1,0:T(8,128)(2,1)S(1)} collective-permute-done((bf16[16,128]{1,0:T(8,128)(2,1)S(1)}, bf16[16,128]{1,0:T(8,128)(2,1)S(1)}, u32[]{:S(2)}, u32[]{:S(2)}) %collective-permute-start.8) | collective-permute-done | bytes 4128 | tf_op jit(solution)/shard_map/ppermute | solution.py:39
  16.6 1.6 %collective-permute-start.10 = (bf16[16,128]{1,0:T(8,128)(2,1)S(1)}, bf16[16,128]{1,0:T(8,128)(2,1)S(1)}, u32[]{:S(2)}, u32[]{:S(2)}) collective-permute-start(bf16[16,128]{1,0:T(8,128)(2,1)S(1)} %get-tuple-element.48.w_own_ref.after_ref), channel_id=1, source_target_pairs={{0,4},{1,5},{2,6},{3,7},{4,0},{5,1},{6,2},{7,3},{8,12},{9,13},{10,... | collective-permute-start | bytes 12296 | tf_op jit(solution)/shard_map/ppermute | solution.py:39
  18.3 0.9 %collective-permute-start.11 = (bf16[16,128]{1,0:T(8,128)(2,1)S(1)}, bf16[16,128]{1,0:T(8,128)(2,1)S(1)}, u32[]{:S(2)}, u32[]{:S(2)}) collective-permute-start(bf16[16,128]{1,0:T(8,128)(2,1)S(1)} %get-tuple-element.48.w_own_ref.after_ref), channel_id=1, source_target_pairs={{0,1},{1,0},{2,3},{3,2},{4,8},{5,9},{6,10},{7,11},{8,4},{9,5},{10,... | collective-permute-start | bytes 12296 | tf_op jit(solution)/shard_map/ppermute | solution.py:39
  19.2 0.0 collective-permute-done.10.w_even_ref
  19.2 0.0 copy-done
  19.2 1.0 %early_pairs.1.refs_0_.early_ref = f32[4,512,128]{2,1,0:T(8,128)S(1)} custom-call(s32[74]{0:T(128)S(4)} %get-tuple-element.42.code_ref, bf16[4,12,128,128]{3,2,1,0:T(8,128)(2,1)S(1)} %copy-done, bf16[36,512,128]{2,1,0:T(8,128)(2,1)S(1)} %get-tuple-element.47.basis_ref.refs_1_, bf16[16,128]{1,0:T(8,128)(2,1)S(1)} %get-tuple-element.48.w_own_ref.after_ref, ...), custom_call_target="tpu_custom_call" | custom-call | flops 1 | bytes 1 | tf_op jit(solution)/shard_map/early_pairs/pallas_call | solution.py:445
  20.2 0.1 collective-permute-done.5.feat_ref
  20.4 1.1 %basis2.1.basis_ref = bf16[36,512,128]{2,1,0:T(8,128)(2,1)S(1)} custom-call(bf16[96,256]{1,0:T(8,128)(2,1)S(1)} %get-tuple-element.29.freq_ref, bf16[288,512]{1,0:T(8,128)(2,1)S(1)} %collective-permute-done.5.feat_ref, f32[4,512,128]{2,1,0:T(8,128)S(1)} %early_pairs.1.refs_0_.early_ref, ...), custom_call_target="tpu_custom_call", output_to_operand_aliasing={{}: (3, {})} | custom-call | flops 1 | bytes 1 | tf_op jit(solution)/shard_map/basis2/pallas_call | solution.py:445
  21.5 0.1 collective-permute-done.11.w_odd_ref
  21.6 1.5 %pairs.1 = bf16[256,512]{1,0:T(8,128)(2,1)} custom-call(s32[74]{0:T(128)S(4)} %get-tuple-element.42.code_ref, bf16[4,12,128,128]{3,2,1,0:T(8,128)(2,1)S(1)} %copy-done, bf16[36,512,128]{2,1,0:T(8,128)(2,1)S(1)} %basis2.1.basis_ref, f32[4,512,128]{2,1,0:T(8,128)S(1)} %early_pairs.1.refs_0_.early_ref, ...), custom_call_target="tpu_custom_call" | custom-call | tf_op jit(solution)/shard_map/pairs/pallas_call | solution.py:517
  (4 shorter events, 0.1 us)
Async XLA Ops:
  1.8 5.7 %collective-permute-start.2 = (bf16[16,128]{1,0:T(8,128)(2,1)S(1)}, bf16[16,128]{1,0:T(8,128)(2,1)S(1)}, u32[]{:S(2)}, u32[]{:S(2)}) collective-permute-start(bf16[16,128]{1,0:T(8,128)(2,1)S(1)} %get-tuple-element.34.rim_ref), channel_id=1, source_target_pairs={{0,4},{1,2},{2,1},{3,7},{4,0},{5,6},{6,5},{7,3},{8,12},{9,10},{10,... | collective-permute-start | bytes 12296 | tf_op jit(solution)/shard_map/ppermute | solution.py:39
  1.9 5.6 %collective-permute-start.3 = (bf16[16,128]{1,0:T(8,128)(2,1)S(1)}, bf16[16,128]{1,0:T(8,128)(2,1)S(1)}, u32[]{:S(2)}, u32[]{:S(2)}) collective-permute-start(bf16[16,128]{1,0:T(8,128)(2,1)S(1)} %get-tuple-element.34.rim_ref), channel_id=1, source_target_pairs={{0,1},{1,0},{2,3},{3,2},{4,5},{5,4},{6,7},{7,6},{8,9},{9,8},{10,11... | collective-permute-start | bytes 12296 | tf_op jit(solution)/shard_map/ppermute | solution.py:39
  4.8 6.0 %collective-permute-start = (bf16[96,512]{1,0:T(8,128)(2,1)S(1)}, bf16[96,512]{1,0:T(8,128)(2,1)S(1)}, u32[]{:S(2)}, u32[]{:S(2)}) collective-permute-start(bf16[96,512]{1,0:T(8,128)(2,1)S(1)} %get-tuple-element.30.a_ref.feat_ref), channel_id=1, source_target_pairs={{0,4},{1,2},{2,1},{3,7},{4,0},{5,6},{6,5},{7,3},{8,12},{9,10},{10,... | collective-permute-start | bytes 294920 | tf_op jit(solution)/shard_map/ppermute | solution.py:39
  6.0 4.8 %collective-permute-start.1 = (bf16[96,512]{1,0:T(8,128)(2,1)S(1)}, bf16[96,512]{1,0:T(8,128)(2,1)S(1)}, u32[]{:S(2)}, u32[]{:S(2)}) collective-permute-start(bf16[96,512]{1,0:T(8,128)(2,1)S(1)} %get-tuple-element.30.a_ref.feat_ref), channel_id=1, source_target_pairs={{0,1},{1,0},{2,3},{3,2},{4,5},{5,4},{6,7},{7,6},{8,9},{9,8},{10,11... | collective-permute-start | bytes 294920 | tf_op jit(solution)/shard_map/ppermute | solution.py:39
  7.6 2.7 %collective-permute-start.4 = (bf16[144,128]{1,0:T(8,128)(2,1)S(1)}, bf16[144,128]{1,0:T(8,128)(2,1)S(1)}, u32[]{:S(2)}, u32[]{:S(2)}) collective-permute-start(bf16[144,128]{1,0:T(8,128)(2,1)S(1)} %get-tuple-element.38), channel_id=1, source_target_pairs={{0,4},{1,5},{2,6},{3,7},{4,0},{5,1},{6,2},{7,3},{8,12},{9,13},{10,... | collective-permute-start | bytes 110600 | tf_op jit(solution)/shard_map/ppermute | solution.py:39
  8.5 4.6 %collective-permute-start.6 = (bf16[144,128]{1,0:T(8,128)(2,1)S(1)}, bf16[144,128]{1,0:T(8,128)(2,1)S(1)}, u32[]{:S(2)}, u32[]{:S(2)}) collective-permute-start(bf16[144,128]{1,0:T(8,128)(2,1)S(1)} %get-tuple-element.43), channel_id=1, source_target_pairs={{0,1},{1,0},{2,3},{3,2},{4,8},{5,9},{6,10},{7,11},{8,4},{9,5},{10,... | collective-permute-start | bytes 110600 | tf_op jit(solution)/shard_map/ppermute | solution.py:39
  10.8 4.4 %collective-permute-start.9 = (bf16[288,512]{1,0:T(8,128)(2,1)S(1)}, bf16[288,512]{1,0:T(8,128)(2,1)S(1)}, u32[]{:S(2)}, u32[]{:S(2)}) collective-permute-start(bf16[288,512]{1,0:T(8,128)(2,1)S(1)} %stack_features.1.after_ref.feat_ref), channel_id=1, source_target_pairs={{0,4},{1,5},{2,6},{3,7},{4,0},{5,1},{6,2},{7,3},{8,12},{9,13},{10,... | collective-permute-start | bytes 884744 | tf_op jit(solution)/shard_map/ppermute | solution.py:39
  11.3 9.0 %collective-permute-start.5 = (bf16[288,512]{1,0:T(8,128)(2,1)S(1)}, bf16[288,512]{1,0:T(8,128)(2,1)S(1)}, u32[]{:S(2)}, u32[]{:S(2)}) collective-permute-start(bf16[288,512]{1,0:T(8,128)(2,1)S(1)} %stack_features.1.after_ref.feat_ref), channel_id=1, source_target_pairs={{0,1},{1,0},{2,3},{3,2},{4,8},{5,9},{6,10},{7,11},{8,4},{9,5},{10,... | collective-permute-start | bytes 884744 | tf_op jit(solution)/shard_map/ppermute | solution.py:39
  13.6 2.7 %collective-permute-start.7 = (bf16[16,128]{1,0:T(8,128)(2,1)S(1)}, bf16[16,128]{1,0:T(8,128)(2,1)S(1)}, u32[]{:S(2)}, u32[]{:S(2)}) collective-permute-start(bf16[16,128]{1,0:T(8,128)(2,1)S(1)} %get-tuple-element.45.refs_0_.own_ref), channel_id=1, source_target_pairs={{0,4},{1,2},{2,1},{3,7},{4,0},{5,6},{6,5},{7,3},{8,12},{9,10},{10,... | collective-permute-start | bytes 12296 | tf_op jit(solution)/shard_map/ppermute | solution.py:39
  13.7 2.9 %collective-permute-start.8 = (bf16[16,128]{1,0:T(8,128)(2,1)S(1)}, bf16[16,128]{1,0:T(8,128)(2,1)S(1)}, u32[]{:S(2)}, u32[]{:S(2)}) collective-permute-start(bf16[16,128]{1,0:T(8,128)(2,1)S(1)} %get-tuple-element.45.refs_0_.own_ref), channel_id=1, source_target_pairs={{0,1},{1,0},{2,3},{3,2},{4,5},{5,4},{6,7},{7,6},{8,9},{9,8},{10,11... | collective-permute-start | bytes 12296 | tf_op jit(solution)/shard_map/ppermute | solution.py:39
  16.3 2.9 %copy-start = (bf16[4,12,128,128]{3,2,1,0:T(8,128)(2,1)S(1)}, bf16[4,12,128,128]{3,2,1,0:T(8,128)(2,1)}, u32[]{:S(2)}) copy-start(bf16[4,12,128,128]{3,2,1,0:T(8,128)(2,1)} %pip_ref.3) | copy-start | bytes 4718596
  16.6 2.6 %collective-permute-start.10 = (bf16[16,128]{1,0:T(8,128)(2,1)S(1)}, bf16[16,128]{1,0:T(8,128)(2,1)S(1)}, u32[]{:S(2)}, u32[]{:S(2)}) collective-permute-start(bf16[16,128]{1,0:T(8,128)(2,1)S(1)} %get-tuple-element.48.w_own_ref.after_ref), channel_id=1, source_target_pairs={{0,4},{1,5},{2,6},{3,7},{4,0},{5,1},{6,2},{7,3},{8,12},{9,13},{10,... | collective-permute-start | bytes 12296 | tf_op jit(solution)/shard_map/ppermute | solution.py:39
  18.3 3.3 %collective-permute-start.11 = (bf16[16,128]{1,0:T(8,128)(2,1)S(1)}, bf16[16,128]{1,0:T(8,128)(2,1)S(1)}, u32[]{:S(2)}, u32[]{:S(2)}) collective-permute-start(bf16[16,128]{1,0:T(8,128)(2,1)S(1)} %get-tuple-element.48.w_own_ref.after_ref), channel_id=1, source_target_pairs={{0,1},{1,0},{2,3},{3,2},{4,8},{5,9},{6,10},{7,11},{8,4},{9,5},{10,... | collective-permute-start | bytes 12296 | tf_op jit(solution)/shard_map/ppermute | solution.py:39

commit v6 on v5

--- a/solution.py
+++ b/solution.py
@@ -189,14 +189,16 @@
     return total[0:8] + total[8:16]
 
 
-def extend(ext_ref, cells):
+def shifts(cells):
     ny = cells.shape[1]
     at = lax.broadcasted_iota(jnp.int32, cells.shape, 1)
-    ext_ref[2] = cells
-    ext_ref[3] = jnp.where(at > ny - 2, 0.0, pltpu.roll(cells, ny - 1, 1))
-    ext_ref[4] = jnp.where(at > ny - 3, 0.0, pltpu.roll(cells, ny - 2, 1))
-    ext_ref[1] = jnp.where(at < 1, 0.0, pltpu.roll(cells, 1, 1))
-    ext_ref[0] = jnp.where(at < 2, 0.0, pltpu.roll(cells, 2, 1))
+    return (
+        jnp.where(at < 2, 0.0, pltpu.roll(cells, 2, 1)),
+        jnp.where(at < 1, 0.0, pltpu.roll(cells, 1, 1)),
+        cells,
+        jnp.where(at > ny - 2, 0.0, pltpu.roll(cells, ny - 1, 1)),
+        jnp.where(at > ny - 3, 0.0, pltpu.roll(cells, ny - 2, 1)),
+    )
 
 
 def split(x):
@@ -219,42 +221,43 @@
     return jnp.sum(jnp.where(lax.broadcasted_iota(jnp.int32, found.shape, 0) == row, found, 0.0), axis=0, keepdims=True)
 
 
-def inner_kernel(bands, rows_ref, taps_ref, out_ref, ext_ref):
+def inner_kernel(bands, rows_ref, taps_ref, out_ref):
     n, ny = rows_ref.shape
     nx = n // bands
-    extend(ext_ref, rows_ref[...])
     for g in range(0, bands, 8):
+        cells = [shifts(rows_ref[x * bands + g : x * bands + g + 8, :]) for x in range(nx)]
         accs = [jnp.zeros((8, ny), F32) for _ in range(nx)]
         for c in range(5):
             for a in range(5):
                 w = taps_ref[(5 * a + c) * bands + g : (5 * a + c) * bands + g + 8, :]
                 for x in range(nx):
                     if 0 <= x + a - 2 < nx:
-                        base = (x + a - 2) * bands + g
-                        accs[x] = accs[x] + w * ext_ref[c, base : base + 8, :]
+                        accs[x] = accs[x] + w * cells[x + a - 2][c]
         for x in range(nx):
             out_ref[x * bands + g : x * bands + g + 8, :] = accs[x]
 
 
-def side_sums(ext_ref, taps_ref, bands, up, put):
+def side_sums(rows_ref, taps_ref, bands, up, there, put):
     parts = (((4, 0),), ((3, 0), (4, 1))) if up else (((0, 0), (1, 1)), ((0, 1),))
-    for g in range(0, bands, 8):
-        for x, terms in enumerate(parts):
-            acc = None
-            for a, e in terms:
-                for c in range(5):
-                    tap = (5 * a + c) * bands + g
-                    term = taps_ref[tap : tap + 8, :] * ext_ref[c, e * bands + g : e * bands + g + 8, :]
-                    acc = term if acc is None else acc + term
-            put(x * bands + g, acc)
-
-
-def even_side_kernel(bands, inner_ref, odd_ref, even_ref, rows_ref, taps_ref, lane_taps_ref, hit_ref, cell_ref, out_ref, ext_ref, sum_ref):
+    for g in range(0, bands, 16):
+        pairs = [rows_ref[e * bands + g : e * bands + g + 16, :].astype(F32) for e in range(2)]
+        for h in (0, 8):
+            cells = [shifts(jnp.where(there, pair[h : h + 8], 0.0)) for pair in pairs]
+            for x, terms in enumerate(parts):
+                acc = None
+                for a, e in terms:
+                    for c in range(5):
+                        tap = (5 * a + c) * bands + g + h
+                        term = taps_ref[tap : tap + 8, :] * cells[e][c]
+                        acc = term if acc is None else acc + term
+                put(x * bands + g + h, acc)
+
+
+def even_side_kernel(bands, inner_ref, odd_ref, even_ref, rows_ref, taps_ref, lane_taps_ref, hit_ref, cell_ref, out_ref, sum_ref):
     n, ny = inner_ref.shape
     two = 2 * bands
     ra_odd, _ = sides("ra")
     sum_ref[...] = inner_ref[...]
-    extend(ext_ref, rows_ref[0:two, :].astype(F32))
 
     def add_from(start):
         def put(at, value):
@@ -262,8 +265,8 @@
 
         return put
 
-    pl.when(ra_odd)(lambda: side_sums(ext_ref, taps_ref, bands, False, add_from(0)))
-    pl.when(jnp.logical_not(ra_odd))(lambda: side_sums(ext_ref, taps_ref, bands, True, add_from(n - two)))
+    pl.when(ra_odd)(lambda: side_sums(rows_ref, taps_ref, bands, False, True, add_from(0)))
+    pl.when(jnp.logical_not(ra_odd))(lambda: side_sums(rows_ref, taps_ref, bands, True, True, add_from(n - two)))
 
     own = beside(columns_of(odd_ref[...].astype(F32)), columns_of(even_ref[...].astype(F32)))
     rims = rows_ref[two : two + RIM, :].astype(F32)
@@ -275,17 +278,16 @@
     out_ref[...] = jnp.broadcast_to(value, out_ref.shape)
 
 
-def weight_kernel(bands, even_side_ref, rows_ref, taps_ref, lane_taps_ref, hit_ref, cell_ref, basis_in_ref, out_ref, basis_ref, ext_ref, sum_ref):
+def weight_kernel(bands, even_side_ref, rows_ref, taps_ref, lane_taps_ref, hit_ref, cell_ref, basis_in_ref, out_ref, basis_ref, sum_ref):
     two, ny = sum_ref.shape
     n = hit_ref.shape[0]
     ra_odd, has_odd = sides("ra")
-    extend(ext_ref, jnp.where(has_odd, rows_ref[0:two, :].astype(F32), 0.0))
 
     def put(at, value):
         sum_ref[at : at + 8, :] = value
 
-    pl.when(ra_odd)(lambda: side_sums(ext_ref, taps_ref, bands, True, put))
-    pl.when(jnp.logical_not(ra_odd))(lambda: side_sums(ext_ref, taps_ref, bands, False, put))
+    pl.when(ra_odd)(lambda: side_sums(rows_ref, taps_ref, bands, True, has_odd, put))
+    pl.when(jnp.logical_not(ra_odd))(lambda: side_sums(rows_ref, taps_ref, bands, False, has_odd, put))
 
     rims = rows_ref[two : two + RIM, :].astype(F32)
     side = jnp.where(has_odd, beside(rims[0:4], rims[4:8]), 0.0)
@@ -329,7 +331,7 @@
     return c, s * r
 
 
-def basis_kernel(first, tiles, nblk, freq_ref, feat_ref, out_ref, ft_ref):
+def basis_kernel(first, tiles, nblk, freq_ref, feat_ref, out_ref, ft_ref, wide_ref=None):
     feats, nfreq = freq_ref.shape
     blk = out_ref.shape[2]
     ft_ref[...] = freq_ref[...].astype(F32).T.astype(BF16)
@@ -337,6 +339,9 @@
     def work(t):
         for b in range(nblk):
             c, s = sincos(dot(ft_ref[...], feat_ref[t * feats : (t + 1) * feats, b * blk : (b + 1) * blk], 1, 0))
+            if wide_ref is not None:
+                wide_ref[b, 0:nfreq, :] = c
+                wide_ref[b, nfreq:, :] = s
             out_ref[first + t * nblk + b, 0:nfreq, :] = c.astype(BF16)
             out_ref[first + t * nblk + b, nfreq:, :] = s.astype(BF16)
 
@@ -353,9 +358,9 @@
         inside()
 
 
-def own_basis_kernel(nblk, src_ref, count_ref, freq_ref, feat_ref, after_ref, out_ref, code_ref, ft_ref, tile_ref):
+def own_basis_kernel(nblk, src_ref, count_ref, freq_ref, feat_ref, after_ref, out_ref, wide_ref, code_ref, ft_ref, tile_ref):
     list_slots(nblk, src_ref, count_ref, code_ref, tile_ref)
-    basis_kernel(0, (0,), nblk, freq_ref, feat_ref, out_ref, ft_ref)
+    basis_kernel(0, (0,), nblk, freq_ref, feat_ref, out_ref, ft_ref, wide_ref)
 
 
 def pair_sums(code_ref, pip_ref, basis_ref, w_ref, at, a):
@@ -387,7 +392,7 @@
         sum_ref[a] = total
 
 
-def pair_kernel(code_ref, pip_ref, basis_ref, early_ref, w_own_ref, w_even_ref, w_odd_ref, out_ref, w_ref, sum_ref, done_ref, sems):
+def pair_kernel(code_ref, pip_ref, basis_ref, own_ref, early_ref, w_own_ref, w_even_ref, w_odd_ref, out_ref, w_ref, sum_ref, done_ref, sems):
     nblk, slots, blk, _ = pip_ref.shape
     nfreq = out_ref.shape[0]
     half, steps = nblk * FIRST, (slots - FIRST) // 2
@@ -400,8 +405,7 @@
             total = start_ref[a]
             for t in range(count):
                 total = total + pair_sums(code_ref, pip_ref, basis_ref, w_ref, half + a * slots + 2 * t, a)
-            own = basis_ref[a].astype(F32)
-            folded = own[:nfreq] * total[:nfreq] + own[nfreq:] * total[nfreq:]
+            folded = own_ref[a, 0:nfreq] * total[:nfreq] + own_ref[a, nfreq:] * total[nfreq:]
             done_ref[a] = (folded * w_ref[a : a + 1, :]).astype(BF16)
             copies.append(pltpu.make_async_copy(done_ref.at[a], out_ref.at[:, a * blk : (a + 1) * blk], sems.at[a]))
             copies[-1].start()
@@ -469,7 +473,7 @@
         [pltpu.VMEM((32, 128), F32)], "ready", {2: 0, 3: 1},
     )
     inner = call(
-        functools.partial(inner_kernel, bands), vm((n, ny), F32), (rows, taps), (), [pltpu.VMEM((5, n, ny), F32)], "inner",
+        functools.partial(inner_kernel, bands), vm((n, ny), F32), (rows, taps), (), (), "inner",
     )
     to_odd, to_even = call(
         row_kernel, (vm((two + RIM, ny), BF16),) * 2, (rows, d_odd, d_even), (inner,), name="rows", cost=LONG
@@ -478,15 +482,15 @@
     even_side = call(
         functools.partial(even_side_kernel, bands), vm((8, galaxies), F32),
         (inner, d_odd, d_even, r_even, taps, lane_taps, hit, cells), (),
-        [pltpu.VMEM((5, two, ny), F32), pltpu.VMEM((n, ny), F32)], "even_side",
+        [pltpu.VMEM((n, ny), F32)], "even_side",
     )
     column = call(stack_rows_kernel, vm((3 * feats, galaxies), BF16), (features, f_odd, f_even), (even_side,), name="stack_features")
     c_odd, c_even = exchange("ra", column, column)
 
     blocks = vm((9 * nblk, 2 * nfreq, blk), BF16)
     scratch = [pltpu.VMEM((nfreq, feats), BF16)]
-    table, code = call(
-        functools.partial(own_basis_kernel, nblk), (blocks, sm((nblk * (FIRST + slots) + 2,))), (frequencies, features), (column,),
+    table, own_wide, code = call(
+        functools.partial(own_basis_kernel, nblk), (blocks, vm((nblk, 2 * nfreq, blk), F32), sm((nblk * (FIRST + slots) + 2,))), (frequencies, features), (column,),
         scratch + [pltpu.SMEM((9,), jnp.int32)], "own_basis", scalars=(pair_src, pair_count),
     )
 
@@ -499,7 +503,7 @@
     weight, table = call(
         functools.partial(weight_kernel, bands), (vm((3 * nblk + 15 & -16, blk), BF16), blocks),
         (even_side, r_odd, taps, lane_taps, hit, cells), (table,),
-        [pltpu.VMEM((5, two, ny), F32), pltpu.VMEM((two, ny), F32)], "weight", {6: 1}, LONG,
+        [pltpu.VMEM((two, ny), F32)], "weight", {6: 1}, LONG,
     )
     w_odd, w_even = exchange("dec", weight, weight)
     table = basis(0, (1, 2), column, table, weight)
@@ -515,13 +519,13 @@
     )
     table = basis(2, (0, 1, 2), c_odd, table, early)
     return pl.pallas_call(
-        pair_kernel, out_shape=jax.ShapeDtypeStruct((nfreq, galaxies), BF16), in_specs=[SMEM] + [VMEM] * 6, out_specs=ANY,
+        pair_kernel, out_shape=jax.ShapeDtypeStruct((nfreq, galaxies), BF16), in_specs=[SMEM] + [VMEM] * 7, out_specs=ANY,
         scratch_shapes=[
             pltpu.VMEM((9 * nblk + 4, blk), F32), pltpu.VMEM((nblk, 2 * nfreq, blk), F32),
             pltpu.VMEM((nblk, nfreq, blk), BF16), pltpu.SemaphoreType.DMA((nblk,)),
         ],
         compiler_params=params(), name="pairs",
-    )(code, pip, table, early, w_column, x_even, x_odd)
+    )(code, pip, table, own_wide, early, w_column, x_even, x_odd)
 
 
 def solution(mesh):

time: 23.2 us -> 23.2 us (level)
  transfers between devices with their start and end apart: 12 -> 12, of which waited for: 3 -> 2; matrix products, arithmetic and copies ran while one was open for 0% -> 0% of each run, Pallas kernels for 27% -> 27%
where the time goes in v6:
time: 23.2 us; the launch traced here: 23 us
  starting transfers between devices  12.9 us (56%)
  Pallas kernels  9.4 us (41%)
  waiting for transfers between devices  0.53 us (2%)
    ppermute x12, starting transfers between devices, swap(): lax.ppermute(payload, ('ra', 'dec'), sorted(pairs + [(b, a) for a, b in p...  12.9 us
    pallas_call x13, Pallas kernels, call(): pl.pallas_call(body, out_shape=out, in_specs=[SMEM] * len(scalars) + [VME...  6.7 us
    pallas_call x1, Pallas kernels, per_device(): pl.pallas_call(pair_kernel, out_shape=jax.ShapeDtypeStruct((nfreq, galaxi...  1.45 us
    pallas_call x1, Pallas kernels, per_device(): pl.pallas_call(rim_kernel, out_shape=(vm((RIM, 128), BF16), vm((n, ny), F...  1.25 us
    ppermute x12, waiting for transfers between devices, swap(): lax.ppermute(payload, ('ra', 'dec'), sorted(pairs + [(b, a) for a, b in p...  0.53 us
  transfers between devices with their start and end apart: 12, of which 2 were waited for; matrix products, arithmetic and copies ran while one was open for 0% of the time, Pallas kernels for 27%

profile of v6, /device:TPU:1, one launch (start us, length us, event | category | flops | bytes accessed | tf_op | source)
XLA Modules:
  0.0 23.0 jit_solution(14808699814088252439)
XLA Ops:
  0.0 1.3 %rim.1 = (bf16[16,128]{1,0:T(8,128)(2,1)S(1)}, f32[512,128]{1,0:T(8,128)S(1)}, bf16[512,512]{1,0:T(8,128)(2,1)S(1)}, s32[1,512]{1,0:T(1,128)S(1)}, f32[25,64]{1,...) custom-call(f32[64,8,128]{2,1,0:T(8,128)} %refs_0_.1, ...), custom_call_target="tpu_custom_call" | custom-call | tf_op jit(solution)/shard_map/rim/pallas_call | solution.py:459
  1.3 0.5 %ahead.1 = (bf16[16,128]{1,0:T(8,128)(2,1)S(1)}, f32[1600,128]{1,0:T(8,128)S(1)}, f32[80,512]{1,0:T(8,128)S(1)}) custom-call(bf16[16,128]{1,0:T(8,128)(2,1)S(1)} %get-tuple-element.34.rim_in_ref, f32[25,64]{1,0:T(8,128)S(1)} %get-tuple-element.33.stencil_ref), custom_call_target="tpu_custom_call" | custom-call | flops 1 | bytes 1 | tf_op jit(solution)/shard_map/ahead/pallas_call | solution.py:449
  1.8 0.1 collective-permute-start.2
  1.9 2.9 %collective-permute-start.3 = (bf16[16,128]{1,0:T(8,128)(2,1)S(1)}, bf16[16,128]{1,0:T(8,128)(2,1)S(1)}, u32[]{:S(2)}, u32[]{:S(2)}) collective-permute-start(bf16[16,128]{1,0:T(8,128)(2,1)S(1)} %get-tuple-element.35.rim_ref), channel_id=1, source_target_pairs={{0,1},{1,0},{2,3},{3,2},{4,5},{5,4},{6,7},{7,6},{8,9},{9,8},{10,11... | collective-permute-start | bytes 12296 | tf_op jit(solution)/shard_map/ppermute | solution.py:39
  4.8 1.2 %collective-permute-start = (bf16[96,512]{1,0:T(8,128)(2,1)S(1)}, bf16[96,512]{1,0:T(8,128)(2,1)S(1)}, u32[]{:S(2)}, u32[]{:S(2)}) collective-permute-start(bf16[96,512]{1,0:T(8,128)(2,1)S(1)} %get-tuple-element.31.a_ref.feat_ref), channel_id=1, source_target_pairs={{0,4},{1,2},{2,1},{3,7},{4,0},{5,6},{6,5},{7,3},{8,12},{9,10},{10,... | collective-permute-start | bytes 294920 | tf_op jit(solution)/shard_map/ppermute | solution.py:39
  6.0 0.8 %collective-permute-start.1 = (bf16[96,512]{1,0:T(8,128)(2,1)S(1)}, bf16[96,512]{1,0:T(8,128)(2,1)S(1)}, u32[]{:S(2)}, u32[]{:S(2)}) collective-permute-start(bf16[96,512]{1,0:T(8,128)(2,1)S(1)} %get-tuple-element.31.a_ref.feat_ref), channel_id=1, source_target_pairs={{0,1},{1,0},{2,3},{3,2},{4,5},{5,4},{6,7},{7,6},{8,9},{9,8},{10,11... | collective-permute-start | bytes 294920 | tf_op jit(solution)/shard_map/ppermute | solution.py:39
  6.8 0.5 %inner.1.after_ref.inner_ref = f32[512,128]{1,0:T(8,128)S(1)} custom-call(f32[512,128]{1,0:T(8,128)S(1)} %get-tuple-element.32.rows_ref, f32[1600,128]{1,0:T(8,128)S(1)} %get-tuple-element.38.taps_ref), custom_call_target="tpu_custom_call" | custom-call | flops 1 | bytes 1 | tf_op jit(solution)/shard_map/inner/pallas_call | solution.py:449
  7.3 0.0 collective-permute-done.2.odd_ref
  7.3 0.0 collective-permute-done.3.even_ref
  7.3 1.0 %collective-permute-start.4 = (bf16[144,128]{1,0:T(8,128)(2,1)S(1)}, bf16[144,128]{1,0:T(8,128)(2,1)S(1)}, u32[]{:S(2)}, u32[]{:S(2)}) collective-permute-start(bf16[144,128]{1,0:T(8,128)(2,1)S(1)} %get-tuple-element.39), channel_id=1, source_target_pairs={{0,4},{1,5},{2,6},{3,7},{4,0},{5,1},{6,2},{7,3},{8,12},{9,13},{10,... | collective-permute-start | bytes 110600 | tf_op jit(solution)/shard_map/ppermute | solution.py:39
  8.3 1.7 %collective-permute-start.6 = (bf16[144,128]{1,0:T(8,128)(2,1)S(1)}, bf16[144,128]{1,0:T(8,128)(2,1)S(1)}, u32[]{:S(2)}, u32[]{:S(2)}) collective-permute-start(bf16[144,128]{1,0:T(8,128)(2,1)S(1)} %get-tuple-element.44), channel_id=1, source_target_pairs={{0,1},{1,0},{2,3},{3,2},{4,8},{5,9},{6,10},{7,11},{8,4},{9,5},{10,... | collective-permute-start | bytes 110600 | tf_op jit(solution)/shard_map/ppermute | solution.py:39
  10.0 0.0 collective-permute-done.4.rows_ref
  10.0 0.5 %even_side.1.after_ref.even_side_ref = f32[8,512]{1,0:T(8,128)S(1)} custom-call(f32[512,128]{1,0:T(8,128)S(1)} %inner.1.after_ref.inner_ref, bf16[16,128]{1,0:T(8,128)(2,1)S(1)} %collective-permute-done.2.odd_ref, bf16[16,128]{1,0:T(8,128)(2,1)S(1)} %collective-permute-done.3.even_ref, bf16[144,128]{1,0:T(8,128)(2,1)S(1)} %collective-permute-done.4.rows_ref, ...), custom_call_target="tpu_custom_call" | custom-call | flops 1 | bytes 1 | tf_op jit(solution)/shard_map/even_side/pallas_call | solution.py:449
  10.5 0.0 collective-permute-done.b_ref
  10.5 0.0 collective-permute-done.1.c_ref
  10.6 0.7 %collective-permute-start.9 = (bf16[288,512]{1,0:T(8,128)(2,1)S(1)}, bf16[288,512]{1,0:T(8,128)(2,1)S(1)}, u32[]{:S(2)}, u32[]{:S(2)}) collective-permute-start(bf16[288,512]{1,0:T(8,128)(2,1)S(1)} %stack_features.1.after_ref.feat_ref), channel_id=1, source_target_pairs={{0,4},{1,5},{2,6},{3,7},{4,0},{5,1},{6,2},{7,3},{8,12},{9,13},{10,... | collective-permute-start | bytes 884744 | tf_op jit(solution)/shard_map/ppermute | solution.py:39
  11.3 1.2 %collective-permute-start.5 = (bf16[288,512]{1,0:T(8,128)(2,1)S(1)}, bf16[288,512]{1,0:T(8,128)(2,1)S(1)}, u32[]{:S(2)}, u32[]{:S(2)}) collective-permute-start(bf16[288,512]{1,0:T(8,128)(2,1)S(1)} %stack_features.1.after_ref.feat_ref), channel_id=1, source_target_pairs={{0,1},{1,0},{2,3},{3,2},{4,8},{5,9},{6,10},{7,11},{8,4},{9,5},{10,... | collective-permute-start | bytes 884744 | tf_op jit(solution)/shard_map/ppermute | solution.py:39
  12.5 0.8 %own_basis.1 = (bf16[36,512,128]{2,1,0:T(8,128)(2,1)S(1)}, f32[4,512,128]{2,1,0:T(8,128)S(1)}, s32[74]{0:T(128)S(4)}) custom-call(s32[4,12]{1,0:T(4,128)S(4)} %get-tuple-element.28.src_ref, s32[4]{0:T(128)S(4)} %get-tuple-element.29.count_ref, bf16[96,256]{1,0:T(8,128)(2,1)S(1)} %get-tuple-element.30.freq_ref, ...), custom_call_target="tpu_custom_call" | custom-call | flops 1 | bytes 1 | tf_op jit(solution)/shard_map/own_basis/pallas_call | solution.py:449
  13.3 0.0 collective-permute-done.6.rows_ref
  13.3 0.4 %weight.1 = (bf16[16,128]{1,0:T(8,128)(2,1)S(1)}, bf16[36,512,128]{2,1,0:T(8,128)(2,1)S(1)}) custom-call(f32[8,512]{1,0:T(8,128)S(1)} %even_side.1.after_ref.even_side_ref, bf16[144,128]{1,0:T(8,128)(2,1)S(1)} %collective-permute-done.6.rows_ref, f32[1600,128]{1,0:T(8,128)S(1)} %get-tuple-element.38.taps_ref, ...), custom_call_target="tpu_custom_call", output_to_operand_aliasing={{1}: (6, {})} | custom-call | flops 68719476736 | bytes 1 | tf_op jit(solution)/shard_map/weight/pallas_call | solution.py:449
  13.8 0.1 collective-permute-start.7
  13.8 0.9 %collective-permute-start.8 = (bf16[16,128]{1,0:T(8,128)(2,1)S(1)}, bf16[16,128]{1,0:T(8,128)(2,1)S(1)}, u32[]{:S(2)}, u32[]{:S(2)}) collective-permute-start(bf16[16,128]{1,0:T(8,128)(2,1)S(1)} %get-tuple-element.46.refs_0_.own_ref), channel_id=1, source_target_pairs={{0,1},{1,0},{2,3},{3,2},{4,5},{5,4},{6,7},{7,6},{8,9},{9,8},{10,11... | collective-permute-start | bytes 12296 | tf_op jit(solution)/shard_map/ppermute | solution.py:39
  14.7 0.6 %basis0.1.refs_1_ = bf16[36,512,128]{2,1,0:T(8,128)(2,1)S(1)} custom-call(bf16[96,256]{1,0:T(8,128)(2,1)S(1)} %get-tuple-element.30.freq_ref, bf16[288,512]{1,0:T(8,128)(2,1)S(1)} %stack_features.1.after_ref.feat_ref, bf16[16,128]{1,0:T(8,128)(2,1)S(1)} %get-tuple-element.46.refs_0_.own_ref, ...), custom_call_target="tpu_custom_call", output_to_operand_aliasing={{}: (3, {})} | custom-call | flops 1 | bytes 1 | tf_op jit(solution)/shard_map/basis0/pallas_call | solution.py:449
  15.4 0.0 collective-permute-done.9.feat_ref
  15.4 1.1 %basis1.1.basis_in_ref = bf16[36,512,128]{2,1,0:T(8,128)(2,1)S(1)} custom-call(bf16[96,256]{1,0:T(8,128)(2,1)S(1)} %get-tuple-element.30.freq_ref, bf16[288,512]{1,0:T(8,128)(2,1)S(1)} %collective-permute-done.9.feat_ref, bf16[16,128]{1,0:T(8,128)(2,1)S(1)} %get-tuple-element.46.refs_0_.own_ref, ...), custom_call_target="tpu_custom_call", output_to_operand_aliasing={{}: (3, {})} | custom-call | flops 1 | bytes 1 | tf_op jit(solution)/shard_map/basis1/pallas_call | solution.py:449
  16.5 0.0 copy-start
  16.5 0.0 collective-permute-done.7.odd_ref
  16.5 0.3 %collective-permute-done.8.even_ref = bf16[16,128]{1,0:T(8,128)(2,1)S(1)} collective-permute-done((bf16[16,128]{1,0:T(8,128)(2,1)S(1)}, bf16[16,128]{1,0:T(8,128)(2,1)S(1)}, u32[]{:S(2)}, u32[]{:S(2)}) %collective-permute-start.8) | collective-permute-done | bytes 4128 | tf_op jit(solution)/shard_map/ppermute | solution.py:39
  16.8 1.5 %collective-permute-start.10 = (bf16[16,128]{1,0:T(8,128)(2,1)S(1)}, bf16[16,128]{1,0:T(8,128)(2,1)S(1)}, u32[]{:S(2)}, u32[]{:S(2)}) collective-permute-start(bf16[16,128]{1,0:T(8,128)(2,1)S(1)} %get-tuple-element.49.w_own_ref.after_ref), channel_id=1, source_target_pairs={{0,4},{1,5},{2,6},{3,7},{4,0},{5,1},{6,2},{7,3},{8,12},{9,13},{10,... | collective-permute-start | bytes 12296 | tf_op jit(solution)/shard_map/ppermute | solution.py:39
  18.3 0.9 %collective-permute-start.11 = (bf16[16,128]{1,0:T(8,128)(2,1)S(1)}, bf16[16,128]{1,0:T(8,128)(2,1)S(1)}, u32[]{:S(2)}, u32[]{:S(2)}) collective-permute-start(bf16[16,128]{1,0:T(8,128)(2,1)S(1)} %get-tuple-element.49.w_own_ref.after_ref), channel_id=1, source_target_pairs={{0,1},{1,0},{2,3},{3,2},{4,8},{5,9},{6,10},{7,11},{8,4},{9,5},{10,... | collective-permute-start | bytes 12296 | tf_op jit(solution)/shard_map/ppermute | solution.py:39
  19.2 0.0 collective-permute-done.10.w_even_ref
  19.2 0.0 copy-done
  19.2 1.0 %early_pairs.1.refs_0_.early_ref = f32[4,512,128]{2,1,0:T(8,128)S(1)} custom-call(s32[74]{0:T(128)S(4)} %get-tuple-element.43.code_ref, bf16[4,12,128,128]{3,2,1,0:T(8,128)(2,1)S(1)} %copy-done, bf16[36,512,128]{2,1,0:T(8,128)(2,1)S(1)} %get-tuple-element.48.basis_ref.refs_1_, bf16[16,128]{1,0:T(8,128)(2,1)S(1)} %get-tuple-element.49.w_own_ref.after_ref, ...), custom_call_target="tpu_custom_call" | custom-call | flops 1 | bytes 1 | tf_op jit(solution)/shard_map/early_pairs/pallas_call | solution.py:449
  20.2 0.0 collective-permute-done.5.feat_ref
  20.3 1.1 %basis2.1.basis_ref = bf16[36,512,128]{2,1,0:T(8,128)(2,1)S(1)} custom-call(bf16[96,256]{1,0:T(8,128)(2,1)S(1)} %get-tuple-element.30.freq_ref, bf16[288,512]{1,0:T(8,128)(2,1)S(1)} %collective-permute-done.5.feat_ref, f32[4,512,128]{2,1,0:T(8,128)S(1)} %early_pairs.1.refs_0_.early_ref, ...), custom_call_target="tpu_custom_call", output_to_operand_aliasing={{}: (3, {})} | custom-call | flops 1 | bytes 1 | tf_op jit(solution)/shard_map/basis2/pallas_call | solution.py:449
  21.4 0.2 collective-permute-done.11.w_odd_ref
  21.6 1.4 %pairs.1 = bf16[256,512]{1,0:T(8,128)(2,1)} custom-call(s32[74]{0:T(128)S(4)} %get-tuple-element.43.code_ref, bf16[4,12,128,128]{3,2,1,0:T(8,128)(2,1)S(1)} %copy-done, bf16[36,512,128]{2,1,0:T(8,128)(2,1)S(1)} %basis2.1.basis_ref, f32[4,512,128]{2,1,0:T(8,128)S(1)} %get-tuple-element.50.own_ref, f32[4,512,128]{2,1,0:T(8,128)S(1)} %early_pairs.1.refs_0_.early_ref, ...), custom_call_target="tpu_custom_call" | custom-call | tf_op jit(solution)/shard_map/pairs/pallas_call | solution.py:521
  (4 shorter events, 0.1 us)
Async XLA Ops:
  1.8 5.5 %collective-permute-start.2 = (bf16[16,128]{1,0:T(8,128)(2,1)S(1)}, bf16[16,128]{1,0:T(8,128)(2,1)S(1)}, u32[]{:S(2)}, u32[]{:S(2)}) collective-permute-start(bf16[16,128]{1,0:T(8,128)(2,1)S(1)} %get-tuple-element.35.rim_ref), channel_id=1, source_target_pairs={{0,4},{1,2},{2,1},{3,7},{4,0},{5,6},{6,5},{7,3},{8,12},{9,10},{10,... | collective-permute-start | bytes 12296 | tf_op jit(solution)/shard_map/ppermute | solution.py:39
  1.9 5.4 %collective-permute-start.3 = (bf16[16,128]{1,0:T(8,128)(2,1)S(1)}, bf16[16,128]{1,0:T(8,128)(2,1)S(1)}, u32[]{:S(2)}, u32[]{:S(2)}) collective-permute-start(bf16[16,128]{1,0:T(8,128)(2,1)S(1)} %get-tuple-element.35.rim_ref), channel_id=1, source_target_pairs={{0,1},{1,0},{2,3},{3,2},{4,5},{5,4},{6,7},{7,6},{8,9},{9,8},{10,11... | collective-permute-start | bytes 12296 | tf_op jit(solution)/shard_map/ppermute | solution.py:39
  4.8 5.7 %collective-permute-start = (bf16[96,512]{1,0:T(8,128)(2,1)S(1)}, bf16[96,512]{1,0:T(8,128)(2,1)S(1)}, u32[]{:S(2)}, u32[]{:S(2)}) collective-permute-start(bf16[96,512]{1,0:T(8,128)(2,1)S(1)} %get-tuple-element.31.a_ref.feat_ref), channel_id=1, source_target_pairs={{0,4},{1,2},{2,1},{3,7},{4,0},{5,6},{6,5},{7,3},{8,12},{9,10},{10,... | collective-permute-start | bytes 294920 | tf_op jit(solution)/shard_map/ppermute | solution.py:39
  6.0 4.5 %collective-permute-start.1 = (bf16[96,512]{1,0:T(8,128)(2,1)S(1)}, bf16[96,512]{1,0:T(8,128)(2,1)S(1)}, u32[]{:S(2)}, u32[]{:S(2)}) collective-permute-start(bf16[96,512]{1,0:T(8,128)(2,1)S(1)} %get-tuple-element.31.a_ref.feat_ref), channel_id=1, source_target_pairs={{0,1},{1,0},{2,3},{3,2},{4,5},{5,4},{6,7},{7,6},{8,9},{9,8},{10,11... | collective-permute-start | bytes 294920 | tf_op jit(solution)/shard_map/ppermute | solution.py:39
  7.3 2.7 %collective-permute-start.4 = (bf16[144,128]{1,0:T(8,128)(2,1)S(1)}, bf16[144,128]{1,0:T(8,128)(2,1)S(1)}, u32[]{:S(2)}, u32[]{:S(2)}) collective-permute-start(bf16[144,128]{1,0:T(8,128)(2,1)S(1)} %get-tuple-element.39), channel_id=1, source_target_pairs={{0,4},{1,5},{2,6},{3,7},{4,0},{5,1},{6,2},{7,3},{8,12},{9,13},{10,... | collective-permute-start | bytes 110600 | tf_op jit(solution)/shard_map/ppermute | solution.py:39
  8.3 5.0 %collective-permute-start.6 = (bf16[144,128]{1,0:T(8,128)(2,1)S(1)}, bf16[144,128]{1,0:T(8,128)(2,1)S(1)}, u32[]{:S(2)}, u32[]{:S(2)}) collective-permute-start(bf16[144,128]{1,0:T(8,128)(2,1)S(1)} %get-tuple-element.44), channel_id=1, source_target_pairs={{0,1},{1,0},{2,3},{3,2},{4,8},{5,9},{6,10},{7,11},{8,4},{9,5},{10,... | collective-permute-start | bytes 110600 | tf_op jit(solution)/shard_map/ppermute | solution.py:39
  10.6 4.8 %collective-permute-start.9 = (bf16[288,512]{1,0:T(8,128)(2,1)S(1)}, bf16[288,512]{1,0:T(8,128)(2,1)S(1)}, u32[]{:S(2)}, u32[]{:S(2)}) collective-permute-start(bf16[288,512]{1,0:T(8,128)(2,1)S(1)} %stack_features.1.after_ref.feat_ref), channel_id=1, source_target_pairs={{0,4},{1,5},{2,6},{3,7},{4,0},{5,1},{6,2},{7,3},{8,12},{9,13},{10,... | collective-permute-start | bytes 884744 | tf_op jit(solution)/shard_map/ppermute | solution.py:39
  11.3 9.0 %collective-permute-start.5 = (bf16[288,512]{1,0:T(8,128)(2,1)S(1)}, bf16[288,512]{1,0:T(8,128)(2,1)S(1)}, u32[]{:S(2)}, u32[]{:S(2)}) collective-permute-start(bf16[288,512]{1,0:T(8,128)(2,1)S(1)} %stack_features.1.after_ref.feat_ref), channel_id=1, source_target_pairs={{0,1},{1,0},{2,3},{3,2},{4,8},{5,9},{6,10},{7,11},{8,4},{9,5},{10,... | collective-permute-start | bytes 884744 | tf_op jit(solution)/shard_map/ppermute | solution.py:39
  13.8 2.7 %collective-permute-start.7 = (bf16[16,128]{1,0:T(8,128)(2,1)S(1)}, bf16[16,128]{1,0:T(8,128)(2,1)S(1)}, u32[]{:S(2)}, u32[]{:S(2)}) collective-permute-start(bf16[16,128]{1,0:T(8,128)(2,1)S(1)} %get-tuple-element.46.refs_0_.own_ref), channel_id=1, source_target_pairs={{0,4},{1,2},{2,1},{3,7},{4,0},{5,6},{6,5},{7,3},{8,12},{9,10},{10,... | collective-permute-start | bytes 12296 | tf_op jit(solution)/shard_map/ppermute | solution.py:39
  13.8 2.9 %collective-permute-start.8 = (bf16[16,128]{1,0:T(8,128)(2,1)S(1)}, bf16[16,128]{1,0:T(8,128)(2,1)S(1)}, u32[]{:S(2)}, u32[]{:S(2)}) collective-permute-start(bf16[16,128]{1,0:T(8,128)(2,1)S(1)} %get-tuple-element.46.refs_0_.own_ref), channel_id=1, source_target_pairs={{0,1},{1,0},{2,3},{3,2},{4,5},{5,4},{6,7},{7,6},{8,9},{9,8},{10,11... | collective-permute-start | bytes 12296 | tf_op jit(solution)/shard_map/ppermute | solution.py:39
  16.5 2.7 %copy-start = (bf16[4,12,128,128]{3,2,1,0:T(8,128)(2,1)S(1)}, bf16[4,12,128,128]{3,2,1,0:T(8,128)(2,1)}, u32[]{:S(2)}) copy-start(bf16[4,12,128,128]{3,2,1,0:T(8,128)(2,1)} %pip_ref.3) | copy-start | bytes 4718596
  16.8 2.4 %collective-permute-start.10 = (bf16[16,128]{1,0:T(8,128)(2,1)S(1)}, bf16[16,128]{1,0:T(8,128)(2,1)S(1)}, u32[]{:S(2)}, u32[]{:S(2)}) collective-permute-start(bf16[16,128]{1,0:T(8,128)(2,1)S(1)} %get-tuple-element.49.w_own_ref.after_ref), channel_id=1, source_target_pairs={{0,4},{1,5},{2,6},{3,7},{4,0},{5,1},{6,2},{7,3},{8,12},{9,13},{10,... | collective-permute-start | bytes 12296 | tf_op jit(solution)/shard_map/ppermute | solution.py:39
  18.3 3.3 %collective-permute-start.11 = (bf16[16,128]{1,0:T(8,128)(2,1)S(1)}, bf16[16,128]{1,0:T(8,128)(2,1)S(1)}, u32[]{:S(2)}, u32[]{:S(2)}) collective-permute-start(bf16[16,128]{1,0:T(8,128)(2,1)S(1)} %get-tuple-element.49.w_own_ref.after_ref), channel_id=1, source_target_pairs={{0,1},{1,0},{2,3},{3,2},{4,8},{5,9},{6,10},{7,11},{8,4},{9,5},{10,... | collective-permute-start | bytes 12296 | tf_op jit(solution)/shard_map/ppermute | solution.py:39

commit v7 on v6

--- a/solution.py
+++ b/solution.py
@@ -19,7 +19,7 @@
 ANY = pl.BlockSpec(memory_space=pl.ANY)
 HBM = pl.BlockSpec(memory_space=pltpu.HBM)
 
-COS = (0.99999922, -19.73898252, 64.92872662, -85.27239701, 58.79403871, -21.07678212)
+COS = (0.99995979, -19.73104169, 64.67343113, -82.40355036, 45.64655658)
 SIN = (6.2830558, -41.33121431, 81.36681529, -74.47800454, 32.7814008)
 
 
@@ -331,7 +331,7 @@
     return c, s * r
 
 
-def basis_kernel(first, tiles, nblk, freq_ref, feat_ref, out_ref, ft_ref, wide_ref=None):
+def basis_kernel(first, tiles, nblk, freq_ref, feat_ref, out_ref, ft_ref):
     feats, nfreq = freq_ref.shape
     blk = out_ref.shape[2]
     ft_ref[...] = freq_ref[...].astype(F32).T.astype(BF16)
@@ -339,9 +339,6 @@
     def work(t):
         for b in range(nblk):
             c, s = sincos(dot(ft_ref[...], feat_ref[t * feats : (t + 1) * feats, b * blk : (b + 1) * blk], 1, 0))
-            if wide_ref is not None:
-                wide_ref[b, 0:nfreq, :] = c
-                wide_ref[b, nfreq:, :] = s
             out_ref[first + t * nblk + b, 0:nfreq, :] = c.astype(BF16)
             out_ref[first + t * nblk + b, nfreq:, :] = s.astype(BF16)
 
@@ -358,9 +355,9 @@
         inside()
 
 
-def own_basis_kernel(nblk, src_ref, count_ref, freq_ref, feat_ref, after_ref, out_ref, wide_ref, code_ref, ft_ref, tile_ref):
+def own_basis_kernel(nblk, src_ref, count_ref, freq_ref, feat_ref, after_ref, out_ref, code_ref, ft_ref, tile_ref):
     list_slots(nblk, src_ref, count_ref, code_ref, tile_ref)
-    basis_kernel(0, (0,), nblk, freq_ref, feat_ref, out_ref, ft_ref, wide_ref)
+    basis_kernel(0, (0,), nblk, freq_ref, feat_ref, out_ref, ft_ref)
 
 
 def pair_sums(code_ref, pip_ref, basis_ref, w_ref, at, a):
@@ -392,7 +389,7 @@
         sum_ref[a] = total
 
 
-def pair_kernel(code_ref, pip_ref, basis_ref, own_ref, early_ref, w_own_ref, w_even_ref, w_odd_ref, out_ref, w_ref, sum_ref, done_ref, sems):
+def pair_kernel(code_ref, pip_ref, basis_ref, early_ref, w_own_ref, w_even_ref, w_odd_ref, out_ref, w_ref, sum_ref, done_ref, sems):
     nblk, slots, blk, _ = pip_ref.shape
     nfreq = out_ref.shape[0]
     half, steps = nblk * FIRST, (slots - FIRST) // 2
@@ -405,14 +402,15 @@
             total = start_ref[a]
             for t in range(count):
                 total = total + pair_sums(code_ref, pip_ref, basis_ref, w_ref, half + a * slots + 2 * t, a)
-            folded = own_ref[a, 0:nfreq] * total[:nfreq] + own_ref[a, nfreq:] * total[nfreq:]
+            own = basis_ref[a].astype(F32)
+            folded = own[:nfreq] * total[:nfreq] + own[nfreq:] * total[nfreq:]
             done_ref[a] = (folded * w_ref[a : a + 1, :]).astype(BF16)
             copies.append(pltpu.make_async_copy(done_ref.at[a], out_ref.at[:, a * blk : (a + 1) * blk], sems.at[a]))
             copies[-1].start()
         for copy in copies:
             copy.wait()
 
-    @pl.when(many > steps)
+    @pl.when(many > steps + 1)
     def _():
         sum_ref[...] = early_ref[...]
 
@@ -424,9 +422,8 @@
         lax.fori_loop(steps, many, step, 0)
         finish(sum_ref, steps)
 
-    pl.when(many == steps)(lambda: finish(early_ref, steps))
-    pl.when(jnp.logical_and(many > 0, many < steps))(lambda: finish(early_ref, steps - 1))
-    pl.when(many == 0)(lambda: finish(early_ref, 0))
+    for count in range(steps + 2):
+        pl.when(many == count)(functools.partial(finish, early_ref, count))
 
 
 def vm(shape, dtype):
@@ -485,12 +482,13 @@
         [pltpu.VMEM((n, ny), F32)], "even_side",
     )
     column = call(stack_rows_kernel, vm((3 * feats, galaxies), BF16), (features, f_odd, f_even), (even_side,), name="stack_features")
-    c_odd, c_even = exchange("ra", column, column)
+    c_even = swap("ra", 0, column)
+    c_odd = swap("ra", 1, column)
 
     blocks = vm((9 * nblk, 2 * nfreq, blk), BF16)
     scratch = [pltpu.VMEM((nfreq, feats), BF16)]
-    table, own_wide, code = call(
-        functools.partial(own_basis_kernel, nblk), (blocks, vm((nblk, 2 * nfreq, blk), F32), sm((nblk * (FIRST + slots) + 2,))), (frequencies, features), (column,),
+    table, code = call(
+        functools.partial(own_basis_kernel, nblk), (blocks, sm((nblk * (FIRST + slots) + 2,))), (frequencies, features), (column,),
         scratch + [pltpu.SMEM((9,), jnp.int32)], "own_basis", scalars=(pair_src, pair_count),
     )
 
@@ -519,13 +517,13 @@
     )
     table = basis(2, (0, 1, 2), c_odd, table, early)
     return pl.pallas_call(
-        pair_kernel, out_shape=jax.ShapeDtypeStruct((nfreq, galaxies), BF16), in_specs=[SMEM] + [VMEM] * 7, out_specs=ANY,
+        pair_kernel, out_shape=jax.ShapeDtypeStruct((nfreq, galaxies), BF16), in_specs=[SMEM] + [VMEM] * 6, out_specs=ANY,
         scratch_shapes=[
             pltpu.VMEM((9 * nblk + 4, blk), F32), pltpu.VMEM((nblk, 2 * nfreq, blk), F32),
             pltpu.VMEM((nblk, nfreq, blk), BF16), pltpu.SemaphoreType.DMA((nblk,)),
         ],
         compiler_params=params(), name="pairs",
-    )(code, pip, table, own_wide, early, w_column, x_even, x_odd)
+    )(code, pip, table, early, w_column, x_even, x_odd)
 
 
 def solution(mesh):

time: 23.2 us -> 23.2 us (level)
  waiting for transfers between devices: 0.53 us -> 0.89 us
  Pallas kernels: 9.4 us -> 9.05 us
    pallas_call x13, Pallas kernels: 6.7 us -> 6.34 us  [call(): pl.pallas_call(body, out_shape=out, in_specs=[SMEM] * len(scalars) + [VME...]
    ppermute x12, waiting for transfers between devices: 0.53 us -> 0.89 us  [swap(): lax.ppermute(payload, ('ra', 'dec'), sorted(pairs + [(b, a) for a, b in p...]
  transfers between devices with their start and end apart: 12 -> 12, of which waited for: 2 -> 4; matrix products, arithmetic and copies ran while one was open for 0% -> 0% of each run, Pallas kernels for 27% -> 25%
where the time goes in v7:
time: 23.2 us; the launch traced here: 23 us
  starting transfers between devices  12.9 us (56%)
  Pallas kernels  9.05 us (39%)
  waiting for transfers between devices  0.89 us (4%)
    ppermute x12, starting transfers between devices, swap(): lax.ppermute(payload, ('ra', 'dec'), sorted(pairs + [(b, a) for a, b in p...  12.9 us
    pallas_call x13, Pallas kernels, call(): pl.pallas_call(body, out_shape=out, in_specs=[SMEM] * len(scalars) + [VME...  6.34 us
    pallas_call x1, Pallas kernels, per_device(): pl.pallas_call(pair_kernel, out_shape=jax.ShapeDtypeStruct((nfreq, galaxi...  1.46 us
    pallas_call x1, Pallas kernels, per_device(): pl.pallas_call(rim_kernel, out_shape=(vm((RIM, 128), BF16), vm((n, ny), F...  1.25 us
    ppermute x12, waiting for transfers between devices, swap(): lax.ppermute(payload, ('ra', 'dec'), sorted(pairs + [(b, a) for a, b in p...  0.89 us
  transfers between devices with their start and end apart: 12, of which 4 were waited for; matrix products, arithmetic and copies ran while one was open for 0% of the time, Pallas kernels for 25%

profile of v7, /device:TPU:1, one launch (start us, length us, event | category | flops | bytes accessed | tf_op | source)
XLA Modules:
  0.0 23.0 jit_solution(8157026931002952273)
XLA Ops:
  0.0 1.3 %rim.1 = (bf16[16,128]{1,0:T(8,128)(2,1)S(1)}, f32[512,128]{1,0:T(8,128)S(1)}, bf16[512,512]{1,0:T(8,128)(2,1)S(1)}, s32[1,512]{1,0:T(1,128)S(1)}, f32[25,64]{1,...) custom-call(f32[64,8,128]{2,1,0:T(8,128)} %refs_0_.1, ...), custom_call_target="tpu_custom_call" | custom-call | tf_op jit(solution)/shard_map/rim/pallas_call | solution.py:456
  1.3 0.5 %ahead.1 = (bf16[16,128]{1,0:T(8,128)(2,1)S(1)}, f32[1600,128]{1,0:T(8,128)S(1)}, f32[80,512]{1,0:T(8,128)S(1)}) custom-call(bf16[16,128]{1,0:T(8,128)(2,1)S(1)} %get-tuple-element.33.rim_in_ref, f32[25,64]{1,0:T(8,128)S(1)} %get-tuple-element.32.stencil_ref), custom_call_target="tpu_custom_call" | custom-call | flops 1 | bytes 1 | tf_op jit(solution)/shard_map/ahead/pallas_call | solution.py:446
  1.8 0.1 collective-permute-start.2
  1.9 2.9 %collective-permute-start.3 = (bf16[16,128]{1,0:T(8,128)(2,1)S(1)}, bf16[16,128]{1,0:T(8,128)(2,1)S(1)}, u32[]{:S(2)}, u32[]{:S(2)}) collective-permute-start(bf16[16,128]{1,0:T(8,128)(2,1)S(1)} %get-tuple-element.34.rim_ref), channel_id=1, source_target_pairs={{0,1},{1,0},{2,3},{3,2},{4,5},{5,4},{6,7},{7,6},{8,9},{9,8},{10,11... | collective-permute-start | bytes 12296 | tf_op jit(solution)/shard_map/ppermute | solution.py:39
  4.8 1.2 %collective-permute-start = (bf16[96,512]{1,0:T(8,128)(2,1)S(1)}, bf16[96,512]{1,0:T(8,128)(2,1)S(1)}, u32[]{:S(2)}, u32[]{:S(2)}) collective-permute-start(bf16[96,512]{1,0:T(8,128)(2,1)S(1)} %get-tuple-element.30.a_ref.feat_ref), channel_id=1, source_target_pairs={{0,4},{1,2},{2,1},{3,7},{4,0},{5,6},{6,5},{7,3},{8,12},{9,10},{10,... | collective-permute-start | bytes 294920 | tf_op jit(solution)/shard_map/ppermute | solution.py:39
  6.0 0.8 %collective-permute-start.1 = (bf16[96,512]{1,0:T(8,128)(2,1)S(1)}, bf16[96,512]{1,0:T(8,128)(2,1)S(1)}, u32[]{:S(2)}, u32[]{:S(2)}) collective-permute-start(bf16[96,512]{1,0:T(8,128)(2,1)S(1)} %get-tuple-element.30.a_ref.feat_ref), channel_id=1, source_target_pairs={{0,1},{1,0},{2,3},{3,2},{4,5},{5,4},{6,7},{7,6},{8,9},{9,8},{10,11... | collective-permute-start | bytes 294920 | tf_op jit(solution)/shard_map/ppermute | solution.py:39
  6.8 0.5 %inner.1.after_ref.inner_ref = f32[512,128]{1,0:T(8,128)S(1)} custom-call(f32[512,128]{1,0:T(8,128)S(1)} %get-tuple-element.31.rows_ref, f32[1600,128]{1,0:T(8,128)S(1)} %get-tuple-element.37.taps_ref), custom_call_target="tpu_custom_call" | custom-call | flops 1 | bytes 1 | tf_op jit(solution)/shard_map/inner/pallas_call | solution.py:446
  7.3 0.0 collective-permute-done.2.odd_ref
  7.3 0.0 collective-permute-done.3.even_ref
  7.3 1.0 %collective-permute-start.4 = (bf16[144,128]{1,0:T(8,128)(2,1)S(1)}, bf16[144,128]{1,0:T(8,128)(2,1)S(1)}, u32[]{:S(2)}, u32[]{:S(2)}) collective-permute-start(bf16[144,128]{1,0:T(8,128)(2,1)S(1)} %get-tuple-element.38), channel_id=1, source_target_pairs={{0,4},{1,5},{2,6},{3,7},{4,0},{5,1},{6,2},{7,3},{8,12},{9,13},{10,... | collective-permute-start | bytes 110600 | tf_op jit(solution)/shard_map/ppermute | solution.py:39
  8.3 1.7 %collective-permute-start.6 = (bf16[144,128]{1,0:T(8,128)(2,1)S(1)}, bf16[144,128]{1,0:T(8,128)(2,1)S(1)}, u32[]{:S(2)}, u32[]{:S(2)}) collective-permute-start(bf16[144,128]{1,0:T(8,128)(2,1)S(1)} %get-tuple-element.43), channel_id=1, source_target_pairs={{0,1},{1,0},{2,3},{3,2},{4,8},{5,9},{6,10},{7,11},{8,4},{9,5},{10,... | collective-permute-start | bytes 110600 | tf_op jit(solution)/shard_map/ppermute | solution.py:39
  10.0 0.0 collective-permute-done.4.rows_ref
  10.0 0.5 %even_side.1.after_ref.even_side_ref = f32[8,512]{1,0:T(8,128)S(1)} custom-call(f32[512,128]{1,0:T(8,128)S(1)} %inner.1.after_ref.inner_ref, bf16[16,128]{1,0:T(8,128)(2,1)S(1)} %collective-permute-done.2.odd_ref, bf16[16,128]{1,0:T(8,128)(2,1)S(1)} %collective-permute-done.3.even_ref, bf16[144,128]{1,0:T(8,128)(2,1)S(1)} %collective-permute-done.4.rows_ref, ...), custom_call_target="tpu_custom_call" | custom-call | flops 1 | bytes 1 | tf_op jit(solution)/shard_map/even_side/pallas_call | solution.py:446
  10.5 0.0 collective-permute-done.b_ref
  10.5 0.0 collective-permute-done.1.c_ref
  10.6 0.8 %collective-permute-start.9 = (bf16[288,512]{1,0:T(8,128)(2,1)S(1)}, bf16[288,512]{1,0:T(8,128)(2,1)S(1)}, u32[]{:S(2)}, u32[]{:S(2)}) collective-permute-start(bf16[288,512]{1,0:T(8,128)(2,1)S(1)} %stack_features.1.after_ref.feat_ref), channel_id=1, source_target_pairs={{0,4},{1,5},{2,6},{3,7},{4,0},{5,1},{6,2},{7,3},{8,12},{9,13},{10,... | collective-permute-start | bytes 884744 | tf_op jit(solution)/shard_map/ppermute | solution.py:39
  11.3 1.2 %collective-permute-start.5 = (bf16[288,512]{1,0:T(8,128)(2,1)S(1)}, bf16[288,512]{1,0:T(8,128)(2,1)S(1)}, u32[]{:S(2)}, u32[]{:S(2)}) collective-permute-start(bf16[288,512]{1,0:T(8,128)(2,1)S(1)} %stack_features.1.after_ref.feat_ref), channel_id=1, source_target_pairs={{0,1},{1,0},{2,3},{3,2},{4,8},{5,9},{6,10},{7,11},{8,4},{9,5},{10,... | collective-permute-start | bytes 884744 | tf_op jit(solution)/shard_map/ppermute | solution.py:39
  12.5 0.6 %own_basis.1 = (bf16[36,512,128]{2,1,0:T(8,128)(2,1)S(1)}, s32[74]{0:T(128)S(4)}) custom-call(s32[4,12]{1,0:T(4,128)S(4)} %get-tuple-element.27.src_ref, s32[4]{0:T(128)S(4)} %get-tuple-element.28.count_ref, bf16[96,256]{1,0:T(8,128)(2,1)S(1)} %get-tuple-element.29.freq_ref, bf16[96,512]{1,0:T(8,128)(2,1)S(1)} %get-tuple-element.30.a_ref.feat_ref, ...), custom_call_target="tpu_custom_call" | custom-call | flops 1 | bytes 1 | tf_op jit(solution)/shard_map/own_basis/pallas_call | solution.py:446
  13.1 0.0 collective-permute-done.6.rows_ref
  13.1 0.4 %weight.1 = (bf16[16,128]{1,0:T(8,128)(2,1)S(1)}, bf16[36,512,128]{2,1,0:T(8,128)(2,1)S(1)}) custom-call(f32[8,512]{1,0:T(8,128)S(1)} %even_side.1.after_ref.even_side_ref, bf16[144,128]{1,0:T(8,128)(2,1)S(1)} %collective-permute-done.6.rows_ref, f32[1600,128]{1,0:T(8,128)S(1)} %get-tuple-element.37.taps_ref, ...), custom_call_target="tpu_custom_call", output_to_operand_aliasing={{1}: (6, {})} | custom-call | flops 68719476736 | bytes 1 | tf_op jit(solution)/shard_map/weight/pallas_call | solution.py:446
  13.6 0.1 collective-permute-start.7
  13.6 0.9 %collective-permute-start.8 = (bf16[16,128]{1,0:T(8,128)(2,1)S(1)}, bf16[16,128]{1,0:T(8,128)(2,1)S(1)}, u32[]{:S(2)}, u32[]{:S(2)}) collective-permute-start(bf16[16,128]{1,0:T(8,128)(2,1)S(1)} %get-tuple-element.45.refs_0_.own_ref), channel_id=1, source_target_pairs={{0,1},{1,0},{2,3},{3,2},{4,5},{5,4},{6,7},{7,6},{8,9},{9,8},{10,11... | collective-permute-start | bytes 12296 | tf_op jit(solution)/shard_map/ppermute | solution.py:39
  14.5 0.6 %basis0.1.refs_1_ = bf16[36,512,128]{2,1,0:T(8,128)(2,1)S(1)} custom-call(bf16[96,256]{1,0:T(8,128)(2,1)S(1)} %get-tuple-element.29.freq_ref, bf16[288,512]{1,0:T(8,128)(2,1)S(1)} %stack_features.1.after_ref.feat_ref, bf16[16,128]{1,0:T(8,128)(2,1)S(1)} %get-tuple-element.45.refs_0_.own_ref, ...), custom_call_target="tpu_custom_call", output_to_operand_aliasing={{}: (3, {})} | custom-call | flops 1 | bytes 1 | tf_op jit(solution)/shard_map/basis0/pallas_call | solution.py:446
  15.1 0.0 collective-permute-done.9.feat_ref
  15.1 1.0 %basis1.1.basis_in_ref = bf16[36,512,128]{2,1,0:T(8,128)(2,1)S(1)} custom-call(bf16[96,256]{1,0:T(8,128)(2,1)S(1)} %get-tuple-element.29.freq_ref, bf16[288,512]{1,0:T(8,128)(2,1)S(1)} %collective-permute-done.9.feat_ref, bf16[16,128]{1,0:T(8,128)(2,1)S(1)} %get-tuple-element.45.refs_0_.own_ref, ...), custom_call_target="tpu_custom_call", output_to_operand_aliasing={{}: (3, {})} | custom-call | flops 1 | bytes 1 | tf_op jit(solution)/shard_map/basis1/pallas_call | solution.py:446
  16.2 0.0 copy-start
  16.2 0.0 collective-permute-done.7.odd_ref
  16.2 0.4 %collective-permute-done.8.even_ref = bf16[16,128]{1,0:T(8,128)(2,1)S(1)} collective-permute-done((bf16[16,128]{1,0:T(8,128)(2,1)S(1)}, bf16[16,128]{1,0:T(8,128)(2,1)S(1)}, u32[]{:S(2)}, u32[]{:S(2)}) %collective-permute-start.8) | collective-permute-done | bytes 4128 | tf_op jit(solution)/shard_map/ppermute | solution.py:39
  16.6 1.7 %collective-permute-start.10 = (bf16[16,128]{1,0:T(8,128)(2,1)S(1)}, bf16[16,128]{1,0:T(8,128)(2,1)S(1)}, u32[]{:S(2)}, u32[]{:S(2)}) collective-permute-start(bf16[16,128]{1,0:T(8,128)(2,1)S(1)} %get-tuple-element.48.w_own_ref.after_ref), channel_id=1, source_target_pairs={{0,4},{1,5},{2,6},{3,7},{4,0},{5,1},{6,2},{7,3},{8,12},{9,13},{10,... | collective-permute-start | bytes 12296 | tf_op jit(solution)/shard_map/ppermute | solution.py:39
  18.3 0.7 %collective-permute-start.11 = (bf16[16,128]{1,0:T(8,128)(2,1)S(1)}, bf16[16,128]{1,0:T(8,128)(2,1)S(1)}, u32[]{:S(2)}, u32[]{:S(2)}) collective-permute-start(bf16[16,128]{1,0:T(8,128)(2,1)S(1)} %get-tuple-element.48.w_own_ref.after_ref), channel_id=1, source_target_pairs={{0,1},{1,0},{2,3},{3,2},{4,8},{5,9},{6,10},{7,11},{8,4},{9,5},{10,... | collective-permute-start | bytes 12296 | tf_op jit(solution)/shard_map/ppermute | solution.py:39
  19.0 0.1 collective-permute-done.10.w_even_ref
  19.1 0.0 copy-done
  19.1 1.0 %early_pairs.1.refs_0_.early_ref = f32[4,512,128]{2,1,0:T(8,128)S(1)} custom-call(s32[74]{0:T(128)S(4)} %get-tuple-element.42.code_ref, bf16[4,12,128,128]{3,2,1,0:T(8,128)(2,1)S(1)} %copy-done, bf16[36,512,128]{2,1,0:T(8,128)(2,1)S(1)} %get-tuple-element.47.basis_ref.refs_1_, bf16[16,128]{1,0:T(8,128)(2,1)S(1)} %get-tuple-element.48.w_own_ref.after_ref, ...), custom_call_target="tpu_custom_call" | custom-call | flops 1 | bytes 1 | tf_op jit(solution)/shard_map/early_pairs/pallas_call | solution.py:446
  20.1 0.1 collective-permute-done.5.feat_ref
  20.3 1.1 %basis2.1.basis_ref = bf16[36,512,128]{2,1,0:T(8,128)(2,1)S(1)} custom-call(bf16[96,256]{1,0:T(8,128)(2,1)S(1)} %get-tuple-element.29.freq_ref, bf16[288,512]{1,0:T(8,128)(2,1)S(1)} %collective-permute-done.5.feat_ref, f32[4,512,128]{2,1,0:T(8,128)S(1)} %early_pairs.1.refs_0_.early_ref, ...), custom_call_target="tpu_custom_call", output_to_operand_aliasing={{}: (3, {})} | custom-call | flops 1 | bytes 1 | tf_op jit(solution)/shard_map/basis2/pallas_call | solution.py:446
  21.3 0.2 %collective-permute-done.11.w_odd_ref = bf16[16,128]{1,0:T(8,128)(2,1)S(1)} collective-permute-done((bf16[16,128]{1,0:T(8,128)(2,1)S(1)}, bf16[16,128]{1,0:T(8,128)(2,1)S(1)}, u32[]{:S(2)}, u32[]{:S(2)}) %collective-permute-start.11) | collective-permute-done | bytes 4128 | tf_op jit(solution)/shard_map/ppermute | solution.py:39
  21.6 1.5 %pairs.1 = bf16[256,512]{1,0:T(8,128)(2,1)} custom-call(s32[74]{0:T(128)S(4)} %get-tuple-element.42.code_ref, bf16[4,12,128,128]{3,2,1,0:T(8,128)(2,1)S(1)} %copy-done, bf16[36,512,128]{2,1,0:T(8,128)(2,1)S(1)} %basis2.1.basis_ref, f32[4,512,128]{2,1,0:T(8,128)S(1)} %early_pairs.1.refs_0_.early_ref, ...), custom_call_target="tpu_custom_call" | custom-call | tf_op jit(solution)/shard_map/pairs/pallas_call | solution.py:519
  (4 shorter events, 0.1 us)
Async XLA Ops:
  1.8 5.5 %collective-permute-start.2 = (bf16[16,128]{1,0:T(8,128)(2,1)S(1)}, bf16[16,128]{1,0:T(8,128)(2,1)S(1)}, u32[]{:S(2)}, u32[]{:S(2)}) collective-permute-start(bf16[16,128]{1,0:T(8,128)(2,1)S(1)} %get-tuple-element.34.rim_ref), channel_id=1, source_target_pairs={{0,4},{1,2},{2,1},{3,7},{4,0},{5,6},{6,5},{7,3},{8,12},{9,10},{10,... | collective-permute-start | bytes 12296 | tf_op jit(solution)/shard_map/ppermute | solution.py:39
  1.9 5.4 %collective-permute-start.3 = (bf16[16,128]{1,0:T(8,128)(2,1)S(1)}, bf16[16,128]{1,0:T(8,128)(2,1)S(1)}, u32[]{:S(2)}, u32[]{:S(2)}) collective-permute-start(bf16[16,128]{1,0:T(8,128)(2,1)S(1)} %get-tuple-element.34.rim_ref), channel_id=1, source_target_pairs={{0,1},{1,0},{2,3},{3,2},{4,5},{5,4},{6,7},{7,6},{8,9},{9,8},{10,11... | collective-permute-start | bytes 12296 | tf_op jit(solution)/shard_map/ppermute | solution.py:39
  4.8 5.7 %collective-permute-start = (bf16[96,512]{1,0:T(8,128)(2,1)S(1)}, bf16[96,512]{1,0:T(8,128)(2,1)S(1)}, u32[]{:S(2)}, u32[]{:S(2)}) collective-permute-start(bf16[96,512]{1,0:T(8,128)(2,1)S(1)} %get-tuple-element.30.a_ref.feat_ref), channel_id=1, source_target_pairs={{0,4},{1,2},{2,1},{3,7},{4,0},{5,6},{6,5},{7,3},{8,12},{9,10},{10,... | collective-permute-start | bytes 294920 | tf_op jit(solution)/shard_map/ppermute | solution.py:39
  6.0 4.5 %collective-permute-start.1 = (bf16[96,512]{1,0:T(8,128)(2,1)S(1)}, bf16[96,512]{1,0:T(8,128)(2,1)S(1)}, u32[]{:S(2)}, u32[]{:S(2)}) collective-permute-start(bf16[96,512]{1,0:T(8,128)(2,1)S(1)} %get-tuple-element.30.a_ref.feat_ref), channel_id=1, source_target_pairs={{0,1},{1,0},{2,3},{3,2},{4,5},{5,4},{6,7},{7,6},{8,9},{9,8},{10,11... | collective-permute-start | bytes 294920 | tf_op jit(solution)/shard_map/ppermute | solution.py:39
  7.3 2.7 %collective-permute-start.4 = (bf16[144,128]{1,0:T(8,128)(2,1)S(1)}, bf16[144,128]{1,0:T(8,128)(2,1)S(1)}, u32[]{:S(2)}, u32[]{:S(2)}) collective-permute-start(bf16[144,128]{1,0:T(8,128)(2,1)S(1)} %get-tuple-element.38), channel_id=1, source_target_pairs={{0,4},{1,5},{2,6},{3,7},{4,0},{5,1},{6,2},{7,3},{8,12},{9,13},{10,... | collective-permute-start | bytes 110600 | tf_op jit(solution)/shard_map/ppermute | solution.py:39
  8.3 4.8 %collective-permute-start.6 = (bf16[144,128]{1,0:T(8,128)(2,1)S(1)}, bf16[144,128]{1,0:T(8,128)(2,1)S(1)}, u32[]{:S(2)}, u32[]{:S(2)}) collective-permute-start(bf16[144,128]{1,0:T(8,128)(2,1)S(1)} %get-tuple-element.43), channel_id=1, source_target_pairs={{0,1},{1,0},{2,3},{3,2},{4,8},{5,9},{6,10},{7,11},{8,4},{9,5},{10,... | collective-permute-start | bytes 110600 | tf_op jit(solution)/shard_map/ppermute | solution.py:39
  10.6 4.6 %collective-permute-start.9 = (bf16[288,512]{1,0:T(8,128)(2,1)S(1)}, bf16[288,512]{1,0:T(8,128)(2,1)S(1)}, u32[]{:S(2)}, u32[]{:S(2)}) collective-permute-start(bf16[288,512]{1,0:T(8,128)(2,1)S(1)} %stack_features.1.after_ref.feat_ref), channel_id=1, source_target_pairs={{0,4},{1,5},{2,6},{3,7},{4,0},{5,1},{6,2},{7,3},{8,12},{9,13},{10,... | collective-permute-start | bytes 884744 | tf_op jit(solution)/shard_map/ppermute | solution.py:39
  11.3 9.0 %collective-permute-start.5 = (bf16[288,512]{1,0:T(8,128)(2,1)S(1)}, bf16[288,512]{1,0:T(8,128)(2,1)S(1)}, u32[]{:S(2)}, u32[]{:S(2)}) collective-permute-start(bf16[288,512]{1,0:T(8,128)(2,1)S(1)} %stack_features.1.after_ref.feat_ref), channel_id=1, source_target_pairs={{0,1},{1,0},{2,3},{3,2},{4,8},{5,9},{6,10},{7,11},{8,4},{9,5},{10,... | collective-permute-start | bytes 884744 | tf_op jit(solution)/shard_map/ppermute | solution.py:39
  13.6 2.6 %collective-permute-start.7 = (bf16[16,128]{1,0:T(8,128)(2,1)S(1)}, bf16[16,128]{1,0:T(8,128)(2,1)S(1)}, u32[]{:S(2)}, u32[]{:S(2)}) collective-permute-start(bf16[16,128]{1,0:T(8,128)(2,1)S(1)} %get-tuple-element.45.refs_0_.own_ref), channel_id=1, source_target_pairs={{0,4},{1,2},{2,1},{3,7},{4,0},{5,6},{6,5},{7,3},{8,12},{9,10},{10,... | collective-permute-start | bytes 12296 | tf_op jit(solution)/shard_map/ppermute | solution.py:39
  13.6 2.9 %collective-permute-start.8 = (bf16[16,128]{1,0:T(8,128)(2,1)S(1)}, bf16[16,128]{1,0:T(8,128)(2,1)S(1)}, u32[]{:S(2)}, u32[]{:S(2)}) collective-permute-start(bf16[16,128]{1,0:T(8,128)(2,1)S(1)} %get-tuple-element.45.refs_0_.own_ref), channel_id=1, source_target_pairs={{0,1},{1,0},{2,3},{3,2},{4,5},{5,4},{6,7},{7,6},{8,9},{9,8},{10,11... | collective-permute-start | bytes 12296 | tf_op jit(solution)/shard_map/ppermute | solution.py:39
  16.2 2.9 %copy-start = (bf16[4,12,128,128]{3,2,1,0:T(8,128)(2,1)S(1)}, bf16[4,12,128,128]{3,2,1,0:T(8,128)(2,1)}, u32[]{:S(2)}) copy-start(bf16[4,12,128,128]{3,2,1,0:T(8,128)(2,1)} %pip_ref.3) | copy-start | bytes 4718596
  16.6 2.5 %collective-permute-start.10 = (bf16[16,128]{1,0:T(8,128)(2,1)S(1)}, bf16[16,128]{1,0:T(8,128)(2,1)S(1)}, u32[]{:S(2)}, u32[]{:S(2)}) collective-permute-start(bf16[16,128]{1,0:T(8,128)(2,1)S(1)} %get-tuple-element.48.w_own_ref.after_ref), channel_id=1, source_target_pairs={{0,4},{1,5},{2,6},{3,7},{4,0},{5,1},{6,2},{7,3},{8,12},{9,13},{10,... | collective-permute-start | bytes 12296 | tf_op jit(solution)/shard_map/ppermute | solution.py:39
  18.3 3.3 %collective-permute-start.11 = (bf16[16,128]{1,0:T(8,128)(2,1)S(1)}, bf16[16,128]{1,0:T(8,128)(2,1)S(1)}, u32[]{:S(2)}, u32[]{:S(2)}) collective-permute-start(bf16[16,128]{1,0:T(8,128)(2,1)S(1)} %get-tuple-element.48.w_own_ref.after_ref), channel_id=1, source_target_pairs={{0,1},{1,0},{2,3},{3,2},{4,8},{5,9},{6,10},{7,11},{8,4},{9,5},{10,... | collective-permute-start | bytes 12296 | tf_op jit(solution)/shard_map/ppermute | solution.py:39

commit v8 on v7

--- a/solution.py
+++ b/solution.py
@@ -11,7 +11,7 @@
 BF16 = jnp.bfloat16
 F32 = jnp.float32
 LONG = 1 << 36
-FIRST = 6
+FIRST = 8
 RIM = 16
 
 VMEM = pl.BlockSpec(memory_space=pltpu.VMEM)
@@ -410,7 +410,7 @@
         for copy in copies:
             copy.wait()
 
-    @pl.when(many > steps + 1)
+    @pl.when(many > steps + 2)
     def _():
         sum_ref[...] = early_ref[...]
 
@@ -422,7 +422,7 @@
         lax.fori_loop(steps, many, step, 0)
         finish(sum_ref, steps)
 
-    for count in range(steps + 2):
+    for count in range(steps + 3):
         pl.when(many == count)(functools.partial(finish, early_ref, count))
 
 

time: 23.2 us -> 23.3 us (level)
  the two profiles are of different devices: /device:TPU:1 before, /device:TPU:3 now
where the time goes in v8:
time: 23.3 us
  starting transfers between devices  12.2 us (52%)
  Pallas kernels  10.1 us (43%)
  waiting for transfers between devices  0.79 us (3%)
    ppermute x12, starting transfers between devices, swap(): lax.ppermute(payload, ('ra', 'dec'), sorted(pairs + [(b, a) for a, b in p...  12.2 us
    pallas_call x13, Pallas kernels, call(): pl.pallas_call(body, out_shape=out, in_specs=[SMEM] * len(scalars) + [VME...  6.79 us
    pallas_call x1, Pallas kernels, per_device(): pl.pallas_call(pair_kernel, out_shape=jax.ShapeDtypeStruct((nfreq, galaxi...  2.08 us
    pallas_call x1, Pallas kernels, per_device(): pl.pallas_call(rim_kernel, out_shape=(vm((RIM, 128), BF16), vm((n, ny), F...  1.25 us
    ppermute x12, waiting for transfers between devices, swap(): lax.ppermute(payload, ('ra', 'dec'), sorted(pairs + [(b, a) for a, b in p...  0.79 us
  transfers between devices with their start and end apart: 12, of which 2 were waited for; matrix products, arithmetic and copies ran while one was open for 0% of the time, Pallas kernels for 29%

profile of v8, /device:TPU:3, one launch (start us, length us, event | category | flops | bytes accessed | tf_op | source)
XLA Modules:
  0.0 23.3 jit_solution(17409019070730894266)
XLA Ops:
  0.0 1.3 %rim.1 = (bf16[16,128]{1,0:T(8,128)(2,1)S(1)}, f32[512,128]{1,0:T(8,128)S(1)}, bf16[512,512]{1,0:T(8,128)(2,1)S(1)}, s32[1,512]{1,0:T(1,128)S(1)}, f32[25,64]{1,...) custom-call(f32[64,8,128]{2,1,0:T(8,128)} %refs_0_.1, ...), custom_call_target="tpu_custom_call" | custom-call | tf_op jit(solution)/shard_map/rim/pallas_call | solution.py:456
  1.3 0.7 %collective-permute-start.2 = (bf16[16,128]{1,0:T(8,128)(2,1)S(1)}, bf16[16,128]{1,0:T(8,128)(2,1)S(1)}, u32[]{:S(2)}, u32[]{:S(2)}) collective-permute-start(bf16[16,128]{1,0:T(8,128)(2,1)S(1)} %get-tuple-element.34.rim_ref), channel_id=1, source_target_pairs={{0,4},{1,2},{2,1},{3,7},{4,0},{5,6},{6,5},{7,3},{8,12},{9,10},{10,... | collective-permute-start | bytes 12296 | tf_op jit(solution)/shard_map/ppermute | solution.py:39
  2.0 1.9 %collective-permute-start.3 = (bf16[16,128]{1,0:T(8,128)(2,1)S(1)}, bf16[16,128]{1,0:T(8,128)(2,1)S(1)}, u32[]{:S(2)}, u32[]{:S(2)}) collective-permute-start(bf16[16,128]{1,0:T(8,128)(2,1)S(1)} %get-tuple-element.34.rim_ref), channel_id=1, source_target_pairs={{0,1},{1,0},{2,3},{3,2},{4,5},{5,4},{6,7},{7,6},{8,9},{9,8},{10,11... | collective-permute-start | bytes 12296 | tf_op jit(solution)/shard_map/ppermute | solution.py:39
  3.9 1.2 %collective-permute-start = (bf16[96,512]{1,0:T(8,128)(2,1)S(1)}, bf16[96,512]{1,0:T(8,128)(2,1)S(1)}, u32[]{:S(2)}, u32[]{:S(2)}) collective-permute-start(bf16[96,512]{1,0:T(8,128)(2,1)S(1)} %get-tuple-element.30.a_ref.feat_ref), channel_id=1, source_target_pairs={{0,4},{1,2},{2,1},{3,7},{4,0},{5,6},{6,5},{7,3},{8,12},{9,10},{10,... | collective-permute-start | bytes 294920 | tf_op jit(solution)/shard_map/ppermute | solution.py:39
  5.2 0.8 %collective-permute-start.1 = (bf16[96,512]{1,0:T(8,128)(2,1)S(1)}, bf16[96,512]{1,0:T(8,128)(2,1)S(1)}, u32[]{:S(2)}, u32[]{:S(2)}) collective-permute-start(bf16[96,512]{1,0:T(8,128)(2,1)S(1)} %get-tuple-element.30.a_ref.feat_ref), channel_id=1, source_target_pairs={{0,1},{1,0},{2,3},{3,2},{4,5},{5,4},{6,7},{7,6},{8,9},{9,8},{10,11... | collective-permute-start | bytes 294920 | tf_op jit(solution)/shard_map/ppermute | solution.py:39
  5.9 0.5 %ready.1 = (f32[1600,128]{1,0:T(8,128)S(1)}, f32[80,512]{1,0:T(8,128)S(1)}) custom-call(f32[25,64]{1,0:T(8,128)S(1)} %get-tuple-element.32.stencil_ref, bf16[16,128]{1,0:T(8,128)(2,1)S(1)} %get-tuple-element.34.rim_ref, f32[1600,128]{1,0:T(8,128)S(1)} %get-tuple-element.35.taps_in_ref, ...), custom_call_target="tpu_custom_call", output_to_operand_aliasing={{0}: (2, {}), {1}: (3, {})} | custom-call | flops 1 | bytes 1 | tf_op jit(solution)/shard_map/ready/pallas_call | solution.py:446
  6.4 0.5 %inner.1.after_ref.inner_ref = f32[512,128]{1,0:T(8,128)S(1)} custom-call(f32[512,128]{1,0:T(8,128)S(1)} %get-tuple-element.31.rows_ref, f32[1600,128]{1,0:T(8,128)S(1)} %get-tuple-element.37.taps_ref), custom_call_target="tpu_custom_call" | custom-call | flops 1 | bytes 1 | tf_op jit(solution)/shard_map/inner/pallas_call | solution.py:446
  6.9 0.0 collective-permute-done.2.odd_ref
  7.0 0.0 collective-permute-done.3.even_ref
  7.0 1.0 %collective-permute-start.4 = (bf16[144,128]{1,0:T(8,128)(2,1)S(1)}, bf16[144,128]{1,0:T(8,128)(2,1)S(1)}, u32[]{:S(2)}, u32[]{:S(2)}) collective-permute-start(bf16[144,128]{1,0:T(8,128)(2,1)S(1)} %get-tuple-element.38), channel_id=1, source_target_pairs={{0,4},{1,5},{2,6},{3,7},{4,0},{5,1},{6,2},{7,3},{8,12},{9,13},{10,... | collective-permute-start | bytes 110600 | tf_op jit(solution)/shard_map/ppermute | solution.py:39
  8.0 1.2 %collective-permute-start.6 = (bf16[144,128]{1,0:T(8,128)(2,1)S(1)}, bf16[144,128]{1,0:T(8,128)(2,1)S(1)}, u32[]{:S(2)}, u32[]{:S(2)}) collective-permute-start(bf16[144,128]{1,0:T(8,128)(2,1)S(1)} %get-tuple-element.43), channel_id=1, source_target_pairs={{0,1},{1,0},{2,3},{3,2},{4,8},{5,9},{6,10},{7,11},{8,4},{9,5},{10,... | collective-permute-start | bytes 110600 | tf_op jit(solution)/shard_map/ppermute | solution.py:39
  9.1 0.0 collective-permute-done.4.rows_ref
  9.1 0.5 %even_side.1.after_ref.even_side_ref = f32[8,512]{1,0:T(8,128)S(1)} custom-call(f32[512,128]{1,0:T(8,128)S(1)} %inner.1.after_ref.inner_ref, bf16[16,128]{1,0:T(8,128)(2,1)S(1)} %collective-permute-done.2.odd_ref, bf16[16,128]{1,0:T(8,128)(2,1)S(1)} %collective-permute-done.3.even_ref, bf16[144,128]{1,0:T(8,128)(2,1)S(1)} %collective-permute-done.4.rows_ref, ...), custom_call_target="tpu_custom_call" | custom-call | flops 1 | bytes 1 | tf_op jit(solution)/shard_map/even_side/pallas_call | solution.py:446
  9.7 0.0 collective-permute-done.b_ref
  9.7 0.0 collective-permute-done.1.c_ref
  9.7 0.7 %collective-permute-start.9 = (bf16[288,512]{1,0:T(8,128)(2,1)S(1)}, bf16[288,512]{1,0:T(8,128)(2,1)S(1)}, u32[]{:S(2)}, u32[]{:S(2)}) collective-permute-start(bf16[288,512]{1,0:T(8,128)(2,1)S(1)} %stack_features.1.after_ref.feat_ref), channel_id=1, source_target_pairs={{0,4},{1,5},{2,6},{3,7},{4,0},{5,1},{6,2},{7,3},{8,12},{9,13},{10,... | collective-permute-start | bytes 884744 | tf_op jit(solution)/shard_map/ppermute | solution.py:39
  10.5 1.2 %collective-permute-start.5 = (bf16[288,512]{1,0:T(8,128)(2,1)S(1)}, bf16[288,512]{1,0:T(8,128)(2,1)S(1)}, u32[]{:S(2)}, u32[]{:S(2)}) collective-permute-start(bf16[288,512]{1,0:T(8,128)(2,1)S(1)} %stack_features.1.after_ref.feat_ref), channel_id=1, source_target_pairs={{0,1},{1,0},{2,3},{3,2},{4,8},{5,9},{6,10},{7,11},{8,4},{9,5},{10,... | collective-permute-start | bytes 884744 | tf_op jit(solution)/shard_map/ppermute | solution.py:39
  11.7 0.8 %own_basis.1 = (bf16[36,512,128]{2,1,0:T(8,128)(2,1)S(1)}, s32[82]{0:T(128)S(4)}) custom-call(s32[4,12]{1,0:T(4,128)S(4)} %get-tuple-element.27.src_ref, s32[4]{0:T(128)S(4)} %get-tuple-element.28.count_ref, bf16[96,256]{1,0:T(8,128)(2,1)S(1)} %get-tuple-element.29.freq_ref, bf16[96,512]{1,0:T(8,128)(2,1)S(1)} %get-tuple-element.30.a_ref.feat_ref, ...), custom_call_target="tpu_custom_call" | custom-call | flops 1 | bytes 1 | tf_op jit(solution)/shard_map/own_basis/pallas_call | solution.py:446
  12.5 0.0 collective-permute-done.6.rows_ref
  12.5 0.4 %weight.1 = (bf16[16,128]{1,0:T(8,128)(2,1)S(1)}, bf16[36,512,128]{2,1,0:T(8,128)(2,1)S(1)}) custom-call(f32[8,512]{1,0:T(8,128)S(1)} %even_side.1.after_ref.even_side_ref, bf16[144,128]{1,0:T(8,128)(2,1)S(1)} %collective-permute-done.6.rows_ref, f32[1600,128]{1,0:T(8,128)S(1)} %get-tuple-element.37.taps_ref, ...), custom_call_target="tpu_custom_call", output_to_operand_aliasing={{1}: (6, {})} | custom-call | flops 68719476736 | bytes 1 | tf_op jit(solution)/shard_map/weight/pallas_call | solution.py:446
  12.9 0.1 collective-permute-start.7
  13.0 0.9 %collective-permute-start.8 = (bf16[16,128]{1,0:T(8,128)(2,1)S(1)}, bf16[16,128]{1,0:T(8,128)(2,1)S(1)}, u32[]{:S(2)}, u32[]{:S(2)}) collective-permute-start(bf16[16,128]{1,0:T(8,128)(2,1)S(1)} %get-tuple-element.45.refs_0_.own_ref), channel_id=1, source_target_pairs={{0,1},{1,0},{2,3},{3,2},{4,5},{5,4},{6,7},{7,6},{8,9},{9,8},{10,11... | collective-permute-start | bytes 12296 | tf_op jit(solution)/shard_map/ppermute | solution.py:39
  13.8 0.6 %basis0.1.refs_1_ = bf16[36,512,128]{2,1,0:T(8,128)(2,1)S(1)} custom-call(bf16[96,256]{1,0:T(8,128)(2,1)S(1)} %get-tuple-element.29.freq_ref, bf16[288,512]{1,0:T(8,128)(2,1)S(1)} %stack_features.1.after_ref.feat_ref, bf16[16,128]{1,0:T(8,128)(2,1)S(1)} %get-tuple-element.45.refs_0_.own_ref, ...), custom_call_target="tpu_custom_call", output_to_operand_aliasing={{}: (3, {})} | custom-call | flops 1 | bytes 1 | tf_op jit(solution)/shard_map/basis0/pallas_call | solution.py:446
  14.5 0.0 collective-permute-done.9.feat_ref
  14.5 1.0 %basis1.1.basis_in_ref = bf16[36,512,128]{2,1,0:T(8,128)(2,1)S(1)} custom-call(bf16[96,256]{1,0:T(8,128)(2,1)S(1)} %get-tuple-element.29.freq_ref, bf16[288,512]{1,0:T(8,128)(2,1)S(1)} %collective-permute-done.9.feat_ref, bf16[16,128]{1,0:T(8,128)(2,1)S(1)} %get-tuple-element.45.refs_0_.own_ref, ...), custom_call_target="tpu_custom_call", output_to_operand_aliasing={{}: (3, {})} | custom-call | flops 1 | bytes 1 | tf_op jit(solution)/shard_map/basis1/pallas_call | solution.py:446
  15.5 0.0 copy-start
  15.5 0.0 collective-permute-done.7.odd_ref
  15.5 0.3 %collective-permute-done.8.even_ref = bf16[16,128]{1,0:T(8,128)(2,1)S(1)} collective-permute-done((bf16[16,128]{1,0:T(8,128)(2,1)S(1)}, bf16[16,128]{1,0:T(8,128)(2,1)S(1)}, u32[]{:S(2)}, u32[]{:S(2)}) %collective-permute-start.8) | collective-permute-done | bytes 4128 | tf_op jit(solution)/shard_map/ppermute | solution.py:39
  15.8 1.4 %collective-permute-start.10 = (bf16[16,128]{1,0:T(8,128)(2,1)S(1)}, bf16[16,128]{1,0:T(8,128)(2,1)S(1)}, u32[]{:S(2)}, u32[]{:S(2)}) collective-permute-start(bf16[16,128]{1,0:T(8,128)(2,1)S(1)} %get-tuple-element.48.w_own_ref.after_ref), channel_id=1, source_target_pairs={{0,4},{1,5},{2,6},{3,7},{4,0},{5,1},{6,2},{7,3},{8,12},{9,13},{10,... | collective-permute-start | bytes 12296 | tf_op jit(solution)/shard_map/ppermute | solution.py:39
  17.2 1.2 %collective-permute-start.11 = (bf16[16,128]{1,0:T(8,128)(2,1)S(1)}, bf16[16,128]{1,0:T(8,128)(2,1)S(1)}, u32[]{:S(2)}, u32[]{:S(2)}) collective-permute-start(bf16[16,128]{1,0:T(8,128)(2,1)S(1)} %get-tuple-element.48.w_own_ref.after_ref), channel_id=1, source_target_pairs={{0,1},{1,0},{2,3},{3,2},{4,8},{5,9},{6,10},{7,11},{8,4},{9,5},{10,... | collective-permute-start | bytes 12296 | tf_op jit(solution)/shard_map/ppermute | solution.py:39
  18.3 0.0 collective-permute-done.10.w_even_ref
  18.4 0.0 copy-done
  18.4 1.3 %early_pairs.1.refs_0_.early_ref = f32[4,512,128]{2,1,0:T(8,128)S(1)} custom-call(s32[82]{0:T(128)S(4)} %get-tuple-element.42.code_ref, bf16[4,12,128,128]{3,2,1,0:T(8,128)(2,1)S(1)} %copy-done, bf16[36,512,128]{2,1,0:T(8,128)(2,1)S(1)} %get-tuple-element.47.basis_ref.refs_1_, bf16[16,128]{1,0:T(8,128)(2,1)S(1)} %get-tuple-element.48.w_own_ref.after_ref, ...), custom_call_target="tpu_custom_call" | custom-call | flops 1 | bytes 1 | tf_op jit(solution)/shard_map/early_pairs/pallas_call | solution.py:446
  19.6 0.5 %collective-permute-done.5.feat_ref = bf16[288,512]{1,0:T(8,128)(2,1)S(1)} collective-permute-done((bf16[288,512]{1,0:T(8,128)(2,1)S(1)}, bf16[288,512]{1,0:T(8,128)(2,1)S(1)}, u32[]{:S(2)}, u32[]{:S(2)}) %collective-permute-start.5) | collective-permute-done | bytes 294944 | tf_op jit(solution)/shard_map/ppermute | solution.py:39
  20.1 1.0 %basis2.1.basis_ref = bf16[36,512,128]{2,1,0:T(8,128)(2,1)S(1)} custom-call(bf16[96,256]{1,0:T(8,128)(2,1)S(1)} %get-tuple-element.29.freq_ref, bf16[288,512]{1,0:T(8,128)(2,1)S(1)} %collective-permute-done.5.feat_ref, f32[4,512,128]{2,1,0:T(8,128)S(1)} %early_pairs.1.refs_0_.early_ref, ...), custom_call_target="tpu_custom_call", output_to_operand_aliasing={{}: (3, {})} | custom-call | flops 1 | bytes 1 | tf_op jit(solution)/shard_map/basis2/pallas_call | solution.py:446
  21.2 0.0 collective-permute-done.11.w_odd_ref
  21.2 2.1 %pairs.1 = bf16[256,512]{1,0:T(8,128)(2,1)} custom-call(s32[82]{0:T(128)S(4)} %get-tuple-element.42.code_ref, bf16[4,12,128,128]{3,2,1,0:T(8,128)(2,1)S(1)} %copy-done, bf16[36,512,128]{2,1,0:T(8,128)(2,1)S(1)} %basis2.1.basis_ref, f32[4,512,128]{2,1,0:T(8,128)S(1)} %early_pairs.1.refs_0_.early_ref, ...), custom_call_target="tpu_custom_call" | custom-call | tf_op jit(solution)/shard_map/pairs/pallas_call | solution.py:519
  (4 shorter events, 0.1 us)
Async XLA Ops:
  1.3 5.7 %collective-permute-start.2 = (bf16[16,128]{1,0:T(8,128)(2,1)S(1)}, bf16[16,128]{1,0:T(8,128)(2,1)S(1)}, u32[]{:S(2)}, u32[]{:S(2)}) collective-permute-start(bf16[16,128]{1,0:T(8,128)(2,1)S(1)} %get-tuple-element.34.rim_ref), channel_id=1, source_target_pairs={{0,4},{1,2},{2,1},{3,7},{4,0},{5,6},{6,5},{7,3},{8,12},{9,10},{10,... | collective-permute-start | bytes 12296 | tf_op jit(solution)/shard_map/ppermute | solution.py:39
  2.0 4.9 %collective-permute-start.3 = (bf16[16,128]{1,0:T(8,128)(2,1)S(1)}, bf16[16,128]{1,0:T(8,128)(2,1)S(1)}, u32[]{:S(2)}, u32[]{:S(2)}) collective-permute-start(bf16[16,128]{1,0:T(8,128)(2,1)S(1)} %get-tuple-element.34.rim_ref), channel_id=1, source_target_pairs={{0,1},{1,0},{2,3},{3,2},{4,5},{5,4},{6,7},{7,6},{8,9},{9,8},{10,11... | collective-permute-start | bytes 12296 | tf_op jit(solution)/shard_map/ppermute | solution.py:39
  3.9 5.7 %collective-permute-start = (bf16[96,512]{1,0:T(8,128)(2,1)S(1)}, bf16[96,512]{1,0:T(8,128)(2,1)S(1)}, u32[]{:S(2)}, u32[]{:S(2)}) collective-permute-start(bf16[96,512]{1,0:T(8,128)(2,1)S(1)} %get-tuple-element.30.a_ref.feat_ref), channel_id=1, source_target_pairs={{0,4},{1,2},{2,1},{3,7},{4,0},{5,6},{6,5},{7,3},{8,12},{9,10},{10,... | collective-permute-start | bytes 294920 | tf_op jit(solution)/shard_map/ppermute | solution.py:39
  5.2 4.5 %collective-permute-start.1 = (bf16[96,512]{1,0:T(8,128)(2,1)S(1)}, bf16[96,512]{1,0:T(8,128)(2,1)S(1)}, u32[]{:S(2)}, u32[]{:S(2)}) collective-permute-start(bf16[96,512]{1,0:T(8,128)(2,1)S(1)} %get-tuple-element.30.a_ref.feat_ref), channel_id=1, source_target_pairs={{0,1},{1,0},{2,3},{3,2},{4,5},{5,4},{6,7},{7,6},{8,9},{9,8},{10,11... | collective-permute-start | bytes 294920 | tf_op jit(solution)/shard_map/ppermute | solution.py:39
  7.0 2.1 %collective-permute-start.4 = (bf16[144,128]{1,0:T(8,128)(2,1)S(1)}, bf16[144,128]{1,0:T(8,128)(2,1)S(1)}, u32[]{:S(2)}, u32[]{:S(2)}) collective-permute-start(bf16[144,128]{1,0:T(8,128)(2,1)S(1)} %get-tuple-element.38), channel_id=1, source_target_pairs={{0,4},{1,5},{2,6},{3,7},{4,0},{5,1},{6,2},{7,3},{8,12},{9,13},{10,... | collective-permute-start | bytes 110600 | tf_op jit(solution)/shard_map/ppermute | solution.py:39
  8.0 4.5 %collective-permute-start.6 = (bf16[144,128]{1,0:T(8,128)(2,1)S(1)}, bf16[144,128]{1,0:T(8,128)(2,1)S(1)}, u32[]{:S(2)}, u32[]{:S(2)}) collective-permute-start(bf16[144,128]{1,0:T(8,128)(2,1)S(1)} %get-tuple-element.43), channel_id=1, source_target_pairs={{0,1},{1,0},{2,3},{3,2},{4,8},{5,9},{6,10},{7,11},{8,4},{9,5},{10,... | collective-permute-start | bytes 110600 | tf_op jit(solution)/shard_map/ppermute | solution.py:39
  9.7 4.7 %collective-permute-start.9 = (bf16[288,512]{1,0:T(8,128)(2,1)S(1)}, bf16[288,512]{1,0:T(8,128)(2,1)S(1)}, u32[]{:S(2)}, u32[]{:S(2)}) collective-permute-start(bf16[288,512]{1,0:T(8,128)(2,1)S(1)} %stack_features.1.after_ref.feat_ref), channel_id=1, source_target_pairs={{0,4},{1,5},{2,6},{3,7},{4,0},{5,1},{6,2},{7,3},{8,12},{9,13},{10,... | collective-permute-start | bytes 884744 | tf_op jit(solution)/shard_map/ppermute | solution.py:39
  10.5 9.7 %collective-permute-start.5 = (bf16[288,512]{1,0:T(8,128)(2,1)S(1)}, bf16[288,512]{1,0:T(8,128)(2,1)S(1)}, u32[]{:S(2)}, u32[]{:S(2)}) collective-permute-start(bf16[288,512]{1,0:T(8,128)(2,1)S(1)} %stack_features.1.after_ref.feat_ref), channel_id=1, source_target_pairs={{0,1},{1,0},{2,3},{3,2},{4,8},{5,9},{6,10},{7,11},{8,4},{9,5},{10,... | collective-permute-start | bytes 884744 | tf_op jit(solution)/shard_map/ppermute | solution.py:39
  12.9 2.6 %collective-permute-start.7 = (bf16[16,128]{1,0:T(8,128)(2,1)S(1)}, bf16[16,128]{1,0:T(8,128)(2,1)S(1)}, u32[]{:S(2)}, u32[]{:S(2)}) collective-permute-start(bf16[16,128]{1,0:T(8,128)(2,1)S(1)} %get-tuple-element.45.refs_0_.own_ref), channel_id=1, source_target_pairs={{0,4},{1,2},{2,1},{3,7},{4,0},{5,6},{6,5},{7,3},{8,12},{9,10},{10,... | collective-permute-start | bytes 12296 | tf_op jit(solution)/shard_map/ppermute | solution.py:39
  13.0 2.8 %collective-permute-start.8 = (bf16[16,128]{1,0:T(8,128)(2,1)S(1)}, bf16[16,128]{1,0:T(8,128)(2,1)S(1)}, u32[]{:S(2)}, u32[]{:S(2)}) collective-permute-start(bf16[16,128]{1,0:T(8,128)(2,1)S(1)} %get-tuple-element.45.refs_0_.own_ref), channel_id=1, source_target_pairs={{0,1},{1,0},{2,3},{3,2},{4,5},{5,4},{6,7},{7,6},{8,9},{9,8},{10,11... | collective-permute-start | bytes 12296 | tf_op jit(solution)/shard_map/ppermute | solution.py:39
  15.5 2.9 %copy-start = (bf16[4,12,128,128]{3,2,1,0:T(8,128)(2,1)S(1)}, bf16[4,12,128,128]{3,2,1,0:T(8,128)(2,1)}, u32[]{:S(2)}) copy-start(bf16[4,12,128,128]{3,2,1,0:T(8,128)(2,1)} %pip_ref.3) | copy-start | bytes 4718596
  15.8 2.5 %collective-permute-start.10 = (bf16[16,128]{1,0:T(8,128)(2,1)S(1)}, bf16[16,128]{1,0:T(8,128)(2,1)S(1)}, u32[]{:S(2)}, u32[]{:S(2)}) collective-permute-start(bf16[16,128]{1,0:T(8,128)(2,1)S(1)} %get-tuple-element.48.w_own_ref.after_ref), channel_id=1, source_target_pairs={{0,4},{1,5},{2,6},{3,7},{4,0},{5,1},{6,2},{7,3},{8,12},{9,13},{10,... | collective-permute-start | bytes 12296 | tf_op jit(solution)/shard_map/ppermute | solution.py:39
  17.2 4.0 %collective-permute-start.11 = (bf16[16,128]{1,0:T(8,128)(2,1)S(1)}, bf16[16,128]{1,0:T(8,128)(2,1)S(1)}, u32[]{:S(2)}, u32[]{:S(2)}) collective-permute-start(bf16[16,128]{1,0:T(8,128)(2,1)S(1)} %get-tuple-element.48.w_own_ref.after_ref), channel_id=1, source_target_pairs={{0,1},{1,0},{2,3},{3,2},{4,8},{5,9},{6,10},{7,11},{8,4},{9,5},{10,... | collective-permute-start | bytes 12296 | tf_op jit(solution)/shard_map/ppermute | solution.py:39
